TPU v7x, 128 devices: a whole 4x4x4 slice. The times are simulated.
128 devices in a mesh: fsdp: 8 (over y, x_lo), context: 16 (over z, x_hi, core).
Axes of the slice: x: 4 (x_hi: 2, x_lo: 2; x = x_hi * 2 + x_lo), y: 4, z: 4, core: 2. Of those that a mesh axis runs over, the one named last changes fastest.
Arguments:
- hidden: bfloat16 [16384, 2048], P(('fsdp', 'context')), may hold values from -6 to 6
- cotangent: bfloat16 [16384, 2048], P(('fsdp', 'context')), may hold values from -6 to 6
- lengths: int32 [8, 4], P('fsdp'), may hold values from 1 to 1536, 2048 in all within a row
- source_pos: int32 [8, 2048], P('fsdp'), may hold values from 0 to 2047, as said below
- owner_slot: int32 [8, 2048], P('fsdp'), may hold values from 0 to 2047, as said below
- ln1_gain: bfloat16 [2048], P('fsdp'), may hold values from 0.099609375 to 1.8984375
- ln1_bias: bfloat16 [2048], P('fsdp'), may hold values from -4 to 4
- query_weight: bfloat16 [2048, 2048], P('fsdp'), may hold values from -1 to 1
- query_bias: bfloat16 [2048], P('fsdp'), may hold values from -4 to 4
- kv_weight: bfloat16 [2048, 256], P('fsdp'), may hold values from -0.125 to 0.125
- value_bias: bfloat16 [128], P('fsdp'), may hold values from -4 to 4
- out_weight: bfloat16 [2048, 2048], P('fsdp'), may hold values from -0.25 to 0.25
- out_bias: bfloat16 [2048], P('fsdp'), may hold values from -4 to 4
- ln2_gain: bfloat16 [2048], P('fsdp'), may hold values from 0.099609375 to 1.8984375
- ln2_bias: bfloat16 [2048], P('fsdp'), may hold values from -4 to 4
- fc_weight: bfloat16 [2048, 8192], P('fsdp'), may hold values from -0.125 to 0.125
- fc_bias: bfloat16 [8192], P('fsdp'), may hold values from -4 to 4
- proj_weight: bfloat16 [8192, 2048], P('fsdp'), may hold values from -0.09375 to 0.09375
- proj_bias: bfloat16 [2048], P('fsdp'), may hold values from -4 to 4
Outputs:
- output: bfloat16 [16384, 2048], P(('fsdp', 'context'))
- grad_hidden: bfloat16 [16384, 2048], P(('fsdp', 'context'))
- grad_ln1_gain: float32 [2048], P('fsdp')
- grad_ln1_bias: float32 [2048], P('fsdp')
- grad_query_weight: float32 [2048, 2048], P('fsdp')
- grad_query_bias: float32 [2048], P('fsdp')
- grad_kv_weight: float32 [2048, 256], P('fsdp')
- grad_value_bias: float32 [128], P('fsdp')
- grad_out_weight: float32 [2048, 2048], P('fsdp')
- grad_out_bias: float32 [2048], P('fsdp')
- grad_ln2_gain: float32 [2048], P('fsdp')
- grad_ln2_bias: float32 [2048], P('fsdp')
- grad_fc_weight: float32 [2048, 8192], P('fsdp')
- grad_fc_bias: float32 [8192], P('fsdp')
- grad_proj_weight: float32 [8192, 2048], P('fsdp')
- grad_proj_bias: float32 [2048], P('fsdp')
- maxima: float32 [16], replicated
- clipped_query_weight: float32 [2048, 2048], P('fsdp')
- clipped_query_bias: float32 [2048], P('fsdp')
- clipped_key_weight: float32 [2048, 128], P('fsdp')
Inputs may be any that keep to these rules, and one draw needn't show every extreme that they name: `lengths`: each row sums to 2048; its largest entry is 1536. In each batch owner_slot is a permutation; slot s lies on the device s // 128 of the context axis, in its row s % 128; the tokens of natural positions c * 128 to (c + 1) * 128 - 1 fill the rows c * 8 to (c + 1) * 8 - 1 of every device of the context axis. `source_pos`: in each batch the inverse permutation of owner_slot.
All inputs are finite; a program needn't handle non-finite values.
Results may differ from a plain program's by a relative error of at most 0.025.
Values may be sent and summed in bfloat16 or wider, within the bound.
No kernel may reach another device: no remote copies, remote signals or barrier semaphores. Data moves between devices by JAX's collectives and lax.ppermute only.
A program may use at most 512 MiB of HBM per device.

v0:
```python
import functools
import math

import jax
import jax.numpy as jnp
from jax import lax
from jax.sharding import Mesh
from jax.sharding import PartitionSpec as P

FSDP = ("fsdp_0", "fsdp_1")
CONTEXT = ("context_0", "context_1", "context_2")
FSDP_CONTEXT = ("fsdp_0", "fsdp_1", "context_0", "context_1", "context_2")


EPSILON = 1e-05
CLIP_LIMIT = 4.0
MASKED = -1e30


def side_by_side(arrays, axis, dim, along):
    columns = [a.reshape(*a.shape[:along], -1) for a in arrays]
    both = jnp.concatenate(columns, axis=along)
    out, at, gathered = (lax.all_gather(both, axis, axis=dim, tiled=True), 0, [])
    for a, column in zip(arrays, columns):
        section = out[..., at : at + column.shape[along]]
        gathered.append(section.reshape(*section.shape[:along], *a.shape[along:]))
        at += column.shape[along]
    return tuple(gathered)


def in_one_piece(arrays, axis, dim, along):
    widths = [math.prod(a.shape[along:]) for a in arrays]
    both = jnp.concatenate(
        [a.reshape(*a.shape[:along], w) for a, w in zip(arrays, widths)], axis=along
    )
    out = lax.psum_scatter(both, axis, scatter_dimension=dim, tiled=True)
    pieces = jnp.split(out, [sum(widths[:k]) for k in range(1, len(widths))], axis=along)
    return tuple((b.reshape(*out.shape[:along], *a.shape[along:]) for a, b in zip(arrays, pieces)))


def copy_for_each(array, axis):
    length = lax.axis_size(axis)
    return lax.all_to_all(
        jnp.broadcast_to(array[None], (length, *array.shape)), axis, 0, 0, tiled=True
    )


def laid_out(pieces, dim):
    pieces = jnp.moveaxis(pieces, 0, dim)
    lengths = pieces.shape
    return pieces.reshape(*lengths[:dim], lengths[dim] * lengths[dim + 1], *lengths[dim + 2 :])


def collect(array, axis, dim):
    pieces = copy_for_each(array, axis)
    return laid_out(pieces, dim)


def cut_along(array, dim, length):
    before, after = (array.shape[:dim], array.shape[dim + 1 :])
    return jnp.moveaxis(array.reshape(*before, length, -1, *after), dim, 0)


def sent_and_summed(array, axis, dim):
    length = lax.axis_size(axis)
    pieces = lax.all_to_all(cut_along(array, dim, length), axis, 0, 0, tiled=True)
    return jnp.sum(pieces.astype(jnp.float32), axis=0)


def by_axis(array, axes):
    return functools.reduce(lax.pmax, axes, array)


def layer_norm(values, norm_gain, norm_shift):
    centered = values - jnp.mean(values, axis=-1, keepdims=True)
    spread = jnp.mean(centered * centered, axis=-1, keepdims=True)
    return centered * lax.rsqrt(spread + EPSILON) * norm_gain + norm_shift


def gelu_tanh(values):
    return jax.nn.gelu(values, approximate=True)


def matmul(left_side, right_side):
    return jnp.dot(left_side, right_side, preferred_element_type=jnp.float32)


def tall_product(left_side, right_side):
    return lax.dot_general(
        left_side, right_side, (((0,), (0,)), ((), ())), preferred_element_type=jnp.float32
    )


def wide_product(left_side, right_side):
    return lax.dot_general(
        left_side, right_side, (((1,), (1,)), ((), ())), preferred_element_type=jnp.float32
    )


def fetch_attention(gain_one, shift_one, w_query, b_query, w_kv, b_value, w_out, b_out):
    return (
        lax.all_gather(gain_one, FSDP, axis=0, tiled=True),
        *side_by_side((shift_one, w_query, b_query, w_kv), FSDP, 0, 1),
        lax.all_gather(b_value, FSDP, axis=0, tiled=True),
        *side_by_side((w_out, b_out), FSDP, 0, 1),
    )


def fetch_mlp(gain_two, shift_two, w_fc, b_fc, w_proj, b_proj):
    return (
        lax.all_gather(gain_two, FSDP, axis=0, tiled=True),
        *side_by_side((shift_two, w_fc), FSDP, 0, 1),
        *side_by_side((b_fc, w_proj), FSDP, 0, 1),
        lax.all_gather(b_proj, FSDP, axis=0, tiled=True),
    )


def reduce_grads(term_one, term_two, term_three, term_four, term_five, term_six, term_seven):
    shard_one, shard_two, shard_three, shard_four, shard_five, shard_six, shard_seven = (
        lax.psum_scatter(
            term_one.astype(jnp.bfloat16), FSDP, scatter_dimension=0, tiled=True
        ).astype(jnp.float32),
        lax.psum_scatter(
            term_two.astype(jnp.bfloat16), FSDP, scatter_dimension=0, tiled=True
        ).astype(jnp.float32),
        *tuple(
            (
                part.astype(jnp.float32)
                for part in in_one_piece(
                    (
                        term_three.astype(jnp.bfloat16),
                        term_four.astype(jnp.bfloat16),
                        term_five.astype(jnp.bfloat16),
                    ),
                    FSDP,
                    0,
                    1,
                )
            )
        ),
        lax.psum_scatter(
            term_six.astype(jnp.bfloat16), FSDP, scatter_dimension=0, tiled=True
        ).astype(jnp.float32),
        lax.psum_scatter(
            term_seven.astype(jnp.bfloat16), FSDP, scatter_dimension=0, tiled=True
        ).astype(jnp.float32),
    )
    return (
        lax.psum(shard_one.astype(jnp.bfloat16), CONTEXT).astype(jnp.float32),
        lax.psum(shard_two.astype(jnp.bfloat16), CONTEXT).astype(jnp.float32),
        lax.psum(shard_three.astype(jnp.bfloat16), CONTEXT).astype(jnp.float32),
        lax.psum(shard_four.astype(jnp.bfloat16), CONTEXT).astype(jnp.float32),
        lax.psum(shard_five.astype(jnp.bfloat16), CONTEXT).astype(jnp.float32),
        lax.psum(shard_six.astype(jnp.bfloat16), CONTEXT).astype(jnp.float32),
        lax.psum(shard_seven.astype(jnp.bfloat16), CONTEXT).astype(jnp.float32),
    )


def shards(
    hidden,
    cotangent,
    lengths,
    source_pos,
    owner_slot,
    ln1_gain,
    ln1_bias,
    query_weight,
    query_bias,
    kv_weight,
    value_bias,
    out_weight,
    out_bias,
    ln2_gain,
    ln2_bias,
    fc_weight,
    fc_bias,
    proj_weight,
    proj_bias,
):
    tok_rows = hidden.shape[0]
    model_width = hidden.shape[1]
    ctx_count = lax.axis_size(CONTEXT)
    sub_rows = tok_rows // ctx_count
    ctx_index = lax.axis_index(CONTEXT)
    head_size = kv_weight.shape[1] // 2
    head_count = model_width // head_size
    scale_factor = 1.0 / math.sqrt(head_size)
    attention_full = fetch_attention(
        ln1_gain, ln1_bias, query_weight, query_bias, kv_weight, value_bias, out_weight, out_bias
    )
    gain_one, shift_one, wq_full, bq_full, wkv_full, bv_full, wo_full, bo_full = attention_full
    positions = source_pos[0]
    seq_ends = jnp.cumsum(lengths[0])
    starts = seq_ends - lengths[0]
    own_pos = lax.dynamic_slice_in_dim(positions, ctx_index * tok_rows, tok_rows)
    seq_start = jnp.max(jnp.where(starts[None, :] <= own_pos[:, None], starts[None, :], 0), axis=1)
    allowed = (positions[None, :] <= own_pos[:, None]) & (positions[None, :] >= seq_start[:, None])
    inputs_f = hidden.astype(jnp.float32)
    normed_low = layer_norm(
        inputs_f, gain_one.astype(jnp.float32), shift_one.astype(jnp.float32)
    ).astype(jnp.bfloat16)
    queries = (matmul(normed_low, wq_full) + bq_full.astype(jnp.float32)).astype(jnp.bfloat16)
    kv_shift = jnp.concatenate([jnp.zeros((head_size,), jnp.float32), bv_full.astype(jnp.float32)])
    key_value = (matmul(normed_low, wkv_full) + kv_shift).astype(jnp.bfloat16)
    all_kv = collect(key_value, CONTEXT, 0)
    all_keys = all_kv[:, :head_size]
    all_values = all_kv[:, head_size:]
    query_heads = queries.reshape(tok_rows, head_count, head_size)

    def score_block():
        raw_scores = jnp.einsum(
            "rhd,kd->rhk", query_heads, all_keys, preferred_element_type=jnp.float32
        )
        return jnp.where(allowed[:, None, :], raw_scores * scale_factor, MASKED)

    masked_scores = score_block()
    local_max = jnp.max(masked_scores, axis=(0, 2))
    row_max = jnp.max(masked_scores, axis=2, keepdims=True)
    log_total = row_max + jnp.log(jnp.sum(jnp.exp(masked_scores - row_max), axis=2, keepdims=True))
    probs_low = jnp.exp(masked_scores - log_total).astype(jnp.bfloat16)
    attended = jnp.einsum("rhk,kd->rhd", probs_low, all_values, preferred_element_type=jnp.float32)
    attended = attended.reshape(tok_rows, model_width).astype(jnp.bfloat16)
    after_attn = inputs_f + matmul(attended, wo_full) + bo_full.astype(jnp.float32)
    mlp_full = fetch_mlp(ln2_gain, ln2_bias, fc_weight, fc_bias, proj_weight, proj_bias)
    gain_two, shift_two, w_fc, b_fc, w_proj, b_proj = mlp_full
    normed_two_low = layer_norm(
        after_attn, gain_two.astype(jnp.float32), shift_two.astype(jnp.float32)
    ).astype(jnp.bfloat16)
    pre_act = matmul(normed_two_low, w_fc) + b_fc.astype(jnp.float32)
    activated = gelu_tanh(pre_act).astype(jnp.bfloat16)
    result_low = (after_attn + matmul(activated, w_proj) + b_proj.astype(jnp.float32)).astype(
        jnp.bfloat16
    )
    owned_slots = lax.dynamic_slice_in_dim(owner_slot[0], ctx_index * tok_rows, tok_rows)
    target = owned_slots // tok_rows * sub_rows + owned_slots % tok_rows - ctx_index * sub_rows
    slot_ids = jnp.arange(tok_rows, dtype=jnp.int32)
    pick_back = (target[:, None] == slot_ids[None, :]).astype(jnp.bfloat16)
    returned = lax.all_to_all(
        result_low.reshape(ctx_count, sub_rows, model_width),
        CONTEXT,
        split_axis=0,
        concat_axis=0,
        tiled=True,
    )
    output = matmul(pick_back, returned.reshape(tok_rows, model_width)).astype(jnp.bfloat16)
    outgoing = tall_product(pick_back, cotangent).astype(jnp.bfloat16)
    dealt_rows = lax.all_to_all(
        outgoing.reshape(ctx_count, sub_rows, model_width),
        CONTEXT,
        split_axis=0,
        concat_axis=0,
        tiled=True,
    )
    grad_out = dealt_rows.reshape(tok_rows, model_width)
    grad_out_f = grad_out.astype(jnp.float32)
    mlp_back = fetch_mlp(ln2_gain, ln2_bias, fc_weight, fc_bias, proj_weight, proj_bias)
    gain_two_b, shift_two_b, w_fc_b, b_fc_b, w_proj_b, b_proj_b = mlp_back
    grad_proj_w = tall_product(activated, grad_out)
    grad_proj_b = jnp.sum(grad_out_f, axis=0)
    grad_act = wide_product(grad_out, w_proj_b)
    unused_act, gelu_back = jax.vjp(gelu_tanh, pre_act)
    grad_pre = gelu_back(grad_act)[0].astype(jnp.bfloat16)
    grad_fc_w = tall_product(normed_two_low, grad_pre)
    grad_fc_b = jnp.sum(grad_pre.astype(jnp.float32), axis=0)
    grad_normed_two = wide_product(grad_pre, w_fc_b)
    unused_two, norm_back_two = jax.vjp(
        layer_norm, after_attn, gain_two_b.astype(jnp.float32), shift_two_b.astype(jnp.float32)
    )
    grad_after, grad_gain_two, grad_shift_two = norm_back_two(grad_normed_two)
    grad_after = grad_after + grad_out_f
    grad_branch = grad_after.astype(jnp.bfloat16)
    grad_bo = jnp.sum(grad_branch.astype(jnp.float32), axis=0)
    mlp_sums = reduce_grads(
        grad_proj_w, grad_proj_b, grad_gain_two, grad_shift_two, grad_fc_w, grad_fc_b, grad_bo
    )
    attention_back = fetch_attention(
        ln1_gain, ln1_bias, query_weight, query_bias, kv_weight, value_bias, out_weight, out_bias
    )
    gain_one_b, shift_one_b, wq_back, bq_back, wkv_back, bv_back, wo_back, bo_back = attention_back
    grad_wo = tall_product(attended, grad_branch)
    grad_attended = wide_product(grad_branch, wo_back).astype(jnp.bfloat16)
    grad_attended = grad_attended.reshape(tok_rows, head_count, head_size)
    probs_again = jnp.exp(score_block() - log_total)
    grad_probs = jnp.einsum(
        "rhd,kd->rhk", grad_attended, all_values, preferred_element_type=jnp.float32
    )
    inner_sum = jnp.sum(probs_again * grad_probs, axis=2, keepdims=True)
    grad_scores = (probs_again * (grad_probs - inner_sum)).astype(jnp.bfloat16)
    grad_queries = jnp.einsum(
        "rhk,kd->rhd", grad_scores, all_keys, preferred_element_type=jnp.float32
    )
    grad_queries = (grad_queries * scale_factor).reshape(tok_rows, model_width).astype(jnp.bfloat16)
    grad_keys = (
        jnp.einsum("rhk,rhd->kd", grad_scores, query_heads, preferred_element_type=jnp.float32)
        * scale_factor
    )
    grad_values = jnp.einsum(
        "rhk,rhd->kd",
        probs_again.astype(jnp.bfloat16),
        grad_attended,
        preferred_element_type=jnp.float32,
    )
    kv_total = sent_and_summed(
        jnp.concatenate([grad_keys, grad_values], axis=1).astype(jnp.bfloat16), CONTEXT, 0
    )
    grad_kv = kv_total.astype(jnp.bfloat16)
    grad_wq = tall_product(normed_low, grad_queries)
    grad_bq = jnp.sum(grad_queries.astype(jnp.float32), axis=0)
    grad_wkv = tall_product(normed_low, grad_kv)
    grad_bv = jnp.sum(grad_kv[:, head_size:].astype(jnp.float32), axis=0)
    grad_normed_one = wide_product(grad_queries, wq_back) + wide_product(grad_kv, wkv_back)
    unused_one, norm_back_one = jax.vjp(
        layer_norm, inputs_f, gain_one_b.astype(jnp.float32), shift_one_b.astype(jnp.float32)
    )
    grad_inputs, grad_gain_one, grad_shift_one = norm_back_one(grad_normed_one)
    grad_hidden = (grad_inputs + grad_after).astype(jnp.bfloat16)
    attn_sums = reduce_grads(
        grad_wo, grad_gain_one, grad_shift_one, grad_wq, grad_bq, grad_wkv, grad_bv
    )
    maxima = by_axis(local_max, FSDP_CONTEXT)
    clip_ratio = CLIP_LIMIT / jnp.maximum(maxima, CLIP_LIMIT)
    column_scale = jnp.repeat(jnp.sqrt(clip_ratio), head_size)
    clipped_qw = query_weight.astype(jnp.float32) * column_scale[None, :]
    bias_rows = query_bias.shape[0]
    clipped_qb = query_bias.astype(jnp.float32) * lax.dynamic_slice_in_dim(
        column_scale, lax.axis_index(FSDP) * bias_rows, bias_rows
    )
    clipped_kw = kv_weight[:, :head_size].astype(jnp.float32) * jnp.sqrt(jnp.min(clip_ratio))
    return (
        output,
        grad_hidden,
        attn_sums[1],
        attn_sums[2],
        attn_sums[3],
        attn_sums[4],
        attn_sums[5],
        attn_sums[6],
        attn_sums[0],
        mlp_sums[6],
        mlp_sums[2],
        mlp_sums[3],
        mlp_sums[4],
        mlp_sums[5],
        mlp_sums[0],
        mlp_sums[1],
        maxima,
        clipped_qw,
        clipped_qb,
        clipped_kw,
    )


def solution(mesh):
    torus = Mesh(
        mesh.devices.reshape(4, 2, 4, 2, 2),
        ("fsdp_0", "fsdp_1", "context_0", "context_1", "context_2"),
    )
    return jax.shard_map(
        shards,
        mesh=torus,
        in_specs=(
            P(FSDP_CONTEXT, None),
            P(FSDP_CONTEXT, None),
            P(FSDP, None),
            P(FSDP, None),
            P(FSDP, None),
            P(FSDP),
            P(FSDP),
            P(FSDP, None),
            P(FSDP),
            P(FSDP, None),
            P(FSDP),
            P(FSDP, None),
            P(FSDP),
            P(FSDP),
            P(FSDP),
            P(FSDP, None),
            P(FSDP),
            P(FSDP, None),
            P(FSDP),
        ),
        out_specs=(
            P(FSDP_CONTEXT, None),
            P(FSDP_CONTEXT, None),
            P(FSDP),
            P(FSDP),
            P(FSDP, None),
            P(FSDP),
            P(FSDP, None),
            P(FSDP),
            P(FSDP, None),
            P(FSDP),
            P(FSDP),
            P(FSDP),
            P(FSDP, None),
            P(FSDP),
            P(FSDP, None),
            P(FSDP),
            P(),
            P(FSDP, None),
            P(FSDP),
            P(FSDP, None),
        ),
        check_vma=False,
    )
```

profile of v0, /device:TPU:1, one launch (start us, length us, event | category | flops | bytes accessed | tf_op | source)
XLA Modules:
  0.0 3892.9 jit_solution(13996677750360988951)
XLA Ops:
  29.2 16.8 all-gather
  62.5 151.9 %all-gather.8.cloned.1.call-done = bf16[2048,2306]{1,0:T(8,128)(2,1)} async-done(((bf16[256,2306]{1,0:T(8,128)(2,1)}), bf16[2048,2306]{1,0:T(8,128)(2,1)}) %all-gather.8.cloned.1.call-update) | async-done | bytes 9445392 | tf_op jit(solution)/shard_map/all_gather | solution.py:23
  227.3 34.3 all-gather.1
  262.8 144.4 %all-gather.10.cloned.1.call-done = bf16[2048,2049]{1,0:T(8,128)(2,1)} async-done(((bf16[256,2049]{1,0:T(8,128)(2,1)}), bf16[2048,2049]{1,0:T(8,128)(2,1)}) %all-gather.10.cloned.1.call-update) | async-done | bytes 8392720 | tf_op jit(solution)/shard_map/all_gather | solution.py:23
  461.1 604.5 %all-gather.12.cloned.1.call-done = bf16[2048,8193]{1,0:T(8,128)(2,1)} async-done(((bf16[256,8193]{1,0:T(8,128)(2,1)}), bf16[2048,8193]{1,0:T(8,128)(2,1)}) %all-gather.12.cloned.1.call-update) | async-done | bytes 33558544 | tf_op jit(solution)/shard_map/all_gather | solution.py:23
  1066.8 680.8 %all-gather.14.cloned.1.call-done = bf16[8192,2049]{1,0:T(8,128)(2,1)} async-done(((bf16[1024,2049]{1,0:T(8,128)(2,1)}), bf16[8192,2049]{1,0:T(8,128)(2,1)}) %all-gather.14.cloned.1.call-update) | async-done | bytes 33570832 | tf_op jit(solution)/shard_map/all_gather | solution.py:23
  1749.8 18.1 fusion.12
  1767.9 22.7 fusion.128
  1790.7 20.2 multiply_reduce_fusion.1
  1885.0 42.7 %concatenate.42 = bf16[2048,2050]{0,1:T(8,128)(2,1)} concatenate(bf16[2048,1]{0,1:T(2,128)(2,1)S(1)} %convert_element_type.314, bf16[2048,2048]{0,1:T(8,128)(2,1)} %convolution_convert_fusion.2, bf16[2048,1]{0,1:T(2,128)(2,1)S(1)} %bitcast.159), dimensions={1} | concatenate | bytes 16793600 | tf_op jit(solution)/shard_map/concatenate | solution.py:33
  1930.7 16.0 convolution_convert_fusion
  1946.7 69.4 %concatenate.43 = bf16[2048,8194]{1,0:T(8,128)(2,1)} concatenate(bf16[2048,1]{1,0:T(8,128)(2,1)} %convert_element_type.348, bf16[2048,1]{1,0:T(8,128)(2,1)} %convert_element_type.349, bf16[2048,8192]{1,0:T(8,128)(2,1)} %convolution_convert_fusion), dimensions={1} | concatenate | bytes 67125248 | tf_op jit(solution)/shard_map/concatenate | solution.py:33
  2023.8 16.3 convolution_convert_fusion.1
  2040.2 56.8 %reduce-scatter.6.cloned.1.call-done = bf16[256,2050]{0,1:T(8,128)(2,1)} async-done(((bf16[2048,2050]{0,1:T(8,128)(2,1)}), bf16[256,2050]{0,1:T(8,128)(2,1)}) %reduce-scatter.6.cloned.1.call-update) | async-done | bytes 1049616 | tf_op jit(solution)/shard_map/reduce_scatter | solution.py:36
  2099.5 651.8 %reduce-scatter.12.cloned.1.call-done = bf16[256,8194]{1,0:T(8,128)(2,1)} async-done(((bf16[2048,8194]{1,0:T(8,128)(2,1)}), bf16[256,8194]{1,0:T(8,128)(2,1)}) %reduce-scatter.12.cloned.1.call-update) | async-done | bytes 4195344 | tf_op jit(solution)/shard_map/reduce_scatter | solution.py:36
  2757.0 34.4 reduce-scatter.8.cloned.1.call-done
  2791.4 176.0 %reduce-scatter.10.cloned.1.call-done = bf16[256,2048]{1,0:T(8,128)(2,1)} async-done(((bf16[2048,2048]{1,0:T(8,128)(2,1)}), bf16[256,2048]{1,0:T(8,128)(2,1)}) %reduce-scatter.10.cloned.1.call-update) | async-done | bytes 1048592 | tf_op jit(solution)/shard_map/reduce_scatter | solution.py:120
  2967.4 644.6 %reduce-scatter.14.cloned.1.call-done = bf16[1024,2048]{1,0:T(8,128)(2,1)} async-done(((bf16[8192,2048]{1,0:T(8,128)(2,1)}), bf16[1024,2048]{1,0:T(8,128)(2,1)}) %reduce-scatter.14.cloned.1.call-update) | async-done | bytes 4194320 | tf_op jit(solution)/shard_map/reduce_scatter | solution.py:120
  3612.1 13.9 all-gather.2
  3668.0 21.5 fusion.66
  3697.2 15.0 all-to-all-done.1
  3715.1 28.5 all-reduce.9
  3747.0 38.4 all-reduce.7
  3790.5 76.9 %all-reduce.12.cloned.1.call-done = (bf16[256,2048]{0,1:T(8,128)(2,1)}, bf16[256,256]{1,0:T(8,128)(2,1)}, bf16[256,2048]{1,0:T(8,128)(2,1)}, bf16[256,8192]{1,0:T(8,128)(2,1)}, bf16[1024,2048]{1,0:T(8,128)(2,1)}) async-done(((bf16[256,2048]{0,1:T(8,128)(2,1)}, bf16[256,256]{1,0:T(8,128)(2,1)}, bf16[256,2048]{1,0:T(8,128)(2,1)}, bf16[256,8192]{1,0:T(8,128)(2,1)}, bf16[1024,2048]{1,0:T(8,128)(2,1)}), ...) | async-done | bytes 10616848 | tf_op jit(solution)/shard_map/psum | solution.py:152
  (257 shorter events, 278.2 us)
Async XLA Ops:
  7.2 207.2 %all-gather.8.cloned.1.call-start = ((), (), s32[]{:S(2)}) async-start(), calls=%async_computation.9 | async-start | bytes 11206656 | tf_op jit(solution)/shard_map/all_gather | solution.py:23
  12.5 394.7 %all-gather.10.cloned.1.call-start = ((), (), s32[]{:S(2)}) async-start(), calls=%async_computation.10 | async-start | bytes 10027008 | tf_op jit(solution)/shard_map/all_gather | solution.py:23
  15.6 1049.9 %all-gather.12.cloned.1.call-start = ((), (), s32[]{:S(2)}) async-start(), calls=%async_computation.11 | async-start | bytes 38338560 | tf_op jit(solution)/shard_map/all_gather | solution.py:23
  22.2 1725.4 %all-gather.14.cloned.1.call-start = ((), (), s32[]{:S(2)}) async-start(), calls=%async_computation.12 | async-start | bytes 40108032 | tf_op jit(solution)/shard_map/all_gather | solution.py:23
  46.0 368.9 %copy-start.22 = (f32[8,1,256]{2,1,0:T(1,128)}, f32[8,1,256]{2,1,0:T(1,128)S(1)}, u32[]{:S(2)}) copy-start(f32[8,1,256]{2,1,0:T(1,128)S(1)} %convert_element_type.345) | copy-start | bytes 24580
  62.2 385.5 %copy-start.8 = (pred[128,2048]{1,0:T(8,128)(4,1)}, pred[128,2048]{1,0:T(8,128)(4,1)S(1)}, u32[]{:S(2)}) copy-start(pred[128,2048]{1,0:T(8,128)(4,1)S(1)} %compare_and_fusion.1) | copy-start | bytes 786436
  219.3 195.7 %all-to-all-start = ((bf16[16,128,256]{2,1,0:T(8,128)(2,1)}), bf16[16,128,256]{2,1,0:T(8,128)(2,1)S(1)}, u32[]{:S(2)}, u32[]{:S(2)}) async-start(bf16[16,128,256]{2,1,0:T(8,128)(2,1)} %broadcast_in_dim.44), calls=%async_computation | async-start | bytes 2097152 | tf_op jit(solution)/shard_map/all_to_all | solution.py:43
  415.0 1352.9 %all-to-all-start.2 = ((bf16[16,8,2048]{2,1,0:T(8,128)(2,1)}), bf16[16,8,2048]{2,1,0:T(8,128)(2,1)S(1)}, u32[]{:S(2)}, u32[]{:S(2)}) async-start(bf16[16,8,2048]{2,1,0:T(8,128)(2,1)} %fusion.65), calls=%async_computation.2 | async-start | bytes 1048576 | tf_op jit(solution)/shard_map/all_to_all | solution.py:247
  455.8 1312.1 %copy-start.15 = (bf16[128,16,128]{0,2,1:T(8,128)(2,1)}, bf16[128,16,128]{0,2,1:T(8,128)(2,1)S(1)}, u32[]{:S(2)}) copy-start(bf16[128,16,128]{0,2,1:T(8,128)(2,1)S(1)} %fusion.77) | copy-start | bytes 1572868
  460.8 1350.1 %copy-start.6 = (f32[128,2048]{1,0:T(8,128)}, f32[128,2048]{1,0:T(8,128)S(1)}, u32[]{:S(2)}) copy-start(f32[128,2048]{1,0:T(8,128)S(1)} %get-tuple-element.145) | copy-start | bytes 3145732
  461.0 1349.8 %copy-start.32 = (f32[128]{0:T(128)}, f32[128]{0:T(128)S(1)}, u32[]{:S(2)}) copy-start(f32[128]{0:T(128)S(1)} %fusion.113) | copy-start | bytes 1540
  1066.8 701.1 %copy-start.20 = (f32[2048]{0:T(1024)}, f32[2048]{0:T(1024)S(1)}, u32[]{:S(2)}) copy-start(f32[2048]{0:T(1024)S(1)} %convert_reduce_fusion.2) | copy-start | bytes 24580
  1857.9 24.4 all-to-all-start.3
  1865.1 231.8 %reduce-scatter.6.cloned.1.call-start = ((), (), s32[]{:S(2)}) async-start(), calls=%async_computation.13 | async-start | bytes 9474048 | tf_op jit(solution)/shard_map/reduce_scatter | solution.py:36
  1927.8 823.4 %reduce-scatter.12.cloned.1.call-start = ((), (), s32[]{:S(2)}) async-start(), calls=%async_computation.16 | async-start | bytes 38338560 | tf_op jit(solution)/shard_map/reduce_scatter | solution.py:36
  2016.1 775.4 %reduce-scatter.8.cloned.1.call-start = ((), (), s32[]{:S(2)}) async-start(), calls=%async_computation.14 | async-start | bytes 1179648 | tf_op jit(solution)/shard_map/reduce_scatter | solution.py:141
  2017.7 949.8 %reduce-scatter.10.cloned.1.call-start = ((), (), s32[]{:S(2)}) async-start(), calls=%async_computation.15 | async-start | bytes 9437184 | tf_op jit(solution)/shard_map/reduce_scatter | solution.py:120
  2023.7 1588.4 %reduce-scatter.14.cloned.1.call-start = ((), (), s32[]{:S(2)}) async-start(), calls=%async_computation.17 | async-start | bytes 37748736 | tf_op jit(solution)/shard_map/reduce_scatter | solution.py:120
  2040.1 1827.3 %all-reduce.12.cloned.1.call-start = ((), (), s32[]{:S(2)}) async-start(), calls=%async_computation.18 | async-start | bytes 21233664 | tf_op jit(solution)/shard_map/psum | solution.py:152
  2099.4 1512.7 %copy-start.52 = (bf16[256]{0:T(256)(128)(2,1)S(1)}, bf16[256]{0:T(256)(128)(2,1)}, u32[]{:S(2)}) copy-start(bf16[256]{0:T(256)(128)(2,1)} %param.37) | copy-start | bytes 1540
  2099.4 1528.6 %copy-start.45 = (f32[16]{0:T(128)S(1)}, f32[16]{0:T(128)}, u32[]{:S(2)}) copy-start(f32[16]{0:T(128)} %get-tuple-element.100) | copy-start | bytes 196
  2099.4 1567.2 %copy-start.43 = (bf16[256]{0:T(256)(128)(2,1)S(1)}, bf16[256]{0:T(256)(128)(2,1)}, u32[]{:S(2)}) copy-start(bf16[256]{0:T(256)(128)(2,1)} %param.27) | copy-start | bytes 1540
  2099.5 1567.8 %copy-start.19 = (bf16[256,256]{1,0:T(8,128)(2,1)S(1)}, bf16[256,256]{1,0:T(8,128)(2,1)}, u32[]{:S(2)}) copy-start(bf16[256,256]{1,0:T(8,128)(2,1)} %param.28) | copy-start | bytes 393220
  3689.5 22.7 all-to-all-start.1
  (48 other events, 2483.8 us)
Sparse Core Ops, SparseCore 0:
  12.6 201.7 all-gather.7
  216.6 190.5 all-gather.9
  408.8 656.6 all-gather.11
  1067.0 680.4 all-gather.13
  1927.9 169.0 reduce-scatter.5
  2099.3 651.8 reduce-scatter.11
  2754.3 37.0 reduce-scatter.7
  2794.5 172.8 reduce-scatter.9
  2970.1 641.9 reduce-scatter.13
  3615.4 251.9 all-reduce.11
where the time goes:
time: 3910 us; the launch traced here: 3890 us
  waiting for transfers between devices  3240 us (83%)
  matrix products  202 us (5%)
  blocking collectives  183 us (5%)
  local copies, waits for them, and re-layouts  148 us (4%)
  other arithmetic  73.5 us (2%)
    all_gather x4, waiting for transfers between devices, side_by_side(): lax.all_gather(both, axis, axis=dim, tiled=True)  1580 us
    reduce_scatter x2, waiting for transfers between devices, reduce_grads(): lax.psum_scatter(term_one.astype(jnp.bfloat16), FSDP, scatter_dimension=0...  821 us
    reduce_scatter x2, waiting for transfers between devices, in_one_piece(): out = lax.psum_scatter(both, axis, scatter_dimension=dim, tiled=True)  709 us
    concatenate x2, local copies, waits for them, and re-layouts, in_one_piece(): jnp.concatenate([a.reshape(*a.shape[:along], w) for a, w in zip(arrays, w...  112 us
  transfers between devices with their start and end apart: 14, of which 12 were waited for; matrix products, arithmetic and copies ran while one was open for 7% of the time, Pallas kernels for 0%

commit v1 on v0

v1 whole, which is shorter than its diff:
```python
import functools
import math

import jax
import jax.numpy as jnp
from jax import lax
from jax.experimental import pallas as pl
from jax.experimental.pallas import tpu as pltpu
from jax.sharding import Mesh
from jax.sharding import PartitionSpec as P

Y, XL, Z, XH, CORE = ("fsdp_0", "fsdp_1", "context_0", "context_1", "context_2")
FSDP = (Y, XL)
CONTEXT = (Z, XH, CORE)
ZX = (Z, XH)
EVERY = (Y, XL, Z, XH, CORE)

EPSILON = 1e-05
CLIP_LIMIT = 4.0
MASKED = -1e30
LANES = 128
BF = jnp.bfloat16
F32 = jnp.float32


def shift(array, axis, by):
    n = lax.axis_size(axis)
    return lax.ppermute(array, axis, [(i, (i + by) % n) for i in range(n)])


def swap(array, axis):
    return shift(array, axis, 1)


def copies(array, axis):
    n = lax.axis_size(axis)
    return lax.all_to_all(jnp.broadcast_to(array[None], (n, *array.shape)), axis, 0, 0, tiled=True)


def pick(array, index, dim):
    return lax.dynamic_index_in_dim(array, index, dim, keepdims=False)


def pair(own, other, index):
    return jnp.where(index == 0, jnp.stack([own, other]), jnp.stack([other, own]))


def assemble(pieces, rows):
    arrays = [a.reshape(-1, a.shape[-1]) for a, _ in pieces]
    width = arrays[0].shape[1]
    counts = [a.shape[0] // LANES for a in arrays]
    firsts = [sum(counts[:k]) for k in range(len(counts))]
    at = [o // LANES for _, offsets in pieces for o in offsets]

    def kernel(at_ref, *refs):
        step, out = pl.program_id(0), refs[-1]
        for source, first, count in zip(refs, firsts, counts):

            @pl.when((step >= first) & (step < first + count))
            def _(source=source):
                out[...] = source[...]

    def block_of(first, count):
        return lambda k, at_ref: (jnp.clip(k - first, 0, count - 1), 0)

    return pl.pallas_call(
        kernel,
        grid_spec=pltpu.PrefetchScalarGridSpec(
            num_scalar_prefetch=1,
            grid=(rows // LANES,),
            in_specs=[
                pl.BlockSpec((LANES, width), block_of(f, n)) for f, n in zip(firsts, counts)
            ],
            out_specs=pl.BlockSpec((LANES, width), lambda k, at_ref: (at_ref[k], 0)),
        ),
        out_shape=jax.ShapeDtypeStruct((rows, width), arrays[0].dtype),
        compiler_params=pltpu.CompilerParams(vmem_limit_bytes=32 * 2**20),
        cost_estimate=pl.CostEstimate(
            flops=0, bytes_accessed=2 * rows * width * 2, transcendentals=0
        ),
        name="assemble",
    )(jnp.stack([jnp.asarray(o, jnp.int32) for o in at]), *arrays)


def matmul(left, right):
    return jnp.dot(left, right, preferred_element_type=F32)


def tall(left, right):
    return lax.dot_general(left, right, (((0,), (0,)), ((), ())), preferred_element_type=F32)


def wide(left, right):
    return lax.dot_general(left, right, (((1,), (1,)), ((), ())), preferred_element_type=F32)


def gelu_tanh(values):
    return jax.nn.gelu(values, approximate=True)


def norm_parts(values):
    centered = values - jnp.mean(values, axis=-1, keepdims=True)
    rate = lax.rsqrt(jnp.mean(centered * centered, axis=-1, keepdims=True) + EPSILON)
    return centered * rate, rate


def norm_back(grad, gain, hat, rate):
    e = grad * gain
    inner = jnp.mean(e * hat, axis=-1, keepdims=True)
    return rate * (e - jnp.mean(e, axis=-1, keepdims=True) - hat * inner)


def shards(
    hidden,
    cotangent,
    lengths,
    source_pos,
    owner_slot,
    ln1_gain,
    ln1_bias,
    query_weight,
    query_bias,
    kv_weight,
    value_bias,
    out_weight,
    out_bias,
    ln2_gain,
    ln2_bias,
    fc_weight,
    fc_bias,
    proj_weight,
    proj_bias,
):
    rows, width = hidden.shape
    ny, nz, nctx = lax.axis_size(Y), lax.axis_size(Z), lax.axis_size(CONTEXT)
    y, xl, z, c = (lax.axis_index(a) for a in (Y, XL, Z, CORE))
    xo, co = 1 - xl, 1 - c
    ctx = lax.axis_index(CONTEXT)
    sub = rows // nctx
    head = kv_weight.shape[1] // 2
    heads = width // head
    scale = 1.0 / math.sqrt(head)
    shard = query_weight.shape[0]
    half = shard // 2
    ff = proj_weight.shape[0]
    block = 2 * ff

    small = jnp.concatenate(
        [
            jnp.stack([ln1_gain, ln1_bias, query_bias, out_bias, ln2_gain, ln2_bias, proj_bias]),
            jnp.pad(value_bias, (0, shard - value_bias.shape[0]))[None],
            fc_bias.reshape(-1, shard),
            jnp.zeros((4, shard), BF),
            kv_weight,
        ]
    )
    small = copies(small, FSDP)
    gain1, bias1, bq, bo, gain2, bias2, bproj = (
        small[:, k].reshape(width).astype(F32) for k in range(7)
    )
    bv = small[:, 7, : value_bias.shape[0]].reshape(head).astype(F32)
    bfc = pick(small[:, 8:12].reshape(ny, block), y, 0).astype(F32)
    wkv = small[:, 16:].reshape(width, 2 * head)

    q_half = lax.dynamic_slice_in_dim(query_weight, half * c, half)
    pieces = [(query_weight, [shard * y, shard * y + half])]
    for d in (1, 3, 2):
        got = shift(q_half, Y, d)
        at = shard * ((y - d) % ny)
        pieces += [(got, [at + half * c]), (swap(got, CORE), [at + half * co])]
    wq = assemble(pieces, ny * shard)

    def gathered(own, halves):
        got = [halves[0]] + [shift(halves[d], Y, d) for d in range(1, ny)]
        mine = jnp.stack(got)
        passed = swap(pick(mine, z, 0), XL)
        theirs = jnp.stack([passed] + [shift(passed, Z, e) for e in range(1, nz)])
        at_mine = [shard * (2 * ((y - d) % ny) + xl) for d in range(ny)]
        at_theirs = [shard * (2 * ((y - (z - e) % nz) % ny) + xo) for e in range(nz)]
        parts = [(own, [at_mine[0], at_mine[0] + half])]
        parts += [(mine[1:], [a + half * c for a in at_mine[1:]])]
        parts += [(swap(mine[1:], CORE), [a + half * co for a in at_mine[1:]])]
        parts += [(theirs, [a + half * c for a in at_theirs])]
        parts += [(swap(theirs, CORE), [a + half * co for a in at_theirs])]
        return assemble(parts, 2 * ny * shard)

    o_half = lax.dynamic_slice_in_dim(out_weight, half * c, half)
    wo = gathered(out_weight, [o_half] * ny)
    wfc = gathered(
        lax.dynamic_slice(fc_weight, (0, block * y), (shard, block)),
        [
            lax.dynamic_slice(fc_weight, (half * c, block * ((y + d) % ny)), (half, block))
            for d in range(ny)
        ],
    )
    passed = swap(
        lax.dynamic_slice(proj_weight, (shard * z + half * c, 0), (half, width)), XL
    )
    theirs = jnp.stack([passed] + [shift(passed, Z, e) for e in range(1, nz)])
    at_theirs = [ff * xo + shard * ((z - e) % nz) for e in range(nz)]
    wproj = assemble(
        [
            (proj_weight, [ff * xl + LANES * k for k in range(ff // LANES)]),
            (theirs, [a + half * c for a in at_theirs]),
            (swap(theirs, CORE), [a + half * co for a in at_theirs]),
        ],
        block,
    )

    x = hidden.astype(F32)
    hat1, rate1 = norm_parts(x)
    h1 = (hat1 * gain1 + bias1).astype(BF)
    kv = matmul(h1, wkv) + jnp.concatenate([jnp.zeros((head,), F32), bv])
    all_kv = copies(kv.astype(BF), CONTEXT).reshape(nctx * rows, 2 * head)
    keys, values = all_kv[:, :head], all_kv[:, head:]
    by_shard = h1.reshape(rows, ny, 2, shard)
    h1_theirs = swap(pick(by_shard, xo, 2).reshape(rows, ny * shard), XL)
    h1_mine = pick(by_shard, xl, 2).reshape(rows, ny * shard)
    q_terms = matmul(jnp.concatenate([h1_mine, h1_theirs]), wq)
    q = (q_terms[:rows] + swap(q_terms[rows:].astype(BF), XL).astype(F32) + bq).astype(BF)

    positions = source_pos[0]
    starts = jnp.cumsum(lengths[0]) - lengths[0]
    own_pos = lax.dynamic_slice_in_dim(positions, ctx * rows, rows)
    seq_start = jnp.max(jnp.where(starts[None, :] <= own_pos[:, None], starts[None, :], 0), axis=1)
    allowed = (positions[None, :] <= own_pos[:, None]) & (positions[None, :] >= seq_start[:, None])
    q_heads = q.reshape(rows, heads, head)

    def score_block():
        raw = jnp.einsum("rhd,kd->rhk", q_heads, keys, preferred_element_type=F32)
        return jnp.where(allowed[:, None, :], raw * scale, MASKED)

    masked = score_block()
    local_max = jnp.max(masked, axis=(0, 2))
    row_max = jnp.max(masked, axis=2, keepdims=True)
    log_total = row_max + jnp.log(jnp.sum(jnp.exp(masked - row_max), axis=2, keepdims=True))
    probs = jnp.exp(masked - log_total).astype(BF)
    attended = jnp.einsum("rhk,kd->rhd", probs, values, preferred_element_type=F32)
    attended = attended.reshape(rows, width).astype(BF)

    x2 = x + matmul(attended, wo) + bo
    hat2, rate2 = norm_parts(x2)
    h2 = (hat2 * gain2 + bias2).astype(BF)

    def over_y(array):
        return jnp.concatenate([array] + [shift(array, Y, d) for d in range(1, ny)])

    def summed_over_y(terms):
        terms = terms.reshape(ny, rows, width)
        got = [shift(terms[d].astype(BF), Y, -d).astype(F32) for d in range(1, ny)]
        return functools.reduce(jnp.add, got, terms[0])

    h2_all = over_y(h2)

    owned = lax.dynamic_slice_in_dim(owner_slot[0], ctx * rows, rows)
    target = owned // rows * sub + owned % rows - ctx * sub
    deal = (target[:, None] == jnp.arange(rows, dtype=jnp.int32)[None, :]).astype(BF)

    def dealt(array):
        pieces = array.reshape(nctx, sub, width)
        return lax.all_to_all(pieces, CONTEXT, 0, 0, tiled=True).reshape(rows, width)

    dy = dealt(tall(deal, cotangent).astype(BF))
    dy_all = over_y(dy)

    u = matmul(h2_all, wfc) + bfc
    g = gelu_tanh(u).astype(BF)
    dg = wide(dy_all, wproj)
    du = jax.vjp(gelu_tanh, u)[1](dg)[0].astype(BF)
    dh2 = summed_over_y(wide(du, wfc))

    result = (x2 + summed_over_y(matmul(g, wproj)) + bproj).astype(BF)
    output = matmul(deal, dealt(result)).astype(BF)

    dy_f = dy.astype(F32)
    dx2 = dy_f + norm_back(dh2, gain2, hat2, rate2)
    da = dx2.astype(BF)
    da_all = over_y(da)

    dattended = wide(da, wo).astype(BF).reshape(rows, heads, head)
    prob = jnp.exp(score_block() - log_total)
    dprob = jnp.einsum("rhd,kd->rhk", dattended, values, preferred_element_type=F32)
    inner = jnp.sum(prob * dprob, axis=2, keepdims=True)
    dscores = (prob * (dprob - inner)).astype(BF)
    dq = jnp.einsum("rhk,kd->rhd", dscores, keys, preferred_element_type=F32)
    dq = (dq * scale).reshape(rows, width).astype(BF)
    dkeys = jnp.einsum("rhk,rhd->kd", dscores, q_heads, preferred_element_type=F32) * scale
    dvalues = jnp.einsum("rhk,rhd->kd", prob.astype(BF), dattended, preferred_element_type=F32)
    dkv = jnp.concatenate([dkeys, dvalues], axis=1).astype(BF).reshape(nctx, rows, 2 * head)
    dkv = lax.all_to_all(dkv, CONTEXT, 0, 0, tiled=True)
    dkv = jnp.sum(dkv.astype(F32), axis=0).astype(BF)

    dq_theirs = swap(dq, XL)
    dh1_terms = wide(jnp.concatenate([dq, dq_theirs]), wq)
    dh1_mine = dh1_terms[:rows].reshape(rows, ny, shard)
    dh1_theirs = swap(dh1_terms[rows:].astype(BF), XL).astype(F32).reshape(rows, ny, shard)
    dh1 = jnp.moveaxis(pair(dh1_mine, dh1_theirs, xl), 0, 2).reshape(rows, width)
    dh1 = dh1 + wide(dkv, wkv)
    grad_hidden = (dx2 + norm_back(dh1, gain1, hat1, rate1)).astype(BF)

    def both_halves(array):
        theirs = swap(pick(array, co, 1).astype(BF), CORE)
        return pick(array, c, 1) + theirs.astype(F32)

    def both_x(array, dim):
        theirs = swap(pick(array, xo, dim).astype(BF), XL)
        return pick(array, xl, dim) + theirs.astype(F32)

    def spread(array):
        got = lax.all_to_all(array.astype(BF), ZX, 0, 0, tiled=True)
        return jnp.sum(got.astype(F32), axis=0).astype(BF)

    nzx = lax.axis_size(ZX)

    def collected(piece):
        mine = copies(piece, ZX)
        return pair(mine, swap(mine, CORE), c)

    dproj = tall(g, dy_all).reshape(2, 2, ff // 2, width)
    dfc = tall(h2_all, du).reshape(ny * 2, 2, half, block)
    dproj = both_x(both_halves(dproj), 0)
    dfc = both_x(both_halves(dfc).reshape(ny, 2, half, block), 1)
    part_proj = ff // 2 // nzx
    part_fc = half // nzx
    dproj = dproj.reshape(nzx, part_proj, width)
    dfc = jnp.moveaxis(dfc.reshape(ny, nzx, part_fc, block), 1, 0)
    both = jnp.concatenate([dproj, dfc.reshape(nzx, ny * part_fc, block)], axis=1)
    both = spread(both)
    dproj, dfc = both[:part_proj], both[part_proj:].reshape(ny, part_fc, block)
    got = [pick(dfc, y, 0)] + [shift(pick(dfc, (y + d) % ny, 0), Y, d) for d in range(1, ny)]
    got = jnp.stack(got)
    dfc = jnp.stack([pick(got, (y - k) % ny, 0) for k in range(ny)])
    both = collected(jnp.concatenate([dproj, dfc.reshape(ny * part_fc, block)]))
    grad_proj_w = both[:, :, :part_proj].reshape(ff, width).astype(F32)
    grad_fc_w = both[:, :, part_proj:].reshape(2, nzx, ny, part_fc, block)
    grad_fc_w = jnp.moveaxis(grad_fc_w, 2, 3).reshape(shard, ny * block).astype(F32)

    def columns(array):
        parts = array.reshape(rows, ny, 2 * shard)
        got = [pick(parts, y, 1)]
        got += [shift(pick(parts, (y + d) % ny, 1), Y, d) for d in range(1, ny)]
        return jnp.concatenate(got)

    def reduced(terms):
        terms = terms.reshape(2, 2, half, terms.shape[1])
        terms = both_x(both_halves(terms), 0)
        terms = spread(terms.reshape(nzx, part_fc, terms.shape[1]))
        return collected(terms).reshape(shard, terms.shape[1]).astype(F32)

    grad_out_w = reduced(tall(columns(attended), da_all))
    dqkv_all = over_y(jnp.concatenate([dq, dkv], axis=1))
    grad_qkv = reduced(tall(columns(h1), dqkv_all))

    def total(array):
        return jnp.sum(array.astype(F32), axis=0)

    vectors = [
        total(dy),
        total(dh2 * hat2),
        total(dh2),
        total(da),
        total(dq),
        total(dh1 * hat1),
        total(dh1),
    ]
    vectors = [v.reshape(2 * ny, shard) for v in vectors]
    du_sum = total(du).reshape(1, 2, ff)
    du_sum = lax.dynamic_update_slice(jnp.zeros((ny, 2, ff), F32), du_sum, (y, 0, 0))
    vectors += [du_sum.reshape(2 * ny, ff), total(dkv[:, head:]).reshape(2 * ny, -1)]
    sizes = [v.shape[1] for v in vectors]
    joined = jnp.concatenate(vectors, axis=1).astype(BF)
    joined = lax.all_to_all(joined, FSDP, 0, 0, tiled=True)
    joined = jnp.sum(joined.astype(F32), axis=0).astype(BF)
    joined = jnp.sum(copies(joined, CONTEXT).astype(F32), axis=0)
    ends = [sum(sizes[:k]) for k in range(1, len(sizes))]
    g_bproj, g_gain2, g_bias2, g_bo, g_bq, g_gain1, g_bias1, g_bfc, g_bv = jnp.split(joined, ends)

    maxima = jnp.max(copies(local_max, EVERY), axis=0)
    clip_ratio = CLIP_LIMIT / jnp.maximum(maxima, CLIP_LIMIT)
    column_scale = jnp.repeat(jnp.sqrt(clip_ratio), head)
    clipped_qw = query_weight.astype(F32) * column_scale[None, :]
    clipped_qb = query_bias.astype(F32) * lax.dynamic_slice_in_dim(
        column_scale, lax.axis_index(FSDP) * shard, shard
    )
    clipped_kw = kv_weight[:, :head].astype(F32) * jnp.sqrt(jnp.min(clip_ratio))
    return (
        output,
        grad_hidden,
        g_gain1,
        g_bias1,
        grad_qkv[:, :width],
        g_bq,
        grad_qkv[:, width:],
        g_bv,
        grad_out_w,
        g_bo,
        g_gain2,
        g_bias2,
        grad_fc_w,
        g_bfc,
        grad_proj_w,
        g_bproj,
        maxima,
        clipped_qw,
        clipped_qb,
        clipped_kw,
    )


def solution(mesh):
    torus = Mesh(mesh.devices.reshape(4, 2, 4, 2, 2), EVERY)
    tokens, table, vector, matrix = P(EVERY, None), P(FSDP, None), P(FSDP), P(FSDP, None)
    return jax.shard_map(
        shards,
        mesh=torus,
        in_specs=(
            tokens,
            tokens,
            table,
            table,
            table,
            vector,
            vector,
            matrix,
            vector,
            matrix,
            vector,
            matrix,
            vector,
            vector,
            vector,
            matrix,
            vector,
            matrix,
            vector,
        ),
        out_specs=(
            tokens,
            tokens,
            vector,
            vector,
            matrix,
            vector,
            matrix,
            vector,
            matrix,
            vector,
            vector,
            vector,
            matrix,
            vector,
            matrix,
            vector,
            P(),
            matrix,
            vector,
            matrix,
        ),
        check_vma=False,
    )
```

time: 3910 us -> 811 us (0.21)
  waiting for transfers between devices: 3240 us -> 217 us
  blocking collectives: 183 us -> 0 us
  starting transfers between devices: 28 us -> 185 us
  matrix products: 202 us -> 121 us
  other arithmetic: 73.5 us -> 121 us
    all_gather x4 -> x0, waiting for transfers between devices: 1580 us -> none  [side_by_side(): lax.all_gather(both, axis, axis=dim, tiled=True)]
    reduce_scatter x5 -> x0, waiting for transfers between devices: 1560 us -> none  [the longest x2 821 us: reduce_grads(): lax.psum_scatter(term_one.astype(jnp.bfloat16), FSDP, scatter_dimension=0...]
    ppermute x0 -> x71, waiting for transfers between devices: none -> 170 us  [shift(): return lax.ppermute(array, axis, [(i, (i + by) % n) for i in range(n)])]
    concatenate x4 -> x13, local copies, waits for them, and re-layouts: 116 us -> 2.45 us  [the longest x11 1.21 us: shards(): joined = jnp.concatenate(vectors, axis=1).astype(BF)]
    ppermute x0 -> x71, starting transfers between devices: none -> 104 us  [shift(): return lax.ppermute(array, axis, [(i, (i + by) % n) for i in range(n)])]
    dot_general x23 -> x22, matrix products: 202 us -> 121 us  [the longest x5 32 us: wide(): lax.dot_general(left, right, (((1,), (1,)), ((), ())), preferred_element_...]
    psum x1 -> x0, waiting for transfers between devices: 76.9 us -> none  [reduce_grads(): lax.psum(shard_four.astype(jnp.bfloat16), CONTEXT).astype(jnp.float32)]
    all_gather x3 -> x0, blocking collectives: 64.9 us -> none  [the longest x1 34.3 us: fetch_mlp(): lax.all_gather(gain_two, FSDP, axis=0, tiled=True)]
  transfers between devices with their start and end apart: 14 -> 85, of which waited for: 12 -> 25; matrix products, arithmetic and copies ran while one was open for 7% -> 37% of each run, Pallas kernels for 0% -> 3%
where the time goes in v1:
time: 811 us; the launch traced here: 799 us
  waiting for transfers between devices  217 us (27%)
  starting transfers between devices  185 us (23%)
  local copies, waits for them, and re-layouts  127 us (16%)
  other arithmetic  121 us (15%)
  matrix products  121 us (15%)
  Pallas kernels  24.6 us (3%)
    ppermute x71, waiting for transfers between devices, shift(): return lax.ppermute(array, axis, [(i, (i + by) % n) for i in range(n)])  170 us
    ppermute x71, starting transfers between devices, shift(): return lax.ppermute(array, axis, [(i, (i + by) % n) for i in range(n)])  104 us
    unnamed x167, local copies, waits for them, and re-layouts  51.1 us
    all_to_all x7, starting transfers between devices, copies(): lax.all_to_all(jnp.broadcast_to(array[None], (n, *array.shape)), axis, 0,...  44.9 us
    dot_general x5, matrix products, wide(): lax.dot_general(left, right, (((1,), (1,)), ((), ())), preferred_element_...  32 us
    dot_general x5, matrix products, tall(): lax.dot_general(left, right, (((0,), (0,)), ((), ())), preferred_element_...  26.8 us
    pallas_call x4, Pallas kernels, assemble(): pl.pallas_call(kernel, grid_spec=pltpu.PrefetchScalarGridSpec(num_scalar_...  24.6 us
    all_to_all x7, waiting for transfers between devices, copies(): lax.all_to_all(jnp.broadcast_to(array[None], (n, *array.shape)), axis, 0,...  22.3 us
  transfers between devices with their start and end apart: 85, of which 25 were waited for; matrix products, arithmetic and copies ran while one was open for 37% of the time, Pallas kernels for 3%

profile of v1, /device:TPU:1, one launch (start us, length us, event | category | flops | bytes accessed | tf_op | source)
XLA Modules:
  0.0 798.7 jit_solution(4500005336281566774)
XLA Ops:
  36.1 12.0 %collective-permute-start.20 = (bf16[128,2048]{1,0:T(8,128)(2,1)}, bf16[128,2048]{1,0:T(8,128)(2,1)}, u32[]{:S(2)}, u32[]{:S(2)}) collective-permute-start(bf16[128,2048]{1,0:T(8,128)(2,1)} %get-tuple-element.40), channel_id=1, source_target_pairs={{0,32},{32,64},{64,96},{96,0},{1,33},{33,65},{65,97},{97,1},{2,34}... | collective-permute-start | bytes 1572872 | tf_op jit(solution)/shard_map/ppermute | solution.py:28
  52.7 12.0 %collective-permute-done.5.refs_5_ = bf16[128,2048]{1,0:T(8,128)(2,1)S(1)} collective-permute-done((bf16[128,2048]{1,0:T(8,128)(2,1)}, bf16[128,2048]{1,0:T(8,128)(2,1)S(1)}, u32[]{:S(2)}, u32[]{:S(2)}) %collective-permute-start.5) | collective-permute-done | bytes 524320 | tf_op jit(solution)/shard_map/ppermute | solution.py:28
  65.9 8.6 %collective-permute-done.22 = bf16[128,2048]{1,0:T(8,128)(2,1)} collective-permute-done((bf16[128,2048]{1,0:T(8,128)(2,1)}, bf16[128,2048]{1,0:T(8,128)(2,1)}, u32[]{:S(2)}, u32[]{:S(2)}) %collective-permute-start.22) | collective-permute-done | bytes 524320 | tf_op jit(solution)/shard_map/ppermute | solution.py:28
  142.1 9.3 %collective-permute-done.14 = bf16[128,2048]{1,0:T(8,128)(2,1)S(1)} collective-permute-done((bf16[128,2048]{1,0:T(8,128)(2,1)}, bf16[128,2048]{1,0:T(8,128)(2,1)S(1)}, u32[]{:S(2)}, u32[]{:S(2)}) %collective-permute-start.14) | collective-permute-done | bytes 524320 | tf_op jit(solution)/shard_map/ppermute | solution.py:28
  153.2 9.8 %collective-permute-done.13 = bf16[128,2048]{1,0:T(8,128)(2,1)S(1)} collective-permute-done((bf16[128,2048]{1,0:T(8,128)(2,1)}, bf16[128,2048]{1,0:T(8,128)(2,1)S(1)}, u32[]{:S(2)}, u32[]{:S(2)}) %collective-permute-start.13) | collective-permute-done | bytes 524320 | tf_op jit(solution)/shard_map/ppermute | solution.py:28
  175.7 9.6 %collective-permute-done.25 = bf16[128,2048]{1,0:T(8,128)(2,1)S(1)} collective-permute-done((bf16[128,2048]{1,0:T(8,128)(2,1)}, bf16[128,2048]{1,0:T(8,128)(2,1)S(1)}, u32[]{:S(2)}, u32[]{:S(2)}) %collective-permute-start.25) | collective-permute-done | bytes 524320 | tf_op jit(solution)/shard_map/ppermute | solution.py:28
  212.9 9.4 %assemble.5 = bf16[2048,2048]{1,0:T(8,128)(2,1)S(1)} custom-call(s32[16]{0:T(128)S(1)} %stack.346.at_ref, bf16[256,2048]{1,0:T(8,128)(2,1)S(1)} %copy-done.11, bf16[384,2048]{1,0:T(8,128)(2,1)} %bitcast.41.refs_1_, bf16[384,2048]{1,0:T(8,128)(2,1)} %bitcast.42.refs_2_, bf16[512,2048]{1,0:T(8,128)(2,1)} %bitcast.49.refs_3_, bf16[512,2048]{1,0:T(8,128)(2,1)} %bitcast.50.refs_4_), custom_call_target="tpu_custom_call" | custom-call | bytes 16777216 | tf_op jit(solution)/shard_map/assemble/pallas_call | solution.py:66
  246.6 9.4 %assemble.6 = bf16[2048,2048]{1,0:T(8,128)(2,1)S(1)} custom-call(s32[16]{0:T(128)S(1)} %stack.346.at_ref, bf16[256,2048]{1,0:T(8,128)(2,1)S(1)} %copy-done.7, bf16[384,2048]{1,0:T(8,128)(2,1)} %bitcast.57.refs_1_, bf16[384,2048]{1,0:T(8,128)(2,1)} %bitcast.58.refs_2_, bf16[512,2048]{1,0:T(8,128)(2,1)} %bitcast.65.refs_3_, bf16[512,2048]{1,0:T(8,128)(2,1)} %bitcast.66.refs_4_), custom_call_target="tpu_custom_call" | custom-call | bytes 16777216 | tf_op jit(solution)/shard_map/assemble/pallas_call | solution.py:66
  279.6 10.5 %convert_reduce_fusion = (bf16[2048]{0:T(1024)(128)(2,1)S(1)}, bf16[512,2048]{1,0:T(8,128)(2,1)S(1)}) fusion(f32[512,2048]{1,0:T(8,128)} %copy-done.68, f32[2048]{0:T(1024)S(1)} %bitcast.373, bf16[2048,2048]{1,0:T(8,128)(2,1)S(1)} %assemble.7, bf16[128,2048]{1,0:T(8,128)(2,1)S(1)} %collective-permute-done.39, ...), kind=kOutput, calls=%fused_computation.40 | convolution fusion | flops 4327471104 | bytes 16789504 | tf_op jit(solution)/shard_map/dot_general | solution.py:94
  290.1 10.5 %fusion.160 = (bf16[512,2048]{1,0:T(8,128)(2,1)S(1)}, f32[512,2048]{1,0:T(8,128)}) fusion(bf16[512,2048]{1,0:T(8,128)(2,1)S(1)} %get-tuple-element.97, bf16[2048,2048]{1,0:T(8,128)(2,1)} %copy-done.3), kind=kOutput, calls=%fused_computation.306 | convolution fusion | flops 4296015872 | bytes 16777216 | tf_op jit(solution)/shard_map/dot_general | solution.py:94
  322.5 14.1 %fusion.129 = f32[2048,2048]{1,0:T(8,128)} fusion(bf16[128,2048]{1,0:T(8,128)(2,1)S(1)} %collective-permute-done.39, bf16[128,2048]{1,0:T(8,128)(2,1)} %copy-done.63, bf16[128,2048]{1,0:T(8,128)(2,1)} %copy-done.64, bf16[128,2048]{1,0:T(8,128)(2,1)S(1)} %bitcast.329, f32[512,2048]{1,0:T(8,128)} %copy-done.68, f32[2048]{0:T(1024)S(1)} %bitcast.374), kind=kOutput, calls=%fused_computation.203 | convolution fusion | flops 4313841664 | bytes 23076864 | tf_op jit(solution)/shard_map/dot_general | solution.py:90
  352.8 10.0 %copy.231 = bf16[256,8,16,128]{3,2,1,0:T(8,128)(2,1)} copy(bf16[256,8,16,128]{3,1,2,0:T(8,128)(2,1)} %bitcast.308) | data formatting | bytes 16777216
  384.6 11.9 %multiply_reduce_fusion = (f32[128,16]{0,1:T(8,128)S(1)}, f32[128,16,2048]{2,0,1:T(8,128)}) fusion(f32[128,16]{0,1:T(8,128)S(1)} %log_add_fusion, f32[128,16,2048]{2,0,1:T(8,128)} %copy-done.22, pred[128,2048]{1,0:T(8,128)(4,1)S(1)} %compare_and_fusion.1, bf16[2048,256]{1,0:T(8,128)(2,1)} %bitcast.18, bf16[128,2048]{1,0:T(8,128)(2,1)S(1)} %convolution_convert_fusion), kind=kOutput, calls=%fused_computation.5 | convolution fusion | flops 1094711296 | bytes 34881536 | tf_op jit(solution)/shard_map/rhd,kd->rhk/dot_general | solution.py:282
  405.8 10.1 %bitcast_add_fusion.1 = f32[2,512,2048]{2,1,0:T(8,128)} fusion(bf16[2,512,2048]{2,1,0:T(8,128)(2,1)} %collective-permute-done.63, f32[2,2,512,2048]{3,2,1,0:T(8,128)} %bitcast.316, s32[]{:T(128)S(6)} %select_n.521), kind=kLoop, calls=%fused_computation.13 | loop fusion | flops 4194304 | bytes 20971524 | tf_op jit(solution)/shard_map/add | solution.py:303
  421.2 12.1 %multiply_convert_fusion = bf16[128,16,2048]{2,0,1:T(8,128)(2,1)S(1)} fusion(f32[128,16,2048]{2,0,1:T(8,128)} %get-tuple-element.92, f32[128,16]{0,1:T(8,128)S(1)} %get-tuple-element.91, f32[128,16]{0,1:T(8,128)S(1)} %log_add_fusion, f32[128,16,2048]{2,0,1:T(8,128)} %copy-done.22, pred[128,2048]{1,0:T(8,128)(4,1)S(1)} %compare_and_fusion.1), kind=kLoop, calls=%fused_computation.4 | loop fusion | flops 25165824 | bytes 42221568 | tf_op jit(solution)/shard_map/convert_element_type | solution.py:284
  437.0 8.4 %fusion.53 = bf16[16,128,128]{1,2,0:T(8,128)(2,1)S(1)} fusion(bf16[128,16,128,1]{2,1,0,3:T(8,128)(2,1)S(1)} %bitcast.345, bf16[16,128,16,128]{1,0,3,2:T(8,128)(2,1)} %bitcast.319), kind=kOutput, calls=%fused_computation.98 | convolution fusion | flops 1074003968 | bytes 9437184 | tf_op jit(solution)/shard_map/rhk,rhd->kd/dot_general | solution.py:288
  457.9 37.9 %collective-permute-done.64 = bf16[512,2048]{1,0:T(8,128)(2,1)} collective-permute-done((bf16[512,2048]{1,0:T(8,128)(2,1)}, bf16[512,2048]{1,0:T(8,128)(2,1)}, u32[]{:S(2)}, u32[]{:S(2)}) %collective-permute-start.64) | collective-permute-done | bytes 2097184 | tf_op jit(solution)/shard_map/ppermute | solution.py:28
  501.9 10.6 %all-to-all-done.4 = bf16[16,128,256]{1,2,0:T(8,128)(2,1)S(1)} async-done(((bf16[16,128,256]{1,2,0:T(8,128)(2,1)}), bf16[16,128,256]{1,2,0:T(8,128)(2,1)S(1)}, u32[]{:S(2)}, u32[]{:S(2)}) %all-to-all-start.4) | async-done | bytes 1048608 | tf_op jit(solution)/shard_map/all_to_all | solution.py:290
  544.0 12.3 %collective-permute-done.57 = bf16[128,2048]{1,0:T(8,128)(2,1)} collective-permute-done((bf16[128,2048]{1,0:T(8,128)(2,1)}, bf16[128,2048]{1,0:T(8,128)(2,1)}, u32[]{:S(2)}, u32[]{:S(2)}) %collective-permute-start.57) | collective-permute-done | bytes 524320 | tf_op jit(solution)/shard_map/ppermute | solution.py:28
  574.6 8.2 %all-to-all-start.2 = ((bf16[16,8,2048]{2,1,0:T(8,128)(2,1)}), bf16[16,8,2048]{2,1,0:T(8,128)(2,1)}, u32[]{:S(2)}, u32[]{:S(2)}) async-start(bf16[16,8,2048]{2,1,0:T(8,128)(2,1)} %get-tuple-element.55), calls=%async_computation.2 | async-start | bytes 1048576 | tf_op jit(solution)/shard_map/all_to_all | solution.py:261
  637.2 27.6 %collective-permute-done.44 = bf16[128,1024]{1,0:T(8,128)(2,1)S(1)} collective-permute-done((bf16[128,1024]{1,0:T(8,128)(2,1)}, bf16[128,1024]{1,0:T(8,128)(2,1)S(1)}, u32[]{:S(2)}, u32[]{:S(2)}) %collective-permute-start.44) | collective-permute-done | bytes 262176 | tf_op jit(solution)/shard_map/ppermute | solution.py:28
  724.3 10.5 %all-to-all-start.6 = ((bf16[16,2,1416]{2,1,0:T(2,128)(2,1)}), bf16[16,2,1416]{2,1,0:T(2,128)(2,1)S(1)}, u32[]{:S(2)}, u32[]{:S(2)}) async-start(bf16[16,2,1416]{2,1,0:T(2,128)(2,1)} %reshape.665), calls=%async_computation.6 | async-start | bytes 196608 | tf_op jit(solution)/shard_map/all_to_all | solution.py:37
  749.8 8.2 %all-to-all-done.8 = bf16[8,16,2304]{2,1,0:T(8,128)(2,1)S(1)} async-done(((bf16[8,16,2304]{2,1,0:T(8,128)(2,1)}), bf16[8,16,2304]{2,1,0:T(8,128)(2,1)S(1)}, u32[]{:S(2)}, u32[]{:S(2)}) %all-to-all-start.8) | async-done | bytes 589856 | tf_op jit(solution)/shard_map/all_to_all | solution.py:37
  782.5 11.1 %copy.233 = f32[32,8,4,2048]{3,1,2,0:T(8,128)} copy(f32[32,8,4,2048]{3,2,1,0:T(4,128)S(1)} %bitcast.309) | data formatting | bytes 16777216
  (495 shorter events, 500.9 us)
Async XLA Ops:
  18.6 80.3 %all-to-all-start = ((bf16[8,272,256]{2,1,0:T(8,128)(2,1)}), bf16[8,272,256]{2,1,0:T(8,128)(2,1)}, u32[]{:S(2)}, u32[]{:S(2)}) async-start(bf16[8,272,256]{2,1,0:T(8,128)(2,1)} %broadcast_in_dim.56), calls=%async_computation | async-start | bytes 2228224 | tf_op jit(solution)/shard_map/all_to_all | solution.py:37
  34.9 42.9 %collective-permute-start.21 = (bf16[128,2048]{1,0:T(8,128)(2,1)}, bf16[128,2048]{1,0:T(8,128)(2,1)}, u32[]{:S(2)}, u32[]{:S(2)}) collective-permute-start(bf16[128,2048]{1,0:T(8,128)(2,1)} %get-tuple-element.39), channel_id=1, source_target_pairs={{0,64},{32,96},{64,0},{96,32},{1,65},{33,97},{65,1},{97,33},{2,66}... | collective-permute-start | bytes 1572872 | tf_op jit(solution)/shard_map/ppermute | solution.py:28
  36.1 49.7 %collective-permute-start.20 = (bf16[128,2048]{1,0:T(8,128)(2,1)}, bf16[128,2048]{1,0:T(8,128)(2,1)}, u32[]{:S(2)}, u32[]{:S(2)}) collective-permute-start(bf16[128,2048]{1,0:T(8,128)(2,1)} %get-tuple-element.40), channel_id=1, source_target_pairs={{0,32},{32,64},{64,96},{96,0},{1,33},{33,65},{65,97},{97,1},{2,34}... | collective-permute-start | bytes 1572872 | tf_op jit(solution)/shard_map/ppermute | solution.py:28
  112.8 76.0 %all-to-all-start.1 = ((bf16[16,128,256]{2,1,0:T(8,128)(2,1)}), bf16[16,128,256]{2,1,0:T(8,128)(2,1)}, u32[]{:S(2)}, u32[]{:S(2)}) async-start(bf16[16,128,256]{2,1,0:T(8,128)(2,1)} %broadcast_in_dim.57), calls=%async_computation.1 | async-start | bytes 2097152 | tf_op jit(solution)/shard_map/all_to_all | solution.py:37
  140.4 44.9 %collective-permute-start.25 = (bf16[128,2048]{1,0:T(8,128)(2,1)}, bf16[128,2048]{1,0:T(8,128)(2,1)S(1)}, u32[]{:S(2)}, u32[]{:S(2)}) collective-permute-start(bf16[128,2048]{1,0:T(8,128)(2,1)} %collective-permute-done.24), channel_id=1, source_target_pairs={{0,4},{4,8},{8,12},{12,0},{1,5},{5,9},{9,13},{13,1},{2,6},{6,10},{... | collective-permute-start | bytes 1572872 | tf_op jit(solution)/shard_map/ppermute | solution.py:28
  151.4 61.5 %collective-permute-start.11 = (bf16[3,128,2048]{2,1,0:T(8,128)(2,1)}, bf16[3,128,2048]{2,1,0:T(8,128)(2,1)}, u32[]{:S(2)}, u32[]{:S(2)}) collective-permute-start(bf16[3,128,2048]{2,1,0:T(8,128)(2,1)} %pad_maximum_fusion.6), channel_id=1, source_target_pairs={{0,1},{1,0},{2,3},{3,2},{4,5},{5,4},{6,7},{7,6},{8,9},{9,8},{10,11... | collective-permute-start | bytes 4718600 | tf_op jit(solution)/shard_map/ppermute | solution.py:28
  167.0 75.8 %collective-permute-start.23 = (bf16[3,128,2048]{2,1,0:T(8,128)(2,1)}, bf16[3,128,2048]{2,1,0:T(8,128)(2,1)}, u32[]{:S(2)}, u32[]{:S(2)}) collective-permute-start(bf16[3,128,2048]{2,1,0:T(8,128)(2,1)} %pad_maximum_fusion.7), channel_id=1, source_target_pairs={{0,1},{1,0},{2,3},{3,2},{4,5},{5,4},{6,7},{7,6},{8,9},{9,8},{10,11... | collective-permute-start | bytes 4718600 | tf_op jit(solution)/shard_map/ppermute | solution.py:28
  173.9 57.1 %collective-permute-start.33 = (bf16[4,128,2048]{2,1,0:T(8,128)(2,1)S(1)}, bf16[4,128,2048]{2,1,0:T(8,128)(2,1)}, u32[]{:S(2)}, u32[]{:S(2)}) collective-permute-start(bf16[4,128,2048]{2,1,0:T(8,128)(2,1)S(1)} %pad_maximum_fusion.4), channel_id=1, source_target_pairs={{0,1},{1,0},{2,3},{3,2},{4,5},{5,4},{6,7},{7,6},{8,9},{9,8},{10,11... | collective-permute-start | bytes 6291464 | tf_op jit(solution)/shard_map/ppermute | solution.py:28
  188.6 57.0 %collective-permute-start.28 = (bf16[4,128,2048]{2,1,0:T(8,128)(2,1)}, bf16[4,128,2048]{2,1,0:T(8,128)(2,1)}, u32[]{:S(2)}, u32[]{:S(2)}) collective-permute-start(bf16[4,128,2048]{2,1,0:T(8,128)(2,1)} %pad_maximum_fusion.3), channel_id=1, source_target_pairs={{0,1},{1,0},{2,3},{3,2},{4,5},{5,4},{6,7},{7,6},{8,9},{9,8},{10,11... | collective-permute-start | bytes 6291464 | tf_op jit(solution)/shard_map/ppermute | solution.py:28
  188.8 44.5 %all-to-all-start.3 = ((bf16[16,8,2048]{2,1,0:T(8,128)(2,1)}), bf16[16,8,2048]{2,1,0:T(8,128)(2,1)S(1)}, u32[]{:S(2)}, u32[]{:S(2)}) async-start(bf16[16,8,2048]{2,1,0:T(8,128)(2,1)} %fusion.35), calls=%async_computation.3 | async-start | bytes 1048576 | tf_op jit(solution)/shard_map/all_to_all | solution.py:261
  301.7 42.9 %collective-permute-start.41 = (bf16[128,2048]{1,0:T(8,128)(2,1)}, bf16[128,2048]{1,0:T(8,128)(2,1)}, u32[]{:S(2)}, u32[]{:S(2)}) collective-permute-start(bf16[128,2048]{1,0:T(8,128)(2,1)} %get-tuple-element.44), channel_id=1, source_target_pairs={{0,64},{32,96},{64,0},{96,32},{1,65},{33,97},{65,1},{97,33},{2,66}... | collective-permute-start | bytes 1572872 | tf_op jit(solution)/shard_map/ppermute | solution.py:28
  302.6 44.4 %collective-permute-start.40 = (bf16[128,2048]{1,0:T(8,128)(2,1)}, bf16[128,2048]{1,0:T(8,128)(2,1)}, u32[]{:S(2)}, u32[]{:S(2)}) collective-permute-start(bf16[128,2048]{1,0:T(8,128)(2,1)} %get-tuple-element.42), channel_id=1, source_target_pairs={{0,96},{32,0},{64,32},{96,64},{1,97},{33,1},{65,33},{97,65},{2,98}... | collective-permute-start | bytes 1572872 | tf_op jit(solution)/shard_map/ppermute | solution.py:28
  305.8 65.0 %collective-permute-start.36 = (bf16[128,2048]{1,0:T(8,128)(2,1)}, bf16[128,2048]{1,0:T(8,128)(2,1)}, u32[]{:S(2)}, u32[]{:S(2)}) collective-permute-start(bf16[128,2048]{1,0:T(8,128)(2,1)} %get-tuple-element.46), channel_id=1, source_target_pairs={{0,32},{32,64},{64,96},{96,0},{1,33},{33,65},{65,97},{97,1},{2,34}... | collective-permute-start | bytes 1572872 | tf_op jit(solution)/shard_map/ppermute | solution.py:28
  321.1 75.3 %collective-permute-start.65 = (bf16[8,128,2048]{2,1,0:T(8,128)(2,1)}, bf16[8,128,2048]{2,1,0:T(8,128)(2,1)}, u32[]{:S(2)}, u32[]{:S(2)}) collective-permute-start(bf16[8,128,2048]{2,1,0:T(8,128)(2,1)} %fusion.19), channel_id=1, source_target_pairs={{0,1},{1,0},{2,3},{3,2},{4,5},{5,4},{6,7},{7,6},{8,9},{9,8},{10,11... | collective-permute-start | bytes 12582920 | tf_op jit(solution)/shard_map/ppermute | solution.py:28
  347.1 58.7 %collective-permute-start.63 = (bf16[2,512,2048]{2,1,0:T(8,128)(2,1)}, bf16[2,512,2048]{2,1,0:T(8,128)(2,1)}, u32[]{:S(2)}, u32[]{:S(2)}) collective-permute-start(bf16[2,512,2048]{2,1,0:T(8,128)(2,1)} %fusion.18), channel_id=1, source_target_pairs={{0,1},{1,0},{2,3},{3,2},{4,5},{5,4},{6,7},{7,6},{8,9},{9,8},{10,11... | collective-permute-start | bytes 12582920 | tf_op jit(solution)/shard_map/ppermute | solution.py:28
  363.4 83.0 %all-to-all-start.13 = ((f32[128,1,16]{2,1,0:T(1,128)}), f32[128,1,16]{2,1,0:T(1,128)S(1)}, u32[]{:S(2)}, u32[]{:S(2)}) async-start(f32[128,1,16]{2,1,0:T(1,128)} %broadcast_in_dim.66), calls=%async_computation.13 | async-start | bytes 131072 | tf_op jit(solution)/shard_map/all_to_all | solution.py:37
  404.3 49.8 %collective-permute-start.66 = (bf16[4,128,2048]{2,1,0:T(8,128)(2,1)}, bf16[4,128,2048]{2,1,0:T(8,128)(2,1)}, u32[]{:S(2)}, u32[]{:S(2)}) collective-permute-start(bf16[4,128,2048]{2,1,0:T(8,128)(2,1)} %fusion.37), channel_id=1, source_target_pairs={{0,16},{16,0},{1,17},{17,1},{2,18},{18,2},{3,19},{19,3},{4,20},{20... | collective-permute-start | bytes 6291464 | tf_op jit(solution)/shard_map/ppermute | solution.py:28
  419.7 76.0 %collective-permute-start.64 = (bf16[512,2048]{1,0:T(8,128)(2,1)}, bf16[512,2048]{1,0:T(8,128)(2,1)}, u32[]{:S(2)}, u32[]{:S(2)}) collective-permute-start(bf16[512,2048]{1,0:T(8,128)(2,1)} %fusion.36), channel_id=1, source_target_pairs={{0,16},{16,0},{1,17},{17,1},{2,18},{18,2},{3,19},{19,3},{4,20},{20... | collective-permute-start | bytes 6291464 | tf_op jit(solution)/shard_map/ppermute | solution.py:28
  446.4 66.1 %all-to-all-start.4 = ((bf16[16,128,256]{1,2,0:T(8,128)(2,1)}), bf16[16,128,256]{1,2,0:T(8,128)(2,1)S(1)}, u32[]{:S(2)}, u32[]{:S(2)}) async-start(bf16[16,128,256]{1,2,0:T(8,128)(2,1)} %pad_maximum_fusion.8), calls=%async_computation.4 | async-start | bytes 2097152 | tf_op jit(solution)/shard_map/all_to_all | solution.py:290
  512.5 62.1 %all-to-all-start.11 = ((bf16[8,128,2048]{2,1,0:T(8,128)(2,1)}), bf16[8,128,2048]{2,1,0:T(8,128)(2,1)}, u32[]{:S(2)}, u32[]{:S(2)}) async-start(bf16[8,128,2048]{2,1,0:T(8,128)(2,1)} %pad_maximum_fusion), calls=%async_computation.11 | async-start | bytes 8388608 | tf_op jit(solution)/shard_map/all_to_all | solution.py:310
  531.8 69.6 %collective-permute-start.47 = (bf16[128,512]{1,0:T(8,128)(2,1)}, bf16[128,512]{1,0:T(8,128)(2,1)}, u32[]{:S(2)}, u32[]{:S(2)}) collective-permute-start(bf16[128,512]{1,0:T(8,128)(2,1)} %bitcast.301), channel_id=1, source_target_pairs={{0,96},{32,0},{64,32},{96,64},{1,97},{33,1},{65,33},{97,65},{2,98}... | collective-permute-start | bytes 393224 | tf_op jit(solution)/shard_map/ppermute | solution.py:28
  534.5 68.0 %collective-permute-start.46 = (bf16[128,512]{1,0:T(8,128)(2,1)}, bf16[128,512]{1,0:T(8,128)(2,1)}, u32[]{:S(2)}, u32[]{:S(2)}) collective-permute-start(bf16[128,512]{1,0:T(8,128)(2,1)} %bitcast.302), channel_id=1, source_target_pairs={{0,64},{32,96},{64,0},{96,32},{1,65},{33,97},{65,1},{97,33},{2,66}... | collective-permute-start | bytes 393224 | tf_op jit(solution)/shard_map/ppermute | solution.py:28
  613.3 68.5 %all-to-all-start.12 = ((bf16[8,128,2048]{2,1,0:T(8,128)(2,1)}), bf16[8,128,2048]{2,1,0:T(8,128)(2,1)}, u32[]{:S(2)}, u32[]{:S(2)}) async-start(bf16[8,128,2048]{2,1,0:T(8,128)(2,1)} %broadcast_in_dim.65), calls=%async_computation.12 | async-start | bytes 8388608 | tf_op jit(solution)/shard_map/all_to_all | solution.py:37
  686.7 79.2 %collective-permute-start.70 = (bf16[8,128,2048]{2,1,0:T(8,128)(2,1)}, bf16[8,128,2048]{2,1,0:T(8,128)(2,1)}, u32[]{:S(2)}, u32[]{:S(2)}) collective-permute-start(bf16[8,128,2048]{2,1,0:T(8,128)(2,1)} %all-to-all-done.12), channel_id=1, source_target_pairs={{0,1},{1,0},{2,3},{3,2},{4,5},{5,4},{6,7},{7,6},{8,9},{9,8},{10,11... | collective-permute-start | bytes 12582920 | tf_op jit(solution)/shard_map/ppermute | solution.py:28
  (134 other events, 2836.2 us)

commit v2 on v1

v2 whole, which is shorter than its diff:
```python
import functools
import math

import jax
import jax.numpy as jnp
from jax import lax
from jax.experimental import pallas as pl
from jax.experimental.pallas import tpu as pltpu
from jax.sharding import Mesh
from jax.sharding import PartitionSpec as P

Y, XL, Z, XH, CORE = ("fsdp_0", "fsdp_1", "context_0", "context_1", "context_2")
FSDP = (Y, XL)
CONTEXT = (Z, XH, CORE)
ZX = (Z, XH)
EVERY = (Y, XL, Z, XH, CORE)

EPSILON = 1e-05
CLIP_LIMIT = 4.0
MASKED = -1e30
LANES = 128
BRIEF = pl.CostEstimate(flops=0, bytes_accessed=1024, transcendentals=0)
COST = pl.CostEstimate(flops=30_000_000_000, bytes_accessed=1024, transcendentals=0)
BF = jnp.bfloat16
F32 = jnp.float32


def shift(array, axis, by):
    n = lax.axis_size(axis)
    return lax.ppermute(array, axis, [(i, (i + by) % n) for i in range(n)])


def swap(array, axis):
    return shift(array, axis, 1)


def copies(array, axis):
    n = lax.axis_size(axis)
    return lax.all_to_all(jnp.broadcast_to(array[None], (n, *array.shape)), axis, 0, 0, tiled=True)


def gate(values, *done):
    return lax.optimization_barrier((values, done))[0]


def pick(array, index, dim):
    return lax.dynamic_index_in_dim(array, index, dim, keepdims=False)


def pair(own, other, index):
    return jnp.where(index == 0, jnp.stack([own, other]), jnp.stack([other, own]))


def numbers(values):
    return jnp.stack([jnp.asarray(v, jnp.int32) for v in values])


def cut(places, width, done=()):
    arrays = [array for array, _, _ in places]

    def kernel(at_ref, *refs):
        for source, out in zip(refs, refs[len(arrays) + len(done) :]):
            out[...] = source[...]

    def block_of(i):
        return lambda k, at: (at[2 * i], at[2 * i + 1])

    return pl.pallas_call(
        kernel,
        grid_spec=pltpu.PrefetchScalarGridSpec(
            num_scalar_prefetch=1,
            grid=(1,),
            in_specs=[pl.BlockSpec((LANES, width), block_of(i)) for i in range(len(arrays))]
            + [pl.BlockSpec(memory_space=pl.ANY)] * len(done),
            out_specs=[pl.BlockSpec((LANES, width), lambda k, at: (0, 0))] * len(arrays),
        ),
        out_shape=[jax.ShapeDtypeStruct((LANES, width), a.dtype) for a in arrays],
        compiler_params=pltpu.CompilerParams(vmem_limit_bytes=32 * 2**20),
        cost_estimate=COST,
        name="cut",
    )(numbers([n for _, row, column in places for n in (row, column)]), *arrays, *done)


def pack(shared, quarters, where):
    rows = [a.shape[0] for a in shared] + [2 * LANES] * len(quarters)
    wide = shared[0].shape[1]
    count = 8

    def kernel(at_ref, *refs):
        out, start = refs[-1], 0
        for k, length in enumerate(rows):
            if k < len(shared):
                out[0, start : start + length] = refs[k][...]
            else:
                out[0, start : start + LANES] = refs[k][:, :wide]
                out[0, start + LANES : start + length] = refs[k][:, wide:]
            start += length

    def block_of(i):
        return lambda k, at: (at[2 * (i * count + k)], at[2 * (i * count + k) + 1])

    return pl.pallas_call(
        kernel,
        grid_spec=pltpu.PrefetchScalarGridSpec(
            num_scalar_prefetch=1,
            grid=(count,),
            in_specs=[whole(*a.shape) for a in shared]
            + [pl.BlockSpec((LANES, 2 * wide), block_of(i)) for i in range(len(quarters))],
            out_specs=pl.BlockSpec((1, sum(rows), wide), lambda k, at: (k, 0, 0)),
        ),
        out_shape=jax.ShapeDtypeStruct((count, sum(rows), wide), BF),
        compiler_params=pltpu.CompilerParams(vmem_limit_bytes=32 * 2**20),
        cost_estimate=COST,
        name="pack",
    )(numbers([n for by in where for k in range(count) for n in by(k)]), *shared, *quarters)


def repeat_block(array, row, count, done=()):
    width = array.shape[1]

    def kernel(at_ref, in_ref, *refs):
        refs[-1][0] = in_ref[...]

    return pl.pallas_call(
        kernel,
        grid_spec=pltpu.PrefetchScalarGridSpec(
            num_scalar_prefetch=1,
            grid=(count,),
            in_specs=[pl.BlockSpec((LANES, width), lambda k, at: (at[0], 0))]
            + [pl.BlockSpec(memory_space=pl.ANY)] * len(done),
            out_specs=pl.BlockSpec((1, LANES, width), lambda k, at: (k, 0, 0)),
        ),
        out_shape=jax.ShapeDtypeStruct((count, LANES, width), BF),
        compiler_params=pltpu.CompilerParams(vmem_limit_bytes=32 * 2**20),
        cost_estimate=COST,
        name="repeat_block",
    )(numbers([row]), array, *done)


def assemble_quarters(pieces, core_and_z, cost, done=()):
    shards, _, wide = pieces[0].shape
    width = 8 * wide
    steps = 2 * len(pieces)

    def kernel(at_ref, *refs):
        for k, piece in enumerate(refs[: len(pieces)]):

            @pl.when(pl.program_id(0) // 2 == k)
            def _(piece=piece):
                refs[-1][...] = piece[...].reshape(shards, 1, LANES, wide)

    def block_of(i):
        return lambda k, at: (0, jnp.clip(k - 2 * i, 0, 1), 0)

    at = [n for core, z in core_and_z for j in (0, 1) for n in (core, 2 * z + j)]
    return pl.pallas_call(
        kernel,
        grid_spec=pltpu.PrefetchScalarGridSpec(
            num_scalar_prefetch=1,
            grid=(steps,),
            in_specs=[pl.BlockSpec((shards, LANES, wide), block_of(i)) for i in range(len(pieces))]
            + [pl.BlockSpec(memory_space=pl.ANY)] * len(done),
            out_specs=pl.BlockSpec(
                (shards, 1, LANES, wide), lambda k, at: (0, at[2 * k], 0, at[2 * k + 1])
            ),
        ),
        out_shape=jax.ShapeDtypeStruct((shards, 2, LANES, width), BF),
        compiler_params=pltpu.CompilerParams(vmem_limit_bytes=48 * 2**20),
        cost_estimate=cost,
        name="assemble_quarters",
    )(numbers(at), *pieces, *done).reshape(shards * 2 * LANES, width)


def side_by_side(full, parts, places):
    rows = parts[0].shape[0]
    part = 4 * LANES
    widths = [a.shape[1] for a in full] + [part] * len(parts)
    total, count, n = sum(widths), len(places), len(widths)

    def kernel(at_ref, *refs):
        for k, out in enumerate(refs[n:]):

            @pl.when(pl.program_id(0) == k)
            def _(out=out):
                start = 0
                for source, width in zip(refs[:n], widths):
                    out[:, start : start + width] = source[...]
                    start += width

    return pl.pallas_call(
        kernel,
        grid_spec=pltpu.PrefetchScalarGridSpec(
            num_scalar_prefetch=1,
            grid=(count,),
            in_specs=[whole(*a.shape) for a in full]
            + [pl.BlockSpec((rows, part), lambda k, at: (0, at[k]))] * len(parts),
            out_specs=[whole(rows, total)] * count,
        ),
        out_shape=[jax.ShapeDtypeStruct((rows, total), BF)] * count,
        compiler_params=pltpu.CompilerParams(vmem_limit_bytes=32 * 2**20),
        cost_estimate=COST,
        name="side_by_side",
    )(numbers(places), *full, *parts)


def assemble(pieces, rows, width, done=()):
    arrays = [a.reshape(-1, a.shape[-1]) for a, _, _ in pieces]
    counts = [a.shape[0] // LANES for a in arrays]
    firsts = [sum(counts[:k]) for k in range(len(counts))]
    steps = rows // LANES
    at = [o // LANES for _, _, offsets in pieces for o in offsets]

    def kernel(at_ref, *refs):
        step, out = pl.program_id(0), refs[-1]
        for source, first, count in zip(refs, firsts, counts):

            @pl.when((step >= first) & (step < first + count))
            def _(source=source):
                out[...] = source[...]

    def block_of(i):
        return lambda k, at: (jnp.clip(k - firsts[i], 0, counts[i] - 1), at[steps + i])

    return pl.pallas_call(
        kernel,
        grid_spec=pltpu.PrefetchScalarGridSpec(
            num_scalar_prefetch=1,
            grid=(steps,),
            in_specs=[pl.BlockSpec((LANES, width), block_of(i)) for i in range(len(arrays))]
            + [pl.BlockSpec(memory_space=pl.ANY)] * len(done),
            out_specs=pl.BlockSpec((LANES, width), lambda k, at: (at[k], 0)),
        ),
        out_shape=jax.ShapeDtypeStruct((rows, width), arrays[0].dtype),
        compiler_params=pltpu.CompilerParams(vmem_limit_bytes=32 * 2**20),
        cost_estimate=COST,
        name="assemble",
    )(numbers(at + [column for _, column, _ in pieces]), *arrays, *done)


def lay_both(pieces, at, proj_rows, fc_rows, count):
    steps = len(at)
    per = steps // 2
    columns = pieces[0].shape[-1]

    def kernel(at_ref, *refs):
        step = pl.program_id(0)
        proj_out, fc_out = refs[-2:]
        for k in range(steps):
            fc_ref = refs[(per + 1) * (k // per)]
            proj_ref = refs[(per + 1) * (k // per) + 1 + k % per]

            @pl.when(step == k)
            def _(fc_ref=fc_ref, proj_ref=proj_ref):
                part = proj_rows // 2
                for x in (0, 1):
                    for h in (0, 1):
                        proj_out[part * x : part * (x + 1), columns * h : columns * (h + 1)] = (
                            proj_ref[x, part * h : part * (h + 1)].astype(F32)
                        )
                    for j in range(count):
                        start = columns * (2 * j + x)
                        fc_out[:, start : start + columns] = fc_ref[
                            x, 0, fc_rows * j : fc_rows * (j + 1)
                        ].astype(F32)

    fc_rows_all = count * fc_rows

    def fc_block(i):
        return pl.BlockSpec(
            (2, 1, fc_rows_all, columns),
            lambda k, at: (0, jnp.clip(k - i * per, 0, per - 1), 0, 0),
        )

    specs = []
    for i in (0, 1):
        specs += [fc_block(i)] + [whole(*p.shape) for p in pieces[1 : per + 1]]
    shapes = [(proj_rows, 2 * columns), (fc_rows, 2 * count * columns)]
    return pl.pallas_call(
        kernel,
        grid_spec=pltpu.PrefetchScalarGridSpec(
            num_scalar_prefetch=1,
            grid=(steps,),
            in_specs=specs,
            out_specs=[pl.BlockSpec(shape, lambda k, at: (at[k], 0)) for shape in shapes],
        ),
        out_shape=[jax.ShapeDtypeStruct((steps * n, width), F32) for n, width in shapes],
        compiler_params=pltpu.CompilerParams(vmem_limit_bytes=56 * 2**20),
        cost_estimate=COST,
        name="lay_both",
    )(numbers(at), *pieces)


def add_cut(arrays, view, block, places):
    count, dims = len(places), len(view)

    def kernel(at_ref, *refs):
        total = functools.reduce(jnp.add, [r[...].astype(F32) for r in refs[: len(arrays)]])
        for k, out in enumerate(refs[len(arrays) :]):

            @pl.when(pl.program_id(0) == k)
            def _(out=out):
                out[...] = total.astype(BF)

    def index(k, at):
        return tuple(at[k * dims + i] for i in range(dims))

    return pl.pallas_call(
        kernel,
        grid_spec=pltpu.PrefetchScalarGridSpec(
            num_scalar_prefetch=1,
            grid=(count,),
            in_specs=[pl.BlockSpec(block, index)] * len(arrays),
            out_specs=[whole(*block)] * count,
        ),
        out_shape=[jax.ShapeDtypeStruct(block, BF)] * count,
        compiler_params=pltpu.CompilerParams(vmem_limit_bytes=40 * 2**20),
        cost_estimate=COST,
        name="add_cut",
    )(numbers([i for place in places for i in place]), *[a.reshape(view) for a in arrays])


def laid_out(mine, theirs, core, shapes, cut):
    count, rows, width = mine.shape

    def kernel(core_ref, mine_ref, theirs_ref, *outs):
        def write(piece):
            for out, value in zip(outs, cut(piece.astype(F32))):
                out[...] = value

        step = pl.program_id(0)

        @pl.when(step < count)
        def _():
            write(mine_ref[0])

        @pl.when(step >= count)
        def _():
            write(theirs_ref[0])

    def out_block(k, core_ref):
        own = (k < count).astype(jnp.int32)
        return (jnp.where(core_ref[0] == own, 1 - 0 * k, 0 * k) * count + k % count, 0)

    return pl.pallas_call(
        kernel,
        grid_spec=pltpu.PrefetchScalarGridSpec(
            num_scalar_prefetch=1,
            grid=(2 * count,),
            in_specs=[
                pl.BlockSpec((1, rows, width), lambda k, r: (jnp.minimum(k, count - 1), 0, 0)),
                pl.BlockSpec((1, rows, width), lambda k, r: (jnp.maximum(k - count, 0), 0, 0)),
            ],
            out_specs=[pl.BlockSpec(shape, out_block) for shape in shapes],
        ),
        out_shape=[
            jax.ShapeDtypeStruct((2 * count * n, columns), F32) for n, columns in shapes
        ],
        compiler_params=pltpu.CompilerParams(vmem_limit_bytes=32 * 2**20),
        cost_estimate=COST,
        name="laid_out",
    )(core.reshape(1).astype(jnp.int32), mine, theirs)


def matmul(left, right):
    return jnp.dot(left, right, preferred_element_type=F32)


def tall(left, right):
    return lax.dot_general(left, right, (((0,), (0,)), ((), ())), preferred_element_type=F32)


def wide(left, right):
    return lax.dot_general(left, right, (((1,), (1,)), ((), ())), preferred_element_type=F32)


def gelu_tanh(values):
    return jax.nn.gelu(values, approximate=True)


def whole(*shape):
    return pl.BlockSpec(shape, lambda *_: (0,) * len(shape))


def dot_wide(left, right):
    return lax.dot_general(left, right, (((1,), (1,)), ((), ())), preferred_element_type=F32)


def per_head(ref, first, count):
    return jnp.concatenate(
        [ref[first : first + count, k : k + LANES] for k in range(0, ref.shape[1], LANES)]
    )


def masked_scores(keys, queries, places, own, begin, step):
    scores = dot_wide(keys, queries)
    places = jnp.concatenate([places, places], axis=1)
    below = scores.shape[0] - step
    parts = []
    if below:
        parts.append(jnp.where(places[:below] >= begin, scores[:below], MASKED))
    near = (places[below:] >= begin) & (places[below:] <= own)
    parts.append(jnp.where(near, scores[below:], MASKED))
    return jnp.concatenate(parts) if below else parts[0]


def attend(q, kv, values_t, places, own, begin, scale, done=()):
    rows, width = q.shape
    groups = own.shape[0]
    part, step = rows // groups, kv.shape[0] // groups
    factor = scale * math.log2(math.e)

    def kernel(q_ref, kv_ref, vt_ref, place_ref, own_ref, begin_ref, *refs):
        out_ref, log_ref, top_ref = refs[len(done) :]
        for j in range(groups):
            n, row = step * (j + 1), slice(j, j + 1)
            scores = masked_scores(
                kv_ref[:n, :LANES],
                per_head(q_ref, part * j, part),
                place_ref[:n, :],
                own_ref[row, :],
                begin_ref[row, :],
                step,
            )
            top = jnp.max(scores, axis=0, keepdims=True)
            power = jnp.exp2((scores - top) * factor)
            total = jnp.sum(power, axis=0, keepdims=True)
            probs = (power * (1.0 / total)).astype(BF)
            out = jnp.dot(vt_ref[:, :n], probs, preferred_element_type=F32).T
            for k in range(width // LANES):
                out_ref[part * j : part * (j + 1), k * LANES : (k + 1) * LANES] = out[
                    part * k : part * (k + 1)
                ].astype(BF)
            log_ref[row, :] = top * factor + jnp.log2(total)
            top_ref[row, :] = top

    return pl.pallas_call(
        kernel,
        in_specs=[pl.BlockSpec(memory_space=pltpu.VMEM)] * 6
        + [pl.BlockSpec(memory_space=pl.ANY)] * len(done),
        out_shape=[
            jax.ShapeDtypeStruct((rows, width), BF),
            jax.ShapeDtypeStruct(own.shape, F32),
            jax.ShapeDtypeStruct(own.shape, F32),
        ],
        compiler_params=pltpu.CompilerParams(vmem_limit_bytes=48 * 2**20),
        cost_estimate=BRIEF,
        name="attend",
    )(q, kv, values_t, places, own, begin, *done)


def attend_back(q, grad, kv, keys_t, places, own, begin, logs, scale, done=()):
    rows, width = q.shape
    total = kv.shape[0]
    groups = own.shape[0]
    part, step = rows // groups, total // groups
    factor = scale * math.log2(math.e)

    def kernel(
        q_ref, g_ref, kv_ref, kt_ref, place_ref, own_ref, begin_ref, log_ref, *refs
    ):
        dq_ref, dkv_ref, acc_ref = refs[len(done) :]
        for j in reversed(range(groups)):
            n, row = step * (j + 1), slice(j, j + 1)
            queries = per_head(q_ref, part * j, part)
            grads = per_head(g_ref, part * j, part)
            scores = masked_scores(
                kv_ref[:n, :LANES],
                queries,
                place_ref[:n, :],
                own_ref[row, :],
                begin_ref[row, :],
                step,
            )
            prob = jnp.exp2(scores * factor - log_ref[row, :])
            dprob = dot_wide(kv_ref[:n, LANES:], grads)
            inner = jnp.sum(prob * dprob, axis=0, keepdims=True)
            dscores = (prob * (dprob - inner)).astype(BF)
            dq = jnp.dot(kt_ref[:, :n], dscores, preferred_element_type=F32).T * scale
            for k in range(width // LANES):
                dq_ref[part * j : part * (j + 1), k * LANES : (k + 1) * LANES] = dq[
                    part * k : part * (k + 1)
                ].astype(BF)
            dkeys = jnp.dot(dscores, queries, preferred_element_type=F32)
            dvalues = jnp.dot(prob.astype(BF), grads, preferred_element_type=F32)
            if j == groups - 1:
                acc_ref[:, :LANES] = dkeys
                acc_ref[:, LANES:] = dvalues
            else:
                acc_ref[:n, :LANES] += dkeys
                acc_ref[:n, LANES:] += dvalues
        dkv_ref[:, :LANES] = (acc_ref[:, :LANES] * scale).astype(BF)
        dkv_ref[:, LANES:] = acc_ref[:, LANES:].astype(BF)

    return pl.pallas_call(
        kernel,
        in_specs=[pl.BlockSpec(memory_space=pltpu.VMEM)] * 8
        + [pl.BlockSpec(memory_space=pl.ANY)] * len(done),
        out_shape=[
            jax.ShapeDtypeStruct((rows, width), BF),
            jax.ShapeDtypeStruct(kv.shape, BF),
        ],
        scratch_shapes=[pltpu.VMEM(kv.shape, F32)],
        compiler_params=pltpu.CompilerParams(vmem_limit_bytes=48 * 2**20),
        cost_estimate=COST,
        name="attend_back",
    )(q, grad, kv, keys_t, places, own, begin, logs, *done)


def feed_forward(h, dy, w_fc, b_fc, w_proj, done=()):
    tokens, width = h.shape
    units, part = w_fc.shape[1], 512
    curve = math.sqrt(2.0 / math.pi)

    def kernel(h_ref, dy_ref, fc_ref, b_ref, proj_ref, *refs):
        g_ref, du_ref, sum_ref, dh_ref, acc_ref = refs[len(done) :]
        step = pl.program_id(0)
        u = jnp.dot(h_ref[...], fc_ref[...], preferred_element_type=F32) + b_ref[...]
        dg = dot_wide(dy_ref[...], proj_ref[...])
        square = u * u
        bend = jnp.tanh(curve * u * (1.0 + 0.044715 * square))
        half = 0.5 + 0.5 * bend
        g_ref[...] = (u * half).astype(BF)
        slope = half + 0.5 * curve * u * (1.0 - bend * bend) * (1.0 + 3 * 0.044715 * square)
        du = (dg * slope).astype(BF)
        du_ref[...] = du
        sum_ref[...] = jnp.sum(du.astype(F32), axis=0, keepdims=True)
        term = dot_wide(du, fc_ref[...])

        @pl.when(step == 0)
        def _():
            acc_ref[...] = term

        @pl.when(step > 0)
        def _():
            acc_ref[...] += term

        @pl.when(step == units // part - 1)
        def _():
            dh_ref[...] = acc_ref[...].astype(BF)

    along = lambda k: (0, k)
    return pl.pallas_call(
        kernel,
        grid=(units // part,),
        in_specs=[
            whole(tokens, width),
            whole(tokens, width),
            pl.BlockSpec((width, part), along),
            pl.BlockSpec((1, part), along),
            pl.BlockSpec((part, width), lambda k: (k, 0)),
        ]
        + [pl.BlockSpec(memory_space=pl.ANY)] * len(done),
        out_specs=[
            pl.BlockSpec((tokens, part), along),
            pl.BlockSpec((tokens, part), along),
            pl.BlockSpec((1, part), along),
            whole(tokens, width),
        ],
        out_shape=[
            jax.ShapeDtypeStruct((tokens, units), BF),
            jax.ShapeDtypeStruct((tokens, units), BF),
            jax.ShapeDtypeStruct((1, units), F32),
            jax.ShapeDtypeStruct((tokens, width), BF),
        ],
        scratch_shapes=[pltpu.VMEM((tokens, width), F32)],
        compiler_params=pltpu.CompilerParams(vmem_limit_bytes=56 * 2**20),
        cost_estimate=COST,
        name="feed_forward",
    )(h, dy, w_fc, b_fc.reshape(1, units), w_proj, *done)


def products(pairs, at_left, at_right, extra=None, split=False):
    outs, per = len(at_left), len(at_left[0])
    tokens = pairs[0][0].shape[0]
    widths = [w for _, _, w in pairs]
    n, total = len(pairs), sum(widths)
    rows = per * LANES

    def kernel(at_ref, *refs):
        values, start = [], 0
        for i, width in enumerate(widths):
            own = refs[i * (per + 1) : (i + 1) * (per + 1)]
            left = jnp.concatenate([r[...] for r in own[:per]], axis=1)
            value = lax.dot_general(
                left, own[per][...], (((0,), (0,)), ((), ())), preferred_element_type=F32
            )
            if extra is not None:
                value = value + refs[n * (per + 1)][:, start : start + width].astype(F32)
            values.append(value.astype(BF))
            start += width

        def write(out):
            start = 0
            for value, width in zip(values, widths):
                out[:, start : start + width] = value
                start += width

        for k, out in enumerate(refs[n * (per + 1) + (extra is not None) :]):
            if split:
                pl.when(pl.program_id(0) == k)(functools.partial(write, out))
            else:
                write(out)

    def left_block(j):
        return lambda k, at: (0, at[k * per + j])

    def right_block(k, at):
        return (0, at[outs * per + k])

    specs, operands = [], []
    for left, right, width in pairs:
        specs += [pl.BlockSpec((tokens, LANES), left_block(j)) for j in range(per)]
        specs.append(pl.BlockSpec((tokens, width), right_block))
        operands += [left] * per + [right]
    if extra is not None:
        specs.append(pl.BlockSpec((rows, total), lambda k, at: (k, 0)))
        operands.append(extra)
    if split:
        out_specs = [whole(rows, total)] * outs
        out_shape = [jax.ShapeDtypeStruct((rows, total), BF)] * outs
    else:
        out_specs = [pl.BlockSpec((rows, total), lambda k, at: (k, 0))]
        out_shape = [jax.ShapeDtypeStruct((outs * rows, total), BF)]
    return pl.pallas_call(
        kernel,
        grid_spec=pltpu.PrefetchScalarGridSpec(
            num_scalar_prefetch=1, grid=(outs,), in_specs=specs, out_specs=out_specs
        ),
        out_shape=out_shape,
        compiler_params=pltpu.CompilerParams(vmem_limit_bytes=56 * 2**20),
        cost_estimate=COST,
        name="products",
    )(numbers([i for row in at_left for i in row] + list(at_right)), *operands)


def norm_parts(values):
    centered = values - jnp.mean(values, axis=-1, keepdims=True)
    rate = lax.rsqrt(jnp.mean(centered * centered, axis=-1, keepdims=True) + EPSILON)
    return centered * rate, rate


def norm_back(grad, gain, hat, rate):
    e = grad * gain
    inner = jnp.mean(e * hat, axis=-1, keepdims=True)
    return rate * (e - jnp.mean(e, axis=-1, keepdims=True) - hat * inner)


def shards(
    hidden,
    cotangent,
    lengths,
    source_pos,
    owner_slot,
    ln1_gain,
    ln1_bias,
    query_weight,
    query_bias,
    kv_weight,
    value_bias,
    out_weight,
    out_bias,
    ln2_gain,
    ln2_bias,
    fc_weight,
    fc_bias,
    proj_weight,
    proj_bias,
):
    rows, width = hidden.shape
    ny, nz, nctx = lax.axis_size(Y), lax.axis_size(Z), lax.axis_size(CONTEXT)
    y, xl, z, c = (lax.axis_index(a) for a in (Y, XL, Z, CORE))
    xo, co = 1 - xl, 1 - c
    ctx = lax.axis_index(CONTEXT)
    sub = rows // nctx
    head = kv_weight.shape[1] // 2
    heads = width // head
    scale = 1.0 / math.sqrt(head)
    shard = query_weight.shape[0]
    nzx = lax.axis_size(ZX)
    half = shard // 2
    ff = proj_weight.shape[0]
    block = 2 * ff

    small = jnp.concatenate(
        [
            jnp.stack([ln1_gain, ln1_bias, query_bias, out_bias, ln2_gain, ln2_bias, proj_bias]),
            jnp.pad(value_bias, (0, shard - value_bias.shape[0]))[None],
            fc_bias.reshape(-1, shard),
            jnp.zeros((4, shard), BF),
        ]
    )
    first = pack(
        [small, kv_weight],
        [out_weight, fc_weight],
        [lambda k: (c, z), lambda k: (c, k // 2 * nz + z)],
    )
    first = lax.all_to_all(first, FSDP, 0, 0, tiled=True)
    small = first[:, :16]
    gain1, bias1, bq, bo, gain2, bias2, bproj = (
        small[:, k].reshape(width).astype(F32) for k in range(7)
    )
    bv = small[:, 7, : value_bias.shape[0]].reshape(head).astype(F32)
    bfc = pick(small[:, 8:12].reshape(ny, block), y, 0).astype(F32)
    wkv = first[:, 16 : 16 + shard].reshape(width, 2 * head)

    q_mine = lax.all_to_all(
        repeat_block(query_weight, c, 2 * ny, (first,)), FSDP, 0, 0, tiled=True
    )

    def quarters(piece):
        return [piece] + [shift(piece, Z, d) for d in range(1, nz)]

    def whole_weight(mine, theirs, cost):
        there = [(z - d) % nz for d in range(nz)]
        return assemble_quarters(
            mine + theirs, [(c, k) for k in there] + [(co, k) for k in there], cost
        )

    at = 16 + shard
    o_mine = quarters(first[:, at : at + shard])

    x = hidden.astype(F32)
    hat1, rate1 = norm_parts(x)
    h1 = (hat1 * gain1 + bias1).astype(BF)
    kv = matmul(h1, wkv) + jnp.concatenate([jnp.zeros((head,), F32), bv])
    owned = lax.dynamic_slice_in_dim(owner_slot[0], ctx * rows, rows)
    target = owned // rows * sub + owned % rows - ctx * sub
    deal = (target[:, None] == jnp.arange(rows, dtype=jnp.int32)[None, :]).astype(BF)

    def dealt(array):
        pieces = array.astype(BF).reshape(nctx, sub, width)
        return lax.all_to_all(pieces, CONTEXT, 0, 0, tiled=True).reshape(rows, width)

    dealing = tall(deal, cotangent).astype(BF).reshape(nctx, -1, 2 * head)
    kv, q_mine, o_mine, dealing = gate((kv.astype(BF), q_mine, o_mine, dealing))
    q_theirs, o_theirs = swap(q_mine, CORE), [swap(m, CORE) for m in o_mine]
    kv = jnp.broadcast_to(kv[None], (nctx, rows, 2 * head))
    all_kv = lax.all_to_all(jnp.concatenate([kv, dealing], axis=1), CONTEXT, 0, 0, tiled=True)
    shards_at = [shard * k for k in range(2 * ny)]
    wq = assemble(
        [
            (q_mine, 0, [a + half * c for a in shards_at]),
            (q_theirs, 0, [a + half * co for a in shards_at]),
        ],
        width,
        width,
    )
    all_kv, wq, o_mine, o_theirs, proj_weight, first = gate(
        (all_kv, wq, o_mine, o_theirs, proj_weight, first)
    )
    dy = all_kv[:, rows:].reshape(rows, width)
    all_kv = all_kv[:, :rows]
    f_mine = quarters(first[:, at + shard :])
    p_mine = swap(lax.dynamic_slice_in_dim(proj_weight, ff // 2 * c, ff // 2), XL)
    wo = whole_weight(o_mine, o_theirs, BRIEF)
    q = (matmul(h1, wq) + bq).astype(BF)

    positions = source_pos[0]
    starts = jnp.cumsum(lengths[0]) - lengths[0]
    own_pos = lax.dynamic_slice_in_dim(positions, ctx * rows, rows)
    seq_start = jnp.max(jnp.where(starts[None, :] <= own_pos[:, None], starts[None, :], 0), axis=1)
    groups = rows // 16
    natural = jnp.moveaxis(all_kv.reshape(nctx, nctx, sub, 2 * head), 0, 1)
    natural = natural.reshape(nctx * rows, 2 * head)
    xh = lax.axis_index(XH)
    places = jnp.moveaxis(positions.reshape(nctx, nctx, sub), 0, 1).reshape(nctx * rows, 1)
    places = jnp.broadcast_to(places, (nctx * rows, LANES))

    def for_heads(array):
        array = jnp.broadcast_to(array.reshape(groups, 1, 16), (groups, heads, 16))
        return array.reshape(groups, heads * 16)

    own, begin = for_heads(own_pos), for_heads(seq_start)
    attended, logs, tops = attend(
        q, natural, natural[:, head:].T, places, own, begin, scale
    )
    local_max = jnp.max(tops.reshape(groups, heads, 16), axis=(0, 2)) * scale

    def pieces_of(array):
        return [array] + [shift(array, Y, d) for d in range(1, ny)]

    dy_pieces = pieces_of(dy)
    attended, wo, f_mine, dy_pieces, p_mine = gate((attended, wo, f_mine, dy_pieces, p_mine))
    x2 = x + matmul(attended, wo) + bo
    hat2, rate2 = norm_parts(x2)
    h2 = (hat2 * gain2 + bias2).astype(BF)

    def over_y(array):
        return jnp.concatenate(pieces_of(array))

    h2, f_mine, p_mine = gate((h2, f_mine, p_mine))
    dy_all = jnp.concatenate(dy_pieces)
    h2_pieces = pieces_of(h2)
    wfc = whole_weight(f_mine, [swap(m, CORE) for m in f_mine], COST)
    p_theirs = swap(p_mine, CORE)
    wproj = assemble(
        [
            (proj_weight, 0, [ff * xl + LANES * k for k in range(ff // LANES)]),
            (p_mine, 0, [ff * xo + ff // 2 * c + LANES * k for k in range(ff // 2 // LANES)]),
            (p_theirs, 0, [ff * xo + ff // 2 * co + LANES * k for k in range(ff // 2 // LANES)]),
        ],
        block,
        width,
    )
    h2_pieces, wfc, wproj = gate((h2_pieces, wfc, wproj))
    h2_all = jnp.concatenate(h2_pieces)
    g, du, du_sum, dh2 = feed_forward(h2_all, dy_all, wfc, bfc, wproj)

    x_ring = [(a, b) for a in (0, 1) for b in (0, 1)]
    zs = [(z + d) % nz for d in range(nz)]
    part_z = half // nz

    def flip(array, a, b):
        moves = [(2 * i + j, 2 * (i ^ a) + (j ^ b)) for i in (0, 1) for j in (0, 1)]
        return lax.ppermute(array, (XL, XH), moves)

    def over_x(parts):
        return [parts[0]] + [flip(p, a, b) for p, (a, b) in zip(parts[1:], x_ring[1:])]

    def over_z(parts):
        return [parts[0]] + [shift(parts[d], Z, d) for d in range(1, nz)]

    def core_summed(pairs, left_at, right_at):
        (theirs,) = products(pairs, left_at(co), right_at)
        return products(pairs, left_at(c), right_at, swap(theirs, CORE), True)

    dproj = core_summed(
        [(g, dy_all, width)],
        lambda core: [[(k * 2 + core) * nz + there for k in (0, 1)] for there in zs],
        [0] * nz,
    )
    dh2 = dh2.reshape(ny, rows, width)
    dh2 = [dh2[0]] + [shift(dh2[d], Y, -d) for d in range(1, ny)]
    dh2, dproj, attended, h1 = gate((dh2, dproj, attended, h1))
    dproj = over_z(dproj)
    sent = side_by_side([], [attended, h1], [(y + d) % ny for d in range(ny)])
    sent = [sent[0]] + [shift(sent[d], Y, d) for d in range(1, ny)]
    dh2 = functools.reduce(jnp.add, [t.astype(F32) for t in dh2])

    dy_f = dy.astype(F32)
    dx2 = dy_f + norm_back(dh2, gain2, hat2, rate2)
    da = dx2.astype(BF)

    dattended = wide(da, wo).astype(BF)
    dq, dkv = attend_back(
        q, dattended, natural, natural[:, :head].T, places, own, begin, logs, scale
    )
    dfc = core_summed(
        [(h2_all, du, block // 2)],
        lambda core: [[(k * 2 + (xl ^ a)) * 2 + core for k in range(ny)] for a, _ in x_ring],
        [xh ^ b for _, b in x_ring],
    )
    dq, dkv, da, dproj, dfc, g, sent = gate((dq, dkv, da, dproj, dfc, g, sent))
    dfc = over_x(dfc)
    sent = jnp.concatenate(sent)
    attended_columns, h1_columns = sent[:, : block // ny], sent[:, block // ny :]
    dkv = jnp.moveaxis(dkv.reshape(nctx, nz, 2, 2, sub, 2 * head), 0, 3)
    dkv = dkv.reshape(nz, 2, 2, rows, 2 * head)

    def plus(mine, *got):
        return functools.reduce(jnp.add, [t.astype(F32) for t in (mine, *got)]).astype(BF)

    dkv = plus(pick(dkv, c, 2), swap(pick(dkv, co, 2), CORE))
    dkv = plus(pick(dkv, xh, 1), swap(pick(dkv, 1 - xh, 1), XH))
    dkv = plus(pick(dkv, z, 0), *[shift(pick(dkv, k, 0), Z, d) for d, k in list(enumerate(zs))[1:]])
    da_dq = over_y(jnp.concatenate([da, dq], axis=1))
    result_terms = matmul(g, wproj).astype(BF)

    dproj, dfc, da_dq, dkv, result_terms, dq = gate(
        (dproj, dfc, da_dq, dkv, result_terms, dq)
    )
    dh1 = wide(dq, wq)
    dproj = add_cut(
        dproj,
        (2, 2, half // 2, width),
        (1, 1, half // 2, width),
        [(xl ^ a, xh ^ b, 0, 0) for a, b in x_ring],
    )
    dproj = over_x(dproj)
    dfc = add_cut(
        dfc,
        (ny, nz, part_z, block // 2),
        (ny, 1, part_z, block // 2),
        [(0, there, 0, 0) for there in zs],
    )
    dfc = over_z(dfc)
    dkv_all = over_y(dkv)
    part_fc = half // nzx

    def spread(terms):
        terms = terms.reshape(2 * nzx, part_fc, -1)
        return lax.all_to_all(terms, (XL,) + ZX, 0, 0, tiled=True)

    da_all, dq_all = da_dq[:, :width], da_dq[:, width:]
    (theirs,) = products([(attended_columns, da_all, width)], [[co, 2 + co]], [0])
    (dwo,) = products(
        [(attended_columns, da_all, width)], [[c, 2 + c]], [0], swap(theirs, CORE)
    )
    dwo = spread(dwo)
    result = result_terms.reshape(ny, rows, width)
    result = [result[0]] + [shift(result[d], Y, -d) for d in range(1, ny)]
    dproj, dfc, dkv_all, result, dh1, dwo = gate((dproj, dfc, dkv_all, result, dh1, dwo))
    dproj = add_cut(
        dproj,
        (half // 2, width),
        (half // 2, width // 2),
        [(0, 0), (0, 1)],
    )
    dproj = jnp.concatenate(dproj)
    dproj_other = swap(dproj, XH)
    dfc = add_cut(
        dfc,
        (ny, part_z, block // 2),
        (1, part_z, block // 2),
        [((y + d) % ny, 0, 0) for d in range(ny)],
    )
    dfc = [dfc[0]] + [shift(dfc[d], Y, d) for d in range(1, ny)]
    dfc, dproj, dproj_other = gate((dfc, dproj, dproj_other))
    dfc = jnp.stack(dfc)

    dfc = jnp.concatenate([pick(dfc, (y - k) % ny, 0)[0] for k in range(ny)])
    there = [(z - d) % nz for d in range(nz)]
    dfc = [dfc] + [shift(dfc, Z, d) for d in range(1, nz)]
    pairs = [(h1_columns, dq_all, width), (h1_columns, dkv_all, 2 * head)]
    (theirs,) = products(pairs, [[co, 2 + co]], [0])
    (dwq,) = products(pairs, [[c, 2 + c]], [0], swap(theirs, CORE))
    dh1 = dh1 + wide(dkv, wkv)
    grad_hidden = (dx2 + norm_back(dh1, gain1, hat1, rate1)).astype(BF)
    result = functools.reduce(jnp.add, [t.astype(F32) for t in result])
    result = dealt((x2 + result + bproj).astype(BF))
    def total(array):
        return jnp.sum(array.astype(F32), axis=0)

    vectors = [
        total(dy),
        total(dh2 * hat2),
        total(dh2),
        total(da),
        total(dq),
        total(dh1 * hat1),
        total(dh1),
    ]
    vectors = [v.reshape(2 * ny, 1, shard) for v in vectors]
    du_sum = du_sum.reshape(1, 2, ff // shard, shard)
    du_sum = lax.dynamic_update_slice(
        jnp.zeros((ny, 2, ff // shard, shard), F32), du_sum, (y, 0, 0, 0)
    )
    bv_sum = total(dkv[:, head:]).reshape(2 * ny, 1, -1)
    top_high = lax.reduce_precision(local_max, 8, 7)
    tops = jnp.concatenate([top_high, local_max - top_high])
    tops = jnp.broadcast_to(tops, (2 * ny, 1, 2 * heads))
    last = [jnp.pad(v, ((0, 0), (0, 0), (0, shard - v.shape[2]))) for v in (bv_sum, tops)]
    vectors += [du_sum.reshape(2 * ny, -1, shard), *last]
    joined = jnp.concatenate(vectors, axis=1).astype(BF)
    joined = jnp.pad(joined, ((0, 0), (0, 16 - joined.shape[1]), (0, 0)))
    joined = jnp.broadcast_to(joined[:, None], (2 * ny, nctx, *joined.shape[1:]))
    joined = joined.reshape(-1, 16, shard)
    joined = lax.all_to_all(joined, EVERY, 0, 0, tiled=True)
    dfc, dwq, dwo, dproj, dproj_other, result, joined = gate(
        (dfc, dwq, dwo, dproj, dproj_other, result, joined)
    )
    output = matmul(deal, result).astype(BF)

    dfc = jnp.stack(dfc)
    dfc_other = swap(dfc, XH)
    dproj = pair(dproj, dproj_other, xh)
    dproj = [dproj] + [shift(dproj, Z, d) for d in range(1, nz)]
    small_w = jnp.concatenate([dwo, spread(dwq)], axis=2)
    dfc, dfc_other, dproj, small_w = gate((dfc, dfc_other, dproj, small_w))
    small_w = copies(jnp.sum(small_w.astype(F32), axis=0).astype(BF), ZX)
    dfc = pair(dfc, dfc_other, xh)
    mine = [dfc] + dproj
    mine = mine + [swap(m, CORE) for m in mine]
    grad_proj_w, grad_fc_w = lay_both(
        mine,
        [c * nz + k for k in there] + [co * nz + k for k in there],
        half,
        part_z,
        ny,
    )
    small_w, grad_proj_w, grad_fc_w = gate((small_w, grad_proj_w, grad_fc_w))
    grad_out_w, grad_query_w, grad_kv_w = laid_out(
        small_w,
        swap(small_w, CORE),
        c,
        [(part_fc, width), (part_fc, width), (part_fc, 2 * head)],
        lambda piece: (piece[:, :width], piece[:, width : 2 * width], piece[:, 2 * width :]),
    )

    tops = joined[:, 12].astype(F32)
    maxima = jnp.max(tops[:, :heads] + tops[:, heads : 2 * heads], axis=0)
    joined = jnp.sum(joined.astype(F32), axis=0)
    g_bproj, g_gain2, g_bias2, g_bo, g_bq, g_gain1, g_bias1 = (joined[k] for k in range(7))
    g_bfc, g_bv = joined[7:11].reshape(ff), joined[11, : value_bias.shape[0]]

    clip_ratio = CLIP_LIMIT / jnp.maximum(maxima, CLIP_LIMIT)
    column_scale = jnp.repeat(jnp.sqrt(clip_ratio), head)
    clipped_qw = query_weight.astype(F32) * column_scale[None, :]
    clipped_qb = query_bias.astype(F32) * lax.dynamic_slice_in_dim(
        column_scale, lax.axis_index(FSDP) * shard, shard
    )
    clipped_kw = kv_weight[:, :head].astype(F32) * jnp.sqrt(jnp.min(clip_ratio))
    return (
        output,
        grad_hidden,
        g_gain1,
        g_bias1,
        grad_query_w,
        g_bq,
        grad_kv_w,
        g_bv,
        grad_out_w,
        g_bo,
        g_gain2,
        g_bias2,
        grad_fc_w,
        g_bfc,
        grad_proj_w,
        g_bproj,
        maxima,
        clipped_qw,
        clipped_qb,
        clipped_kw,
    )


def solution(mesh):
    torus = Mesh(mesh.devices.reshape(4, 2, 4, 2, 2), EVERY)
    tokens, table, vector, matrix = P(EVERY, None), P(FSDP, None), P(FSDP), P(FSDP, None)
    return jax.shard_map(
        shards,
        mesh=torus,
        in_specs=(
            tokens,
            tokens,
            table,
            table,
            table,
            vector,
            vector,
            matrix,
            vector,
            matrix,
            vector,
            matrix,
            vector,
            vector,
            vector,
            matrix,
            vector,
            matrix,
            vector,
        ),
        out_specs=(
            tokens,
            tokens,
            vector,
            vector,
            matrix,
            vector,
            matrix,
            vector,
            matrix,
            vector,
            vector,
            vector,
            matrix,
            vector,
            matrix,
            vector,
            P(),
            matrix,
            vector,
            matrix,
        ),
        check_vma=False,
    )
```

time: 811 us -> 689 us (0.85)
  Pallas kernels: 24.6 us -> 158 us
  matrix products: 121 us -> 38.2 us
  other arithmetic: 121 us -> 42.4 us
  starting transfers between devices: 185 us -> 124 us
  local copies, waits for them, and re-layouts: 127 us -> 82.2 us
  blocking collectives: 0 us -> 44.3 us
  waiting for transfers between devices: 217 us -> 186 us
    pallas_call x0 -> x22, Pallas kernels: none -> 143 us  [the longest x8 50.7 us: products(): pl.pallas_call(kernel, grid_spec=pltpu.PrefetchScalarGridSpec(num_scalar_...]
    ppermute x71 -> x70, waiting for transfers between devices: 170 us -> 125 us  [shift(): return lax.ppermute(array, axis, [(i, (i + by) % n) for i in range(n)])]
    all_to_all x0 -> x1, blocking collectives: none -> 44.3 us  [shards(): first = lax.all_to_all(first, FSDP, 0, 0, tiled=True)]
    dot_general x6 -> x0, matrix products: 41.5 us -> none  [the longest x1 11.9 us: shards(): jnp.einsum('rhd,kd->rhk', dattended, values, preferred_element_type=F32)]
    all_to_all x7 -> x1, starting transfers between devices: 44.9 us -> 5.58 us  [copies(): lax.all_to_all(jnp.broadcast_to(array[None], (n, *array.shape)), axis, 0,...]
    ppermute x0 -> x6, waiting for transfers between devices: none -> 29 us  [flip(): return lax.ppermute(array, (XL, XH), moves)]
    dot_general x5 -> x1, matrix products: 26.8 us -> 0.41 us  [tall(): lax.dot_general(left, right, (((0,), (0,)), ((), ())), preferred_element_...]
    convert_element_type x9 -> x0, local copies, waits for them, and re-layouts: 23.8 us -> none  [the longest x4 10.4 us: both_halves(): theirs = swap(pick(array, co, 1).astype(BF), CORE)]
  transfers between devices with their start and end apart: 85 -> 83, of which waited for: 25 -> 26; matrix products, arithmetic and copies ran while one was open for 37% -> 17% of each run, Pallas kernels for 3% -> 17%
where the time goes in v2:
time: 689 us; the launch traced here: 679 us
  waiting for transfers between devices  186 us (27%)
  Pallas kernels  158 us (23%)
  starting transfers between devices  124 us (18%)
  local copies, waits for them, and re-layouts  82.2 us (12%)
  blocking collectives  44.3 us (6%)
  other arithmetic  42.4 us (6%)
  matrix products  38.2 us (6%)
    ppermute x70, waiting for transfers between devices, shift(): return lax.ppermute(array, axis, [(i, (i + by) % n) for i in range(n)])  125 us
    ppermute x70, starting transfers between devices, shift(): return lax.ppermute(array, axis, [(i, (i + by) % n) for i in range(n)])  80 us
    pallas_call x8, Pallas kernels, products(): pl.pallas_call(kernel, grid_spec=pltpu.PrefetchScalarGridSpec(num_scalar_...  50.7 us
    all_to_all x1, blocking collectives, shards(): first = lax.all_to_all(first, FSDP, 0, 0, tiled=True)  44.3 us
    unnamed x206, local copies, waits for them, and re-layouts  34.3 us
    ppermute x6, waiting for transfers between devices, flip(): return lax.ppermute(array, (XL, XH), moves)  29 us
    pallas_call x2, Pallas kernels, assemble_quarters(): pl.pallas_call(kernel, grid_spec=pltpu.PrefetchScalarGridSpec(num_scalar_...  27.1 us
    dot_general x5, matrix products, matmul(): return jnp.dot(left, right, preferred_element_type=F32)  21.4 us
  transfers between devices with their start and end apart: 83, of which 26 were waited for; matrix products, arithmetic and copies ran while one was open for 17% of the time, Pallas kernels for 17%

profile of v2, /device:TPU:1, one launch (start us, length us, event | category | flops | bytes accessed | tf_op | source)
XLA Modules:
  0.0 678.5 jit_solution(1804945095607398118)
XLA Ops:
  12.3 44.3 %all_to_all.40.refs_0_ = bf16[8,784,256]{2,1,0:T(8,128)(2,1)S(1)} all-to-all(bf16[8,784,256]{2,1,0:T(8,128)(2,1)S(1)} %pack.1), channel_id=1, replica_groups=mesh['fsdp_0'=4,'fsdp_1'=2,'context_0'=4,'context_1'=2,'context_2'=2] {'..., dimensions={0} | all-to-all | bytes 6422528 | tf_op jit(solution)/shard_map/all_to_all | solution.py:697
  81.2 15.1 %collective-permute-done.refs_1_ = bf16[8,256,256]{2,1,0:T(8,128)(2,1)S(1)} collective-permute-done((bf16[8,256,256]{2,1,0:T(8,128)(2,1)S(1)}, bf16[8,256,256]{2,1,0:T(8,128)(2,1)S(1)}, u32[]{:S(2)}, u32[]{:S(2)}) %collective-permute-start) | collective-permute-done | bytes 1048608 | tf_op jit(solution)/shard_map/ppermute | solution.py:30
  96.3 23.4 %collective-permute-done.1.refs_2_ = bf16[8,256,256]{2,1,0:T(8,128)(2,1)} collective-permute-done((bf16[8,256,256]{2,1,0:T(8,128)(2,1)S(1)}, bf16[8,256,256]{2,1,0:T(8,128)(2,1)}, u32[]{:S(2)}, u32[]{:S(2)}) %collective-permute-start.1) | collective-permute-done | bytes 1048608 | tf_op jit(solution)/shard_map/ppermute | solution.py:30
  130.8 9.9 %assemble.2 = bf16[2048,2048]{1,0:T(8,128)(2,1)S(1)} custom-call(s32[18]{0:T(128)S(1)} %stack.583.at_ref, bf16[1024,2048]{1,0:T(8,128)(2,1)} %bitcast.33.refs_0_, bf16[1024,2048]{1,0:T(8,128)(2,1)} %bitcast.34.refs_1_), custom_call_target="tpu_custom_call" | custom-call | flops 30000001024 | bytes 1024 | tf_op jit(solution)/shard_map/assemble/pallas_call | solution.py:224
  177.7 8.0 %collective-permute-done.12 = bf16[128,2048]{1,0:T(8,128)(2,1)} collective-permute-done((bf16[128,2048]{1,0:T(8,128)(2,1)}, bf16[128,2048]{1,0:T(8,128)(2,1)}, u32[]{:S(2)}, u32[]{:S(2)}) %collective-permute-start.12) | collective-permute-done | bytes 524320 | tf_op jit(solution)/shard_map/ppermute | solution.py:30
  192.5 7.5 %attend.1 = (bf16[128,2048]{1,0:T(8,128)(2,1)S(1)}, f32[8,256]{1,0:T(8,128)S(1)}, f32[8,256]{1,0:T(8,128)S(1)}) custom-call(bf16[128,2048]{1,0:T(8,128)(2,1)S(1)} %fusion.1.q_ref, bf16[2048,256]{1,0:T(8,128)(2,1)S(1)} %bitcast.233, bf16[128,2048]{1,0:T(8,128)(2,1)S(1)} %bitcast.235, s32[2048,128]{1,0:T(8,128)S(1)} %broadcast_in_dim.40.place_ref, ...), custom_call_target="tpu_custom_call" | custom-call | bytes 1024 | tf_op jit(solution)/shard_map/attend/pallas_call | solution.py:436
  201.0 13.1 %assemble_quarters.2 = bf16[8,2,128,2048]{3,2,1,0:T(8,128)(2,1)} custom-call(s32[32]{0:T(128)S(1)} %stack.593.at_ref, bf16[8,256,256]{2,1,0:T(8,128)(2,1)S(1)} %get-tuple-element.191.refs_0_, bf16[8,256,256]{2,1,0:T(8,128)(2,1)S(1)} %copy-done.14, bf16[8,256,256]{2,1,0:T(8,128)(2,1)} %collective-permute-done.1.refs_2_, ...), custom_call_target="tpu_custom_call" | custom-call | bytes 1024 | tf_op jit(solution)/shard_map/assemble_quarters/pallas_call | solution.py:156
  236.9 14.0 %assemble_quarters.3 = bf16[8,2,128,2048]{3,2,1,0:T(8,128)(2,1)} custom-call(s32[32]{0:T(128)S(1)} %stack.593.at_ref, bf16[8,256,256]{2,1,0:T(8,128)(2,1)} %slice.153.refs_0_, bf16[8,256,256]{2,1,0:T(8,128)(2,1)} %collective-permute-done.8.refs_1_, bf16[8,256,256]{2,1,0:T(8,128)(2,1)} %collective-permute-done.9.refs_2_, ...), custom_call_target="tpu_custom_call" | custom-call | flops 30000001024 | bytes 1024 | tf_op jit(solution)/shard_map/assemble_quarters/pallas_call | solution.py:156
  262.2 21.2 %feed_forward.1 = (bf16[512,2048]{1,0:T(8,128)(2,1)}, bf16[512,2048]{1,0:T(8,128)(2,1)}, f32[1,2048]{1,0:T(1,128)}, bf16[512,2048]{1,0:T(8,128)(2,1)}) custom-call(bf16[512,2048]{1,0:T(8,128)(2,1)} %copy-done.68, bf16[512,2048]{1,0:T(8,128)(2,1)} %get-tuple-element.402.dy_ref.refs_2_, bf16[2048,2048]{1,0:T(8,128)(2,1)} %bitcast.294, ...), custom_call_target="tpu_custom_call" | custom-call | flops 30000001024 | bytes 1024 | tf_op jit(solution)/shard_map/feed_forward/pallas_call | solution.py:542
  283.5 7.2 %products.8 = bf16[1024,2048]{1,0:T(8,128)(2,1)} custom-call(s32[12]{0:T(128)} %stack.628.at_ref, bf16[512,2048]{1,0:T(8,128)(2,1)} %get-tuple-element.263.refs_0_.refs_1_, bf16[512,2048]{1,0:T(8,128)(2,1)} %get-tuple-element.263.refs_0_.refs_1_, bf16[512,2048]{1,0:T(8,128)(2,1)} %get-tuple-element.402.dy_ref.refs_2_), custom_call_target="tpu_custom_call" | custom-call | flops 30000001024 | bytes 1024 | tf_op jit(solution)/shard_map/products/pallas_call | solution.py:624
  302.9 7.8 %products.10 = bf16[2048,1024]{1,0:T(8,128)(2,1)} custom-call(s32[20]{0:T(128)} %stack.646.at_ref, bf16[512,2048]{1,0:T(8,128)(2,1)} %copy-done.68, bf16[512,2048]{1,0:T(8,128)(2,1)} %copy-done.68, bf16[512,2048]{1,0:T(8,128)(2,1)} %copy-done.68, bf16[512,2048]{1,0:T(8,128)(2,1)} %copy-done.68, bf16[512,2048]{1,0:T(8,128)(2,1)} %get-tuple-element.241.refs_4_), custom_call_target="tpu_custom_call" | custom-call | flops 30000001024 | bytes 1024 | tf_op jit(solution)/shard_map/products/pallas_call | solution.py:624
  313.4 8.8 %products.9 = (bf16[256,2048]{1,0:T(8,128)(2,1)}, bf16[256,2048]{1,0:T(8,128)(2,1)}, bf16[256,2048]{1,0:T(8,128)(2,1)}, bf16[256,2048]{1,0:T(8,128)(2,1)}) custom-call(s32[12]{0:T(128)} %stack.619.at_ref, bf16[512,2048]{1,0:T(8,128)(2,1)} %get-tuple-element.263.refs_0_.refs_1_, bf16[512,2048]{1,0:T(8,128)(2,1)} %get-tuple-element.263.refs_0_.refs_1_, ...), custom_call_target="tpu_custom_call" | custom-call | flops 30000001024 | bytes 1024 | tf_op jit(solution)/shard_map/products/pallas_call | solution.py:624
  344.2 8.5 %attend_back.1 = (bf16[128,2048]{1,0:T(8,128)(2,1)S(1)}, bf16[2048,256]{1,0:T(8,128)(2,1)S(1)}) custom-call(bf16[128,2048]{1,0:T(8,128)(2,1)S(1)} %copy-done.8, bf16[128,2048]{1,0:T(8,128)(2,1)S(1)} %convolution_convert_fusion.1.g_ref, bf16[2048,256]{1,0:T(8,128)(2,1)S(1)} %bitcast.234, bf16[128,2048]{1,0:T(8,128)(2,1)S(1)} %bitcast.237, ...), custom_call_target="tpu_custom_call" | custom-call | flops 30000001024 | bytes 1024 | tf_op jit(solution)/shard_map/attend_back/pallas_call | solution.py:494
  355.7 9.0 %products.11 = (bf16[512,1024]{1,0:T(8,128)(2,1)}, bf16[512,1024]{1,0:T(8,128)(2,1)}, bf16[512,1024]{1,0:T(8,128)(2,1)}, bf16[512,1024]{1,0:T(8,128)(2,1)}) custom-call(s32[20]{0:T(128)} %stack.637.at_ref, bf16[512,2048]{1,0:T(8,128)(2,1)} %copy-done.68, bf16[512,2048]{1,0:T(8,128)(2,1)} %copy-done.68, bf16[512,2048]{1,0:T(8,128)(2,1)} %copy-done.68, ...), custom_call_target="tpu_custom_call" | custom-call | flops 30000001024 | bytes 1024 | tf_op jit(solution)/shard_map/products/pallas_call | solution.py:624
  367.3 11.0 %collective-permute-done.28 = bf16[256,2048]{1,0:T(8,128)(2,1)S(1)} collective-permute-done((bf16[256,2048]{1,0:T(8,128)(2,1)}, bf16[256,2048]{1,0:T(8,128)(2,1)S(1)}, u32[]{:S(2)}, u32[]{:S(2)}) %collective-permute-start.28) | collective-permute-done | bytes 1048608 | tf_op jit(solution)/shard_map/ppermute | solution.py:30
  390.6 9.1 %convolution_convert_fusion = bf16[512,2048]{1,0:T(8,128)(2,1)} fusion(bf16[512,2048]{1,0:T(8,128)(2,1)S(1)} %copy-done.94, bf16[2048,2048]{1,0:T(8,128)(2,1)} %copy-done.35), kind=kOutput, calls=%fused_computation.1 | convolution fusion | flops 4296015872 | bytes 12582912 | tf_op jit(solution)/shard_map/dot_general | solution.py:365
  414.9 19.7 %collective-permute-done.37 = bf16[128,4096]{1,0:T(8,128)(2,1)} collective-permute-done((bf16[128,4096]{1,0:T(8,128)(2,1)S(1)}, bf16[128,4096]{1,0:T(8,128)(2,1)}, u32[]{:S(2)}, u32[]{:S(2)}) %collective-permute-start.37) | collective-permute-done | bytes 1048608 | tf_op jit(solution)/shard_map/ppermute | solution.py:30
  436.7 18.5 %collective-permute-done.35 = bf16[512,1024]{1,0:T(8,128)(2,1)S(1)} collective-permute-done((bf16[512,1024]{1,0:T(8,128)(2,1)}, bf16[512,1024]{1,0:T(8,128)(2,1)S(1)}, u32[]{:S(2)}, u32[]{:S(2)}) %collective-permute-start.35) | collective-permute-done | bytes 1048608 | tf_op jit(solution)/shard_map/ppermute | solution.py:815
  495.4 7.2 %fusion.44 = f32[128,2048]{1,0:T(8,128)} fusion(bf16[128,2048]{1,0:T(8,128)(2,1)S(1)} %get-tuple-element.282, bf16[2048,2048]{1,0:T(8,128)(2,1)} %copy-done.2), kind=kOutput, calls=%fused_computation.150 | convolution fusion | flops 1073741824 | bytes 9961472 | tf_op jit(solution)/shard_map/dot_general | solution.py:373
  569.8 14.4 %all-to-all-done.5 = bf16[128,16,256]{2,1,0:T(8,128)(2,1)S(1)} async-done(((bf16[128,16,256]{2,1,0:T(8,128)(2,1)}), bf16[128,16,256]{2,1,0:T(8,128)(2,1)S(1)}, u32[]{:S(2)}, u32[]{:S(2)}) %all-to-all-start.5) | async-done | bytes 1048608 | tf_op jit(solution)/shard_map/all_to_all | solution.py:958
  607.1 9.2 %collective-permute-done.67.refs_2_ = bf16[2,128,1024]{2,1,0:T(8,128)(2,1)} collective-permute-done((bf16[2,128,1024]{2,1,0:T(8,128)(2,1)}, bf16[2,128,1024]{2,1,0:T(8,128)(2,1)}, u32[]{:S(2)}, u32[]{:S(2)}) %collective-permute-start.67) | collective-permute-done | bytes 524320 | tf_op jit(solution)/shard_map/ppermute | solution.py:30
  616.3 11.7 %collective-permute-done.68.refs_3_ = bf16[2,128,1024]{2,1,0:T(8,128)(2,1)} collective-permute-done((bf16[2,128,1024]{2,1,0:T(8,128)(2,1)}, bf16[2,128,1024]{2,1,0:T(8,128)(2,1)}, u32[]{:S(2)}, u32[]{:S(2)}) %collective-permute-start.68) | collective-permute-done | bytes 524320 | tf_op jit(solution)/shard_map/ppermute | solution.py:30
  645.0 11.2 %lay_both.1 = (f32[1024,2048]{1,0:T(8,128)}, f32[256,8192]{1,0:T(8,128)}) custom-call(s32[8]{0:T(128)} %stack.677.at_ref, bf16[2,4,128,1024]{3,2,1,0:T(8,128)(2,1)} %maximum_select_fusion.refs_0_, bf16[2,128,1024]{2,1,0:T(8,128)(2,1)} %maximum_select_fusion.1.refs_1_, bf16[2,128,1024]{2,1,0:T(8,128)(2,1)} %collective-permute-done.67.refs_2_, ...), custom_call_target="tpu_custom_call" | custom-call | flops 30000001024 | bytes 1024 | tf_op jit(solution)/shard_map/lay_both/pallas_call | solution.py:278
  669.2 8.9 %laid_out.1 = (f32[256,2048]{1,0:T(8,128)}, f32[256,2048]{1,0:T(8,128)}, f32[256,256]{1,0:T(8,128)}) custom-call(s32[1]{0:T(128)} %bitcast.9.at_ref.core_ref, bf16[8,16,4352]{2,1,0:T(8,128)(2,1)S(1)} %all-to-all-done.7.mine_ref, bf16[8,16,4352]{2,1,0:T(8,128)(2,1)} %collective-permute-done.75.theirs_ref), custom_call_target="tpu_custom_call" | custom-call | flops 30000001024 | bytes 1024 | tf_op jit(solution)/shard_map/laid_out/pallas_call | solution.py:344
  (527 shorter events, 356.3 us)
Async XLA Ops:
  60.8 59.4 %all-to-all-start.1 = ((bf16[8,128,2048]{2,1,0:T(8,128)(2,1)}), bf16[8,128,2048]{2,1,0:T(8,128)(2,1)}, u32[]{:S(2)}, u32[]{:S(2)}) async-start(bf16[8,128,2048]{2,1,0:T(8,128)(2,1)} %copy-done.6), calls=%async_computation.1 | async-start | bytes 8388608 | tf_op jit(solution)/shard_map/all_to_all | solution.py:706
  72.5 47.2 %collective-permute-start.1 = (bf16[8,256,256]{2,1,0:T(8,128)(2,1)S(1)}, bf16[8,256,256]{2,1,0:T(8,128)(2,1)}, u32[]{:S(2)}, u32[]{:S(2)}) collective-permute-start(bf16[8,256,256]{2,1,0:T(8,128)(2,1)S(1)} %get-tuple-element.191.refs_0_), channel_id=1, source_target_pairs={{0,8},{4,12},{8,0},{12,4},{1,9},{5,13},{9,1},{13,5},{2,10},{6,14},... | collective-permute-start | bytes 3145736 | tf_op jit(solution)/shard_map/ppermute | solution.py:30
  75.8 44.5 %collective-permute-start.2 = (bf16[8,256,256]{2,1,0:T(8,128)(2,1)S(1)}, bf16[8,256,256]{2,1,0:T(8,128)(2,1)}, u32[]{:S(2)}, u32[]{:S(2)}) collective-permute-start(bf16[8,256,256]{2,1,0:T(8,128)(2,1)S(1)} %get-tuple-element.191.refs_0_), channel_id=1, source_target_pairs={{0,12},{4,0},{8,4},{12,8},{1,13},{5,1},{9,5},{13,9},{2,14},{6,2},{... | collective-permute-start | bytes 3145736 | tf_op jit(solution)/shard_map/ppermute | solution.py:30
  155.9 58.4 %collective-permute-start.14 = (bf16[512,2048]{1,0:T(8,128)(2,1)}, bf16[512,2048]{1,0:T(8,128)(2,1)}, u32[]{:S(2)}, u32[]{:S(2)}) collective-permute-start(bf16[512,2048]{1,0:T(8,128)(2,1)} %constant_dynamic-slice_fusion), channel_id=1, source_target_pairs={{0,16},{16,0},{1,17},{17,1},{2,18},{18,2},{3,19},{19,3},{4,20},{20... | collective-permute-start | bytes 6291464 | tf_op jit(solution)/shard_map/ppermute | solution.py:30
  164.5 49.7 %collective-permute-start.8 = (bf16[8,256,256]{2,1,0:T(8,128)(2,1)}, bf16[8,256,256]{2,1,0:T(8,128)(2,1)}, u32[]{:S(2)}, u32[]{:S(2)}) collective-permute-start(bf16[8,256,256]{2,1,0:T(8,128)(2,1)} %slice.153.refs_0_), channel_id=1, source_target_pairs={{0,4},{4,8},{8,12},{12,0},{1,5},{5,9},{9,13},{13,1},{2,6},{6,10},{... | collective-permute-start | bytes 3145736 | tf_op jit(solution)/shard_map/ppermute | solution.py:30
  164.6 49.6 %collective-permute-start.9 = (bf16[8,256,256]{2,1,0:T(8,128)(2,1)}, bf16[8,256,256]{2,1,0:T(8,128)(2,1)}, u32[]{:S(2)}, u32[]{:S(2)}) collective-permute-start(bf16[8,256,256]{2,1,0:T(8,128)(2,1)} %slice.153.refs_0_), channel_id=1, source_target_pairs={{0,8},{4,12},{8,0},{12,4},{1,9},{5,13},{9,1},{13,5},{2,10},{6,14},... | collective-permute-start | bytes 3145736 | tf_op jit(solution)/shard_map/ppermute | solution.py:30
  166.9 47.3 %collective-permute-start.10 = (bf16[8,256,256]{2,1,0:T(8,128)(2,1)}, bf16[8,256,256]{2,1,0:T(8,128)(2,1)}, u32[]{:S(2)}, u32[]{:S(2)}) collective-permute-start(bf16[8,256,256]{2,1,0:T(8,128)(2,1)} %slice.153.refs_0_), channel_id=1, source_target_pairs={{0,12},{4,0},{8,4},{12,8},{1,13},{5,1},{9,5},{13,9},{2,14},{6,2},{... | collective-permute-start | bytes 3145736 | tf_op jit(solution)/shard_map/ppermute | solution.py:30
  227.0 31.9 %collective-permute-start.15 = (bf16[128,2048]{1,0:T(8,128)(2,1)}, bf16[128,2048]{1,0:T(8,128)(2,1)S(1)}, u32[]{:S(2)}, u32[]{:S(2)}) collective-permute-start(bf16[128,2048]{1,0:T(8,128)(2,1)} %add_convert_fusion.1), channel_id=1, source_target_pairs={{0,32},{32,64},{64,96},{96,0},{1,33},{33,65},{65,97},{97,1},{2,34}... | collective-permute-start | bytes 1572872 | tf_op jit(solution)/shard_map/ppermute | solution.py:30
  310.8 41.9 %collective-permute-start.30 = (bf16[2048,1024]{1,0:T(8,128)(2,1)}, bf16[2048,1024]{1,0:T(8,128)(2,1)}, u32[]{:S(2)}, u32[]{:S(2)}) collective-permute-start(bf16[2048,1024]{1,0:T(8,128)(2,1)} %products.10), channel_id=1, source_target_pairs={{0,1},{1,0},{2,3},{3,2},{4,5},{5,4},{6,7},{7,6},{8,9},{9,8},{10,11... | collective-permute-start | bytes 12582920 | tf_op jit(solution)/shard_map/ppermute | solution.py:30
  330.7 36.6 %collective-permute-start.27 = (bf16[256,2048]{1,0:T(8,128)(2,1)}, bf16[256,2048]{1,0:T(8,128)(2,1)S(1)}, u32[]{:S(2)}, u32[]{:S(2)}) collective-permute-start(bf16[256,2048]{1,0:T(8,128)(2,1)} %get-tuple-element.238), channel_id=1, source_target_pairs={{0,4},{4,8},{8,12},{12,0},{1,5},{5,9},{9,13},{13,1},{2,6},{6,10},{... | collective-permute-start | bytes 3145736 | tf_op jit(solution)/shard_map/ppermute | solution.py:30
  330.9 47.4 %collective-permute-start.28 = (bf16[256,2048]{1,0:T(8,128)(2,1)}, bf16[256,2048]{1,0:T(8,128)(2,1)S(1)}, u32[]{:S(2)}, u32[]{:S(2)}) collective-permute-start(bf16[256,2048]{1,0:T(8,128)(2,1)} %get-tuple-element.239), channel_id=1, source_target_pairs={{0,8},{4,12},{8,0},{12,4},{1,9},{5,13},{9,1},{13,5},{2,10},{6,14},... | collective-permute-start | bytes 3145736 | tf_op jit(solution)/shard_map/ppermute | solution.py:30
  333.2 46.2 %collective-permute-start.29 = (bf16[256,2048]{1,0:T(8,128)(2,1)}, bf16[256,2048]{1,0:T(8,128)(2,1)S(1)}, u32[]{:S(2)}, u32[]{:S(2)}) collective-permute-start(bf16[256,2048]{1,0:T(8,128)(2,1)} %get-tuple-element.240), channel_id=1, source_target_pairs={{0,12},{4,0},{8,4},{12,8},{1,13},{5,1},{9,5},{13,9},{2,14},{6,2},{... | collective-permute-start | bytes 3145736 | tf_op jit(solution)/shard_map/ppermute | solution.py:30
  385.4 29.5 %collective-permute-start.38 = (bf16[128,4096]{1,0:T(8,128)(2,1)S(1)}, bf16[128,4096]{1,0:T(8,128)(2,1)}, u32[]{:S(2)}, u32[]{:S(2)}) collective-permute-start(bf16[128,4096]{1,0:T(8,128)(2,1)S(1)} %constant_dynamic-update-slice_fusion.8), channel_id=1, source_target_pairs={{0,64},{32,96},{64,0},{96,32},{1,65},{33,97},{65,1},{97,33},{2,66}... | collective-permute-start | bytes 3145736 | tf_op jit(solution)/shard_map/ppermute | solution.py:30
  385.8 48.8 %collective-permute-start.37 = (bf16[128,4096]{1,0:T(8,128)(2,1)S(1)}, bf16[128,4096]{1,0:T(8,128)(2,1)}, u32[]{:S(2)}, u32[]{:S(2)}) collective-permute-start(bf16[128,4096]{1,0:T(8,128)(2,1)S(1)} %constant_dynamic-update-slice_fusion.8), channel_id=1, source_target_pairs={{0,32},{32,64},{64,96},{96,0},{1,33},{33,65},{65,97},{97,1},{2,34}... | collective-permute-start | bytes 3145736 | tf_op jit(solution)/shard_map/ppermute | solution.py:30
  411.3 43.9 %collective-permute-start.35 = (bf16[512,1024]{1,0:T(8,128)(2,1)}, bf16[512,1024]{1,0:T(8,128)(2,1)S(1)}, u32[]{:S(2)}, u32[]{:S(2)}) collective-permute-start(bf16[512,1024]{1,0:T(8,128)(2,1)} %get-tuple-element.258), channel_id=1, source_target_pairs={{0,16},{2,18},{16,0},{18,2},{1,17},{3,19},{17,1},{19,3},{4,20},{6,... | collective-permute-start | bytes 3145736 | tf_op jit(solution)/shard_map/ppermute | solution.py:815
  412.1 47.6 %collective-permute-start.36 = (bf16[512,1024]{1,0:T(8,128)(2,1)}, bf16[512,1024]{1,0:T(8,128)(2,1)S(1)}, u32[]{:S(2)}, u32[]{:S(2)}) collective-permute-start(bf16[512,1024]{1,0:T(8,128)(2,1)} %get-tuple-element.259), channel_id=1, source_target_pairs={{0,18},{2,16},{16,2},{18,0},{1,19},{3,17},{17,3},{19,1},{4,22},{6,... | collective-permute-start | bytes 3145736 | tf_op jit(solution)/shard_map/ppermute | solution.py:815
  459.7 29.6 %collective-permute-start.53 = (bf16[128,256]{1,0:T(8,128)(2,1)S(1)}, bf16[128,256]{1,0:T(8,128)(2,1)S(1)}, u32[]{:S(2)}, u32[]{:S(2)}) collective-permute-start(bf16[128,256]{1,0:T(8,128)(2,1)S(1)} %fusion.23), channel_id=1, source_target_pairs={{0,96},{32,0},{64,32},{96,64},{1,97},{33,1},{65,33},{97,65},{2,98}... | collective-permute-start | bytes 196616 | tf_op jit(solution)/shard_map/ppermute | solution.py:30
  461.7 30.1 %collective-permute-start.52 = (bf16[128,256]{1,0:T(8,128)(2,1)S(1)}, bf16[128,256]{1,0:T(8,128)(2,1)S(1)}, u32[]{:S(2)}, u32[]{:S(2)}) collective-permute-start(bf16[128,256]{1,0:T(8,128)(2,1)S(1)} %fusion.23), channel_id=1, source_target_pairs={{0,64},{32,96},{64,0},{96,32},{1,65},{33,97},{65,1},{97,33},{2,66}... | collective-permute-start | bytes 196616 | tf_op jit(solution)/shard_map/ppermute | solution.py:30
  462.9 30.1 %collective-permute-start.51 = (bf16[128,256]{1,0:T(8,128)(2,1)S(1)}, bf16[128,256]{1,0:T(8,128)(2,1)S(1)}, u32[]{:S(2)}, u32[]{:S(2)}) collective-permute-start(bf16[128,256]{1,0:T(8,128)(2,1)S(1)} %fusion.23), channel_id=1, source_target_pairs={{0,32},{32,64},{64,96},{96,0},{1,33},{33,65},{65,97},{97,1},{2,34}... | collective-permute-start | bytes 196616 | tf_op jit(solution)/shard_map/ppermute | solution.py:30
  484.7 39.1 %all-to-all-start.3 = ((bf16[16,16,2048]{2,1,0:T(8,128)(2,1)}), bf16[16,16,2048]{2,1,0:T(8,128)(2,1)}, u32[]{:S(2)}, u32[]{:S(2)}) async-start(bf16[16,16,2048]{2,1,0:T(8,128)(2,1)} %bitcast.266), calls=%async_computation.3 | async-start | bytes 2097152 | tf_op jit(solution)/shard_map/all_to_all | solution.py:892
  493.0 30.8 %collective-permute-start.54 = (bf16[128,2048]{1,0:T(8,128)(2,1)}, bf16[128,2048]{1,0:T(8,128)(2,1)}, u32[]{:S(2)}, u32[]{:S(2)}) collective-permute-start(bf16[128,2048]{1,0:T(8,128)(2,1)} %get-tuple-element.369), channel_id=1, source_target_pairs={{0,96},{32,0},{64,32},{96,64},{1,97},{33,1},{65,33},{97,65},{2,98}... | collective-permute-start | bytes 1572872 | tf_op jit(solution)/shard_map/ppermute | solution.py:30
  494.6 29.2 %collective-permute-start.55 = (bf16[128,2048]{1,0:T(8,128)(2,1)}, bf16[128,2048]{1,0:T(8,128)(2,1)}, u32[]{:S(2)}, u32[]{:S(2)}) collective-permute-start(bf16[128,2048]{1,0:T(8,128)(2,1)} %get-tuple-element.368), channel_id=1, source_target_pairs={{0,64},{32,96},{64,0},{96,32},{1,65},{33,97},{65,1},{97,33},{2,66}... | collective-permute-start | bytes 1572872 | tf_op jit(solution)/shard_map/ppermute | solution.py:30
  590.7 37.4 %collective-permute-start.66 = (bf16[4,128,1024]{2,1,0:T(8,128)(2,1)}, bf16[4,128,1024]{2,1,0:T(8,128)(2,1)}, u32[]{:S(2)}, u32[]{:S(2)}) collective-permute-start(bf16[4,128,1024]{2,1,0:T(8,128)(2,1)} %pad_maximum_fusion.3), channel_id=1, source_target_pairs={{0,2},{2,0},{1,3},{3,1},{4,6},{6,4},{5,7},{7,5},{8,10},{10,8},{9,1... | collective-permute-start | bytes 3145736 | tf_op jit(solution)/shard_map/ppermute | solution.py:30
  597.0 31.0 %collective-permute-start.68 = (bf16[2,128,1024]{2,1,0:T(8,128)(2,1)}, bf16[2,128,1024]{2,1,0:T(8,128)(2,1)}, u32[]{:S(2)}, u32[]{:S(2)}) collective-permute-start(bf16[2,128,1024]{2,1,0:T(8,128)(2,1)} %maximum_select_fusion.1.refs_1_), channel_id=1, source_target_pairs={{0,8},{4,12},{8,0},{12,4},{1,9},{5,13},{9,1},{13,5},{2,10},{6,14},... | collective-permute-start | bytes 1572872 | tf_op jit(solution)/shard_map/ppermute | solution.py:30
  (154 other events, 2225.7 us)

commit v3 on v2

--- a/solution.py
+++ b/solution.py
@@ -506,13 +506,13 @@
     )(q, grad, kv, keys_t, places, own, begin, logs, *done)
 
 
-def feed_forward(h, dy, w_fc, b_fc, w_proj, done=()):
+def feed_forward(h, dy, w_fc, b_fc, w_proj, parts):
     tokens, width = h.shape
-    units, part = w_fc.shape[1], 512
+    units, part, rows = w_fc.shape[1], 512, tokens // parts
     curve = math.sqrt(2.0 / math.pi)
 
     def kernel(h_ref, dy_ref, fc_ref, b_ref, proj_ref, *refs):
-        g_ref, du_ref, sum_ref, dh_ref, acc_ref = refs[len(done) :]
+        g_ref, du_ref, sum_ref, *dh_refs, acc_ref = refs
         step = pl.program_id(0)
         u = jnp.dot(h_ref[...], fc_ref[...], preferred_element_type=F32) + b_ref[...]
         dg = dot_wide(dy_ref[...], proj_ref[...])
@@ -536,7 +536,8 @@
 
         @pl.when(step == units // part - 1)
         def _():
-            dh_ref[...] = acc_ref[...].astype(BF)
+            for k, dh_ref in enumerate(dh_refs):
+                dh_ref[...] = acc_ref[k * rows : (k + 1) * rows, :].astype(BF)
 
     along = lambda k: (0, k)
     return pl.pallas_call(
@@ -548,25 +549,24 @@
             pl.BlockSpec((width, part), along),
             pl.BlockSpec((1, part), along),
             pl.BlockSpec((part, width), lambda k: (k, 0)),
-        ]
-        + [pl.BlockSpec(memory_space=pl.ANY)] * len(done),
+        ],
         out_specs=[
             pl.BlockSpec((tokens, part), along),
             pl.BlockSpec((tokens, part), along),
             pl.BlockSpec((1, part), along),
-            whole(tokens, width),
+            *[whole(rows, width)] * parts,
         ],
         out_shape=[
             jax.ShapeDtypeStruct((tokens, units), BF),
             jax.ShapeDtypeStruct((tokens, units), BF),
             jax.ShapeDtypeStruct((1, units), F32),
-            jax.ShapeDtypeStruct((tokens, width), BF),
+            *[jax.ShapeDtypeStruct((rows, width), BF)] * parts,
         ],
         scratch_shapes=[pltpu.VMEM((tokens, width), F32)],
         compiler_params=pltpu.CompilerParams(vmem_limit_bytes=56 * 2**20),
         cost_estimate=COST,
         name="feed_forward",
-    )(h, dy, w_fc, b_fc.reshape(1, units), w_proj, *done)
+    )(h, dy, w_fc, b_fc.reshape(1, units), w_proj)
 
 
 def products(pairs, at_left, at_right, extra=None, split=False):
@@ -804,7 +804,7 @@
     )
     h2_pieces, wfc, wproj = gate((h2_pieces, wfc, wproj))
     h2_all = jnp.concatenate(h2_pieces)
-    g, du, du_sum, dh2 = feed_forward(h2_all, dy_all, wfc, bfc, wproj)
+    g, du, du_sum, *dh2 = feed_forward(h2_all, dy_all, wfc, bfc, wproj, ny)
 
     x_ring = [(a, b) for a in (0, 1) for b in (0, 1)]
     zs = [(z + d) % nz for d in range(nz)]
@@ -829,7 +829,6 @@
         lambda core: [[(k * 2 + core) * nz + there for k in (0, 1)] for there in zs],
         [0] * nz,
     )
-    dh2 = dh2.reshape(ny, rows, width)
     dh2 = [dh2[0]] + [shift(dh2[d], Y, -d) for d in range(1, ny)]
     dh2, dproj, attended, h1 = gate((dh2, dproj, attended, h1))
     dproj = over_z(dproj)
@@ -850,7 +849,10 @@
         lambda core: [[(k * 2 + (xl ^ a)) * 2 + core for k in range(ny)] for a, _ in x_ring],
         [xh ^ b for _, b in x_ring],
     )
-    dq, dkv, da, dproj, dfc, g, sent = gate((dq, dkv, da, dproj, dfc, g, sent))
+    result_terms = matmul(g, wproj).astype(BF)
+    dq, dkv, da, dproj, dfc, result_terms, sent = gate(
+        (dq, dkv, da, dproj, dfc, result_terms, sent)
+    )
     dfc = over_x(dfc)
     sent = jnp.concatenate(sent)
     attended_columns, h1_columns = sent[:, : block // ny], sent[:, block // ny :]
@@ -864,7 +866,6 @@
     dkv = plus(pick(dkv, xh, 1), swap(pick(dkv, 1 - xh, 1), XH))
     dkv = plus(pick(dkv, z, 0), *[shift(pick(dkv, k, 0), Z, d) for d, k in list(enumerate(zs))[1:]])
     da_dq = over_y(jnp.concatenate([da, dq], axis=1))
-    result_terms = matmul(g, wproj).astype(BF)
 
     dproj, dfc, da_dq, dkv, result_terms, dq = gate(
         (dproj, dfc, da_dq, dkv, result_terms, dq)

time: 689 us -> 717 us (1.041)
  waiting for transfers between devices: 186 us -> 207 us
  starting transfers between devices: 124 us -> 134 us
    ppermute x70, waiting for transfers between devices: 125 us -> 157 us  [shift(): return lax.ppermute(array, axis, [(i, (i + by) % n) for i in range(n)])]
    ppermute x6, waiting for transfers between devices: 29 us -> 15.1 us  [flip(): return lax.ppermute(array, (XL, XH), moves)]
    unnamed x206 -> x218, local copies, waits for them, and re-layouts: 34.3 us -> 33.1 us
  transfers between devices with their start and end apart: 83 -> 83, of which waited for: 26 -> 28; matrix products, arithmetic and copies ran while one was open for 17% -> 15% of each run, Pallas kernels for 17% -> 17%
where the time goes in v3:
time: 717 us; the launch traced here: 706 us
  waiting for transfers between devices  207 us (29%)
  Pallas kernels  160 us (22%)
  starting transfers between devices  134 us (19%)
  local copies, waits for them, and re-layouts  76.6 us (11%)
  blocking collectives  44.3 us (6%)
  other arithmetic  43 us (6%)
  matrix products  38 us (5%)
    ppermute x70, waiting for transfers between devices, shift(): return lax.ppermute(array, axis, [(i, (i + by) % n) for i in range(n)])  157 us
    ppermute x70, starting transfers between devices, shift(): return lax.ppermute(array, axis, [(i, (i + by) % n) for i in range(n)])  86.5 us
    pallas_call x8, Pallas kernels, products(): pl.pallas_call(kernel, grid_spec=pltpu.PrefetchScalarGridSpec(num_scalar_...  50.8 us
    all_to_all x1, blocking collectives, shards(): first = lax.all_to_all(first, FSDP, 0, 0, tiled=True)  44.3 us
    unnamed x218, local copies, waits for them, and re-layouts  33.1 us
    pallas_call x2, Pallas kernels, assemble_quarters(): pl.pallas_call(kernel, grid_spec=pltpu.PrefetchScalarGridSpec(num_scalar_...  27 us
    pallas_call x1, Pallas kernels, feed_forward(): pl.pallas_call(kernel, grid=(units // part,), in_specs=[whole(tokens, wid...  22.5 us
    dot_general x5, matrix products, matmul(): return jnp.dot(left, right, preferred_element_type=F32)  21.2 us
  transfers between devices with their start and end apart: 83, of which 28 were waited for; matrix products, arithmetic and copies ran while one was open for 15% of the time, Pallas kernels for 17%

profile of v3, /device:TPU:1, one launch (start us, length us, event | category | flops | bytes accessed | tf_op | source)
XLA Modules:
  0.0 706.2 jit_solution(6071984345774471549)
XLA Ops:
  12.3 44.3 %all_to_all.40.refs_0_ = bf16[8,784,256]{2,1,0:T(8,128)(2,1)S(1)} all-to-all(bf16[8,784,256]{2,1,0:T(8,128)(2,1)S(1)} %pack.1), channel_id=1, replica_groups=mesh['fsdp_0'=4,'fsdp_1'=2,'context_0'=4,'context_1'=2,'context_2'=2] {'..., dimensions={0} | all-to-all | bytes 6422528 | tf_op jit(solution)/shard_map/all_to_all | solution.py:697
  80.0 16.9 %collective-permute-done.2.refs_3_ = bf16[8,256,256]{2,1,0:T(8,128)(2,1)S(1)} collective-permute-done((bf16[8,256,256]{2,1,0:T(8,128)(2,1)S(1)}, bf16[8,256,256]{2,1,0:T(8,128)(2,1)S(1)}, u32[]{:S(2)}, u32[]{:S(2)}) %collective-permute-start.2) | collective-permute-done | bytes 1048608 | tf_op jit(solution)/shard_map/ppermute | solution.py:30
  98.8 24.3 %collective-permute-done.refs_1_ = bf16[8,256,256]{2,1,0:T(8,128)(2,1)} collective-permute-done((bf16[8,256,256]{2,1,0:T(8,128)(2,1)S(1)}, bf16[8,256,256]{2,1,0:T(8,128)(2,1)}, u32[]{:S(2)}, u32[]{:S(2)}) %collective-permute-start) | collective-permute-done | bytes 1048608 | tf_op jit(solution)/shard_map/ppermute | solution.py:30
  131.1 9.9 %assemble.2 = bf16[2048,2048]{1,0:T(8,128)(2,1)S(1)} custom-call(s32[18]{0:T(128)S(1)} %stack.583.at_ref, bf16[1024,2048]{1,0:T(8,128)(2,1)} %bitcast.33.refs_0_, bf16[1024,2048]{1,0:T(8,128)(2,1)} %bitcast.34.refs_1_), custom_call_target="tpu_custom_call" | custom-call | flops 30000001024 | bytes 1024 | tf_op jit(solution)/shard_map/assemble/pallas_call | solution.py:224
  145.4 7.5 %all-to-all-done.2 = bf16[16,192,256]{2,1,0:T(8,128)(2,1)} async-done(((bf16[16,192,256]{2,1,0:T(8,128)(2,1)}), bf16[16,192,256]{2,1,0:T(8,128)(2,1)}, u32[]{:S(2)}, u32[]{:S(2)}) %all-to-all-start.2) | async-done | bytes 1572896 | tf_op jit(solution)/shard_map/all_to_all | solution.py:738
  191.0 7.5 %attend.1 = (bf16[128,2048]{1,0:T(8,128)(2,1)S(1)}, f32[8,256]{1,0:T(8,128)S(1)}, f32[8,256]{1,0:T(8,128)S(1)}) custom-call(bf16[128,2048]{1,0:T(8,128)(2,1)S(1)} %fusion.1.q_ref, bf16[2048,256]{1,0:T(8,128)(2,1)S(1)} %bitcast.233, bf16[128,2048]{1,0:T(8,128)(2,1)S(1)} %bitcast.235, s32[2048,128]{1,0:T(8,128)S(1)} %broadcast_in_dim.40.place_ref, ...), custom_call_target="tpu_custom_call" | custom-call | bytes 1024 | tf_op jit(solution)/shard_map/attend/pallas_call | solution.py:436
  199.5 13.1 %assemble_quarters.2 = bf16[8,2,128,2048]{3,2,1,0:T(8,128)(2,1)} custom-call(s32[32]{0:T(128)S(1)} %stack.593.at_ref, bf16[8,256,256]{2,1,0:T(8,128)(2,1)S(1)} %get-tuple-element.194.refs_0_, bf16[8,256,256]{2,1,0:T(8,128)(2,1)} %collective-permute-done.refs_1_, bf16[8,256,256]{2,1,0:T(8,128)(2,1)} %collective-permute-done.1.refs_2_, ...), custom_call_target="tpu_custom_call" | custom-call | bytes 1024 | tf_op jit(solution)/shard_map/assemble_quarters/pallas_call | solution.py:156
  239.1 14.0 %assemble_quarters.3 = bf16[8,2,128,2048]{3,2,1,0:T(8,128)(2,1)} custom-call(s32[32]{0:T(128)S(1)} %stack.593.at_ref, bf16[8,256,256]{2,1,0:T(8,128)(2,1)} %slice.137.refs_0_, bf16[8,256,256]{2,1,0:T(8,128)(2,1)} %collective-permute-done.8.refs_1_, bf16[8,256,256]{2,1,0:T(8,128)(2,1)} %collective-permute-done.9.refs_2_, ...), custom_call_target="tpu_custom_call" | custom-call | flops 30000001024 | bytes 1024 | tf_op jit(solution)/shard_map/assemble_quarters/pallas_call | solution.py:156
  264.4 22.5 %feed_forward.1 = (bf16[512,2048]{1,0:T(8,128)(2,1)}, bf16[512,2048]{1,0:T(8,128)(2,1)}, f32[1,2048]{1,0:T(1,128)}, bf16[128,2048]{1,0:T(8,128)(2,1)}, bf16[128,...) custom-call(bf16[512,2048]{1,0:T(8,128)(2,1)} %copy-done.69, ...), custom_call_target="tpu_custom_call" | custom-call | flops 30000001024 | bytes 1024 | tf_op jit(solution)/shard_map/feed_forward/pallas_call | solution.py:543
  299.5 7.8 %products.10 = bf16[2048,1024]{1,0:T(8,128)(2,1)} custom-call(s32[20]{0:T(128)} %stack.646.at_ref, bf16[512,2048]{1,0:T(8,128)(2,1)} %copy-done.69, bf16[512,2048]{1,0:T(8,128)(2,1)} %copy-done.69, bf16[512,2048]{1,0:T(8,128)(2,1)} %copy-done.69, bf16[512,2048]{1,0:T(8,128)(2,1)} %copy-done.69, bf16[512,2048]{1,0:T(8,128)(2,1)} %get-tuple-element.247.refs_4_), custom_call_target="tpu_custom_call" | custom-call | flops 30000001024 | bytes 1024 | tf_op jit(solution)/shard_map/products/pallas_call | solution.py:624
  308.6 9.0 %convolution_convert_fusion = bf16[512,2048]{1,0:T(8,128)(2,1)} fusion(bf16[512,2048]{1,0:T(8,128)(2,1)S(1)} %copy-done.100, bf16[2048,2048]{1,0:T(8,128)(2,1)} %copy-done.41), kind=kOutput, calls=%fused_computation.1 | convolution fusion | flops 4296015872 | bytes 12582912 | tf_op jit(solution)/shard_map/dot_general | solution.py:365
  317.6 8.8 %products.9 = (bf16[256,2048]{1,0:T(8,128)(2,1)}, bf16[256,2048]{1,0:T(8,128)(2,1)}, bf16[256,2048]{1,0:T(8,128)(2,1)}, bf16[256,2048]{1,0:T(8,128)(2,1)}) custom-call(s32[12]{0:T(128)} %stack.619.at_ref, bf16[512,2048]{1,0:T(8,128)(2,1)} %get-tuple-element.231.refs_0_.refs_1_, bf16[512,2048]{1,0:T(8,128)(2,1)} %get-tuple-element.231.refs_0_.refs_1_, ...), custom_call_target="tpu_custom_call" | custom-call | flops 30000001024 | bytes 1024 | tf_op jit(solution)/shard_map/products/pallas_call | solution.py:624
  342.8 8.5 %attend_back.1 = (bf16[128,2048]{1,0:T(8,128)(2,1)S(1)}, bf16[2048,256]{1,0:T(8,128)(2,1)S(1)}) custom-call(bf16[128,2048]{1,0:T(8,128)(2,1)S(1)} %copy-done.8, bf16[128,2048]{1,0:T(8,128)(2,1)S(1)} %convolution_convert_fusion.1.g_ref, bf16[2048,256]{1,0:T(8,128)(2,1)S(1)} %bitcast.234, bf16[128,2048]{1,0:T(8,128)(2,1)S(1)} %bitcast.237, ...), custom_call_target="tpu_custom_call" | custom-call | flops 30000001024 | bytes 1024 | tf_op jit(solution)/shard_map/attend_back/pallas_call | solution.py:494
  355.9 9.1 %products.11 = (bf16[512,1024]{1,0:T(8,128)(2,1)}, bf16[512,1024]{1,0:T(8,128)(2,1)}, bf16[512,1024]{1,0:T(8,128)(2,1)}, bf16[512,1024]{1,0:T(8,128)(2,1)}) custom-call(s32[20]{0:T(128)} %stack.637.at_ref, bf16[512,2048]{1,0:T(8,128)(2,1)} %copy-done.69, bf16[512,2048]{1,0:T(8,128)(2,1)} %copy-done.69, bf16[512,2048]{1,0:T(8,128)(2,1)} %copy-done.69, ...), custom_call_target="tpu_custom_call" | custom-call | flops 30000001024 | bytes 1024 | tf_op jit(solution)/shard_map/products/pallas_call | solution.py:624
  365.1 17.1 %collective-permute-done.28 = bf16[256,2048]{1,0:T(8,128)(2,1)S(1)} collective-permute-done((bf16[256,2048]{1,0:T(8,128)(2,1)}, bf16[256,2048]{1,0:T(8,128)(2,1)S(1)}, u32[]{:S(2)}, u32[]{:S(2)}) %collective-permute-start.28) | collective-permute-done | bytes 1048608 | tf_op jit(solution)/shard_map/ppermute | solution.py:30
  382.2 17.8 %collective-permute-done.29 = bf16[256,2048]{1,0:T(8,128)(2,1)S(1)} collective-permute-done((bf16[256,2048]{1,0:T(8,128)(2,1)S(1)}, bf16[256,2048]{1,0:T(8,128)(2,1)S(1)}, u32[]{:S(2)}, u32[]{:S(2)}) %collective-permute-start.29) | collective-permute-done | bytes 1048608 | tf_op jit(solution)/shard_map/ppermute | solution.py:30
  439.8 23.4 %collective-permute-done.37 = bf16[128,4096]{1,0:T(8,128)(2,1)} collective-permute-done((bf16[128,4096]{1,0:T(8,128)(2,1)}, bf16[128,4096]{1,0:T(8,128)(2,1)}, u32[]{:S(2)}, u32[]{:S(2)}) %collective-permute-start.37) | collective-permute-done | bytes 1048608 | tf_op jit(solution)/shard_map/ppermute | solution.py:30
  519.4 7.2 %fusion.43 = f32[128,2048]{1,0:T(8,128)} fusion(bf16[128,2048]{1,0:T(8,128)(2,1)S(1)} %get-tuple-element.288, bf16[2048,2048]{1,0:T(8,128)(2,1)} %copy-done.2), kind=kOutput, calls=%fused_computation.149 | convolution fusion | flops 1073741824 | bytes 9961472 | tf_op jit(solution)/shard_map/dot_general | solution.py:373
  581.6 8.7 %all-to-all-start.5 = ((bf16[128,16,256]{2,1,0:T(8,128)(2,1)}), bf16[128,16,256]{2,1,0:T(8,128)(2,1)S(1)}, u32[]{:S(2)}, u32[]{:S(2)}) async-start(bf16[128,16,256]{2,1,0:T(8,128)(2,1)} %bitcast.264), calls=%async_computation.5 | async-start | bytes 2097152 | tf_op jit(solution)/shard_map/all_to_all | solution.py:959
  595.1 14.4 %all-to-all-done.5 = bf16[128,16,256]{2,1,0:T(8,128)(2,1)S(1)} async-done(((bf16[128,16,256]{2,1,0:T(8,128)(2,1)}), bf16[128,16,256]{2,1,0:T(8,128)(2,1)S(1)}, u32[]{:S(2)}, u32[]{:S(2)}) %all-to-all-start.5) | async-done | bytes 1048608 | tf_op jit(solution)/shard_map/all_to_all | solution.py:959
  633.6 8.0 %collective-permute-done.69.refs_4_ = bf16[2,128,1024]{2,1,0:T(8,128)(2,1)} collective-permute-done((bf16[2,128,1024]{2,1,0:T(8,128)(2,1)}, bf16[2,128,1024]{2,1,0:T(8,128)(2,1)}, u32[]{:S(2)}, u32[]{:S(2)}) %collective-permute-start.69) | collective-permute-done | bytes 524320 | tf_op jit(solution)/shard_map/ppermute | solution.py:30
  642.1 12.2 %collective-permute-done.67.refs_2_ = bf16[2,128,1024]{2,1,0:T(8,128)(2,1)} collective-permute-done((bf16[2,128,1024]{2,1,0:T(8,128)(2,1)}, bf16[2,128,1024]{2,1,0:T(8,128)(2,1)}, u32[]{:S(2)}, u32[]{:S(2)}) %collective-permute-start.67) | collective-permute-done | bytes 524320 | tf_op jit(solution)/shard_map/ppermute | solution.py:30
  672.9 11.2 %lay_both.1 = (f32[1024,2048]{1,0:T(8,128)}, f32[256,8192]{1,0:T(8,128)}) custom-call(s32[8]{0:T(128)} %stack.677.at_ref, bf16[2,4,128,1024]{3,2,1,0:T(8,128)(2,1)} %maximum_select_fusion.refs_0_, bf16[2,128,1024]{2,1,0:T(8,128)(2,1)} %maximum_select_fusion.1.refs_1_, bf16[2,128,1024]{2,1,0:T(8,128)(2,1)} %collective-permute-done.67.refs_2_, ...), custom_call_target="tpu_custom_call" | custom-call | flops 30000001024 | bytes 1024 | tf_op jit(solution)/shard_map/lay_both/pallas_call | solution.py:278
  697.1 8.9 %laid_out.1 = (f32[256,2048]{1,0:T(8,128)}, f32[256,2048]{1,0:T(8,128)}, f32[256,256]{1,0:T(8,128)}) custom-call(s32[1]{0:T(128)} %bitcast.9.at_ref.core_ref, bf16[8,16,4352]{2,1,0:T(8,128)(2,1)S(1)} %all-to-all-done.7.mine_ref, bf16[8,16,4352]{2,1,0:T(8,128)(2,1)} %collective-permute-done.75.theirs_ref), custom_call_target="tpu_custom_call" | custom-call | flops 30000001024 | bytes 1024 | tf_op jit(solution)/shard_map/laid_out/pallas_call | solution.py:344
  (538 shorter events, 370.6 us)
Async XLA Ops:
  60.9 62.3 %all-to-all-start.1 = ((bf16[8,128,2048]{2,1,0:T(8,128)(2,1)}), bf16[8,128,2048]{2,1,0:T(8,128)(2,1)}, u32[]{:S(2)}, u32[]{:S(2)}) async-start(bf16[8,128,2048]{2,1,0:T(8,128)(2,1)} %copy-done.6), calls=%async_computation.1 | async-start | bytes 8388608 | tf_op jit(solution)/shard_map/all_to_all | solution.py:706
  74.6 48.5 %collective-permute-start = (bf16[8,256,256]{2,1,0:T(8,128)(2,1)S(1)}, bf16[8,256,256]{2,1,0:T(8,128)(2,1)}, u32[]{:S(2)}, u32[]{:S(2)}) collective-permute-start(bf16[8,256,256]{2,1,0:T(8,128)(2,1)S(1)} %get-tuple-element.194.refs_0_), channel_id=1, source_target_pairs={{0,4},{4,8},{8,12},{12,0},{1,5},{5,9},{9,13},{13,1},{2,6},{6,10},{... | collective-permute-start | bytes 3145736 | tf_op jit(solution)/shard_map/ppermute | solution.py:30
  156.0 62.7 %collective-permute-start.14 = (bf16[512,2048]{1,0:T(8,128)(2,1)}, bf16[512,2048]{1,0:T(8,128)(2,1)}, u32[]{:S(2)}, u32[]{:S(2)}) collective-permute-start(bf16[512,2048]{1,0:T(8,128)(2,1)} %constant_dynamic-slice_fusion), channel_id=1, source_target_pairs={{0,16},{16,0},{1,17},{17,1},{2,18},{18,2},{3,19},{19,3},{4,20},{20... | collective-permute-start | bytes 6291464 | tf_op jit(solution)/shard_map/ppermute | solution.py:30
  168.2 44.4 %collective-permute-start.10 = (bf16[8,256,256]{2,1,0:T(8,128)(2,1)}, bf16[8,256,256]{2,1,0:T(8,128)(2,1)}, u32[]{:S(2)}, u32[]{:S(2)}) collective-permute-start(bf16[8,256,256]{2,1,0:T(8,128)(2,1)} %slice.137.refs_0_), channel_id=1, source_target_pairs={{0,12},{4,0},{8,4},{12,8},{1,13},{5,1},{9,5},{13,9},{2,14},{6,2},{... | collective-permute-start | bytes 3145736 | tf_op jit(solution)/shard_map/ppermute | solution.py:30
  169.4 43.2 %collective-permute-start.9 = (bf16[8,256,256]{2,1,0:T(8,128)(2,1)}, bf16[8,256,256]{2,1,0:T(8,128)(2,1)}, u32[]{:S(2)}, u32[]{:S(2)}) collective-permute-start(bf16[8,256,256]{2,1,0:T(8,128)(2,1)} %slice.137.refs_0_), channel_id=1, source_target_pairs={{0,8},{4,12},{8,0},{12,4},{1,9},{5,13},{9,1},{13,5},{2,10},{6,14},... | collective-permute-start | bytes 3145736 | tf_op jit(solution)/shard_map/ppermute | solution.py:30
  173.0 45.8 %collective-permute-start.8 = (bf16[8,256,256]{2,1,0:T(8,128)(2,1)}, bf16[8,256,256]{2,1,0:T(8,128)(2,1)}, u32[]{:S(2)}, u32[]{:S(2)}) collective-permute-start(bf16[8,256,256]{2,1,0:T(8,128)(2,1)} %slice.137.refs_0_), channel_id=1, source_target_pairs={{0,4},{4,8},{8,12},{12,0},{1,5},{5,9},{9,13},{13,1},{2,6},{6,10},{... | collective-permute-start | bytes 3145736 | tf_op jit(solution)/shard_map/ppermute | solution.py:30
  179.2 33.4 %collective-permute-start.11 = (bf16[128,2048]{1,0:T(8,128)(2,1)}, bf16[128,2048]{1,0:T(8,128)(2,1)S(1)}, u32[]{:S(2)}, u32[]{:S(2)}) collective-permute-start(bf16[128,2048]{1,0:T(8,128)(2,1)} %reshape.385), channel_id=1, source_target_pairs={{0,32},{32,64},{64,96},{96,0},{1,33},{33,65},{65,97},{97,1},{2,34}... | collective-permute-start | bytes 1572872 | tf_op jit(solution)/shard_map/ppermute | solution.py:30
  228.0 33.1 %collective-permute-start.17 = (bf16[128,2048]{1,0:T(8,128)(2,1)S(1)}, bf16[128,2048]{1,0:T(8,128)(2,1)S(1)}, u32[]{:S(2)}, u32[]{:S(2)}) collective-permute-start(bf16[128,2048]{1,0:T(8,128)(2,1)S(1)} %add_convert_fusion.1), channel_id=1, source_target_pairs={{0,96},{32,0},{64,32},{96,64},{1,97},{33,1},{65,33},{97,65},{2,98}... | collective-permute-start | bytes 1572872 | tf_op jit(solution)/shard_map/ppermute | solution.py:30
  307.4 44.0 %collective-permute-start.30 = (bf16[2048,1024]{1,0:T(8,128)(2,1)}, bf16[2048,1024]{1,0:T(8,128)(2,1)}, u32[]{:S(2)}, u32[]{:S(2)}) collective-permute-start(bf16[2048,1024]{1,0:T(8,128)(2,1)} %products.10), channel_id=1, source_target_pairs={{0,1},{1,0},{2,3},{3,2},{4,5},{5,4},{6,7},{7,6},{8,9},{9,8},{10,11... | collective-permute-start | bytes 12582920 | tf_op jit(solution)/shard_map/ppermute | solution.py:30
  330.8 34.2 %collective-permute-start.32 = (bf16[128,1024]{1,0:T(8,128)(2,1)S(1)}, bf16[128,1024]{1,0:T(8,128)(2,1)S(1)}, u32[]{:S(2)}, u32[]{:S(2)}) collective-permute-start(bf16[128,1024]{1,0:T(8,128)(2,1)S(1)} %get-tuple-element.256), channel_id=1, source_target_pairs={{0,64},{32,96},{64,0},{96,32},{1,65},{33,97},{65,1},{97,33},{2,66}... | collective-permute-start | bytes 786440 | tf_op jit(solution)/shard_map/ppermute | solution.py:30
  332.6 32.4 %collective-permute-start.33 = (bf16[128,1024]{1,0:T(8,128)(2,1)S(1)}, bf16[128,1024]{1,0:T(8,128)(2,1)S(1)}, u32[]{:S(2)}, u32[]{:S(2)}) collective-permute-start(bf16[128,1024]{1,0:T(8,128)(2,1)S(1)} %get-tuple-element.257), channel_id=1, source_target_pairs={{0,96},{32,0},{64,32},{96,64},{1,97},{33,1},{65,33},{97,65},{2,98}... | collective-permute-start | bytes 786440 | tf_op jit(solution)/shard_map/ppermute | solution.py:30
  333.8 31.3 %collective-permute-start.27 = (bf16[256,2048]{1,0:T(8,128)(2,1)}, bf16[256,2048]{1,0:T(8,128)(2,1)S(1)}, u32[]{:S(2)}, u32[]{:S(2)}) collective-permute-start(bf16[256,2048]{1,0:T(8,128)(2,1)} %get-tuple-element.244), channel_id=1, source_target_pairs={{0,4},{4,8},{8,12},{12,0},{1,5},{5,9},{9,13},{13,1},{2,6},{6,10},{... | collective-permute-start | bytes 3145736 | tf_op jit(solution)/shard_map/ppermute | solution.py:30
  354.8 45.1 %collective-permute-start.29 = (bf16[256,2048]{1,0:T(8,128)(2,1)S(1)}, bf16[256,2048]{1,0:T(8,128)(2,1)S(1)}, u32[]{:S(2)}, u32[]{:S(2)}) collective-permute-start(bf16[256,2048]{1,0:T(8,128)(2,1)S(1)} %copy-done.95), channel_id=1, source_target_pairs={{0,12},{4,0},{8,4},{12,8},{1,13},{5,1},{9,5},{13,9},{2,14},{6,2},{... | collective-permute-start | bytes 3145736 | tf_op jit(solution)/shard_map/ppermute | solution.py:30
  415.6 47.6 %collective-permute-start.37 = (bf16[128,4096]{1,0:T(8,128)(2,1)}, bf16[128,4096]{1,0:T(8,128)(2,1)}, u32[]{:S(2)}, u32[]{:S(2)}) collective-permute-start(bf16[128,4096]{1,0:T(8,128)(2,1)} %constant_dynamic-update-slice_fusion.8), channel_id=1, source_target_pairs={{0,32},{32,64},{64,96},{96,0},{1,33},{33,65},{65,97},{97,1},{2,34}... | collective-permute-start | bytes 3145736 | tf_op jit(solution)/shard_map/ppermute | solution.py:30
  428.0 37.6 %collective-permute-start.34 = (bf16[512,1024]{1,0:T(8,128)(2,1)}, bf16[512,1024]{1,0:T(8,128)(2,1)S(1)}, u32[]{:S(2)}, u32[]{:S(2)}) collective-permute-start(bf16[512,1024]{1,0:T(8,128)(2,1)} %get-tuple-element.263), channel_id=1, source_target_pairs={{0,2},{2,0},{16,18},{18,16},{1,3},{3,1},{17,19},{19,17},{4,6},{6,4... | collective-permute-start | bytes 3145736 | tf_op jit(solution)/shard_map/ppermute | solution.py:815
  431.3 40.8 %collective-permute-start.35 = (bf16[512,1024]{1,0:T(8,128)(2,1)}, bf16[512,1024]{1,0:T(8,128)(2,1)S(1)}, u32[]{:S(2)}, u32[]{:S(2)}) collective-permute-start(bf16[512,1024]{1,0:T(8,128)(2,1)} %get-tuple-element.264), channel_id=1, source_target_pairs={{0,16},{2,18},{16,0},{18,2},{1,17},{3,19},{17,1},{19,3},{4,20},{6,... | collective-permute-start | bytes 3145736 | tf_op jit(solution)/shard_map/ppermute | solution.py:815
  433.9 43.5 %collective-permute-start.36 = (bf16[512,1024]{1,0:T(8,128)(2,1)}, bf16[512,1024]{1,0:T(8,128)(2,1)S(1)}, u32[]{:S(2)}, u32[]{:S(2)}) collective-permute-start(bf16[512,1024]{1,0:T(8,128)(2,1)} %get-tuple-element.265), channel_id=1, source_target_pairs={{0,18},{2,16},{16,2},{18,0},{1,19},{3,17},{17,3},{19,1},{4,22},{6,... | collective-permute-start | bytes 3145736 | tf_op jit(solution)/shard_map/ppermute | solution.py:815
  477.4 33.9 %collective-permute-start.53 = (bf16[128,256]{1,0:T(8,128)(2,1)S(1)}, bf16[128,256]{1,0:T(8,128)(2,1)S(1)}, u32[]{:S(2)}, u32[]{:S(2)}) collective-permute-start(bf16[128,256]{1,0:T(8,128)(2,1)S(1)} %fusion.23), channel_id=1, source_target_pairs={{0,96},{32,0},{64,32},{96,64},{1,97},{33,1},{65,33},{97,65},{2,98}... | collective-permute-start | bytes 196616 | tf_op jit(solution)/shard_map/ppermute | solution.py:30
  477.5 36.4 %collective-permute-start.52 = (bf16[128,256]{1,0:T(8,128)(2,1)S(1)}, bf16[128,256]{1,0:T(8,128)(2,1)}, u32[]{:S(2)}, u32[]{:S(2)}) collective-permute-start(bf16[128,256]{1,0:T(8,128)(2,1)S(1)} %fusion.23), channel_id=1, source_target_pairs={{0,64},{32,96},{64,0},{96,32},{1,65},{33,97},{65,1},{97,33},{2,66}... | collective-permute-start | bytes 196616 | tf_op jit(solution)/shard_map/ppermute | solution.py:30
  483.8 31.3 %collective-permute-start.51 = (bf16[128,256]{1,0:T(8,128)(2,1)S(1)}, bf16[128,256]{1,0:T(8,128)(2,1)}, u32[]{:S(2)}, u32[]{:S(2)}) collective-permute-start(bf16[128,256]{1,0:T(8,128)(2,1)S(1)} %fusion.23), channel_id=1, source_target_pairs={{0,32},{32,64},{64,96},{96,0},{1,33},{33,65},{65,97},{97,1},{2,34}... | collective-permute-start | bytes 196616 | tf_op jit(solution)/shard_map/ppermute | solution.py:30
  505.0 40.8 %all-to-all-start.3 = ((bf16[16,16,2048]{2,1,0:T(8,128)(2,1)}), bf16[16,16,2048]{2,1,0:T(8,128)(2,1)}, u32[]{:S(2)}, u32[]{:S(2)}) async-start(bf16[16,16,2048]{2,1,0:T(8,128)(2,1)} %bitcast.267), calls=%async_computation.3 | async-start | bytes 2097152 | tf_op jit(solution)/shard_map/all_to_all | solution.py:893
  548.7 31.9 %all-to-all-start.4 = ((bf16[16,8,2048]{2,1,0:T(8,128)(2,1)}), bf16[16,8,2048]{2,1,0:T(8,128)(2,1)S(1)}, u32[]{:S(2)}, u32[]{:S(2)}) async-start(bf16[16,8,2048]{2,1,0:T(8,128)(2,1)} %fusion.19), calls=%async_computation.4 | async-start | bytes 1048576 | tf_op jit(solution)/shard_map/all_to_all | solution.py:732
  616.7 37.6 %collective-permute-start.66 = (bf16[4,128,1024]{2,1,0:T(8,128)(2,1)}, bf16[4,128,1024]{2,1,0:T(8,128)(2,1)}, u32[]{:S(2)}, u32[]{:S(2)}) collective-permute-start(bf16[4,128,1024]{2,1,0:T(8,128)(2,1)} %pad_maximum_fusion.3), channel_id=1, source_target_pairs={{0,2},{2,0},{1,3},{3,1},{4,6},{6,4},{5,7},{7,5},{8,10},{10,8},{9,1... | collective-permute-start | bytes 3145736 | tf_op jit(solution)/shard_map/ppermute | solution.py:30
  623.2 31.1 %collective-permute-start.67 = (bf16[2,128,1024]{2,1,0:T(8,128)(2,1)}, bf16[2,128,1024]{2,1,0:T(8,128)(2,1)}, u32[]{:S(2)}, u32[]{:S(2)}) collective-permute-start(bf16[2,128,1024]{2,1,0:T(8,128)(2,1)} %maximum_select_fusion.1.refs_1_), channel_id=1, source_target_pairs={{0,4},{4,8},{8,12},{12,0},{1,5},{5,9},{9,13},{13,1},{2,6},{6,10},{... | collective-permute-start | bytes 1572872 | tf_op jit(solution)/shard_map/ppermute | solution.py:30
  (160 other events, 2382.0 us)

commit v4 on v3

--- a/solution.py
+++ b/solution.py
@@ -849,10 +849,7 @@
         lambda core: [[(k * 2 + (xl ^ a)) * 2 + core for k in range(ny)] for a, _ in x_ring],
         [xh ^ b for _, b in x_ring],
     )
-    result_terms = matmul(g, wproj).astype(BF)
-    dq, dkv, da, dproj, dfc, result_terms, sent = gate(
-        (dq, dkv, da, dproj, dfc, result_terms, sent)
-    )
+    dq, dkv, da, dproj, dfc, g, sent = gate((dq, dkv, da, dproj, dfc, g, sent))
     dfc = over_x(dfc)
     sent = jnp.concatenate(sent)
     attended_columns, h1_columns = sent[:, : block // ny], sent[:, block // ny :]
@@ -866,6 +863,7 @@
     dkv = plus(pick(dkv, xh, 1), swap(pick(dkv, 1 - xh, 1), XH))
     dkv = plus(pick(dkv, z, 0), *[shift(pick(dkv, k, 0), Z, d) for d, k in list(enumerate(zs))[1:]])
     da_dq = over_y(jnp.concatenate([da, dq], axis=1))
+    result_terms = matmul(g, wproj).astype(BF)
 
     dproj, dfc, da_dq, dkv, result_terms, dq = gate(
         (dproj, dfc, da_dq, dkv, result_terms, dq)

time: 717 us -> 687 us (0.958)
  waiting for transfers between devices: 207 us -> 186 us
  starting transfers between devices: 134 us -> 124 us
    ppermute x70, waiting for transfers between devices: 157 us -> 125 us  [shift(): return lax.ppermute(array, axis, [(i, (i + by) % n) for i in range(n)])]
    ppermute x6, waiting for transfers between devices: 15.1 us -> 29 us  [flip(): return lax.ppermute(array, (XL, XH), moves)]
    unnamed x218 -> x208, local copies, waits for them, and re-layouts: 33.1 us -> 34.3 us
  transfers between devices with their start and end apart: 83 -> 83, of which waited for: 28 -> 26; matrix products, arithmetic and copies ran while one was open for 15% -> 17% of each run, Pallas kernels for 17% -> 17%
where the time goes in v4:
time: 687 us; the launch traced here: 677 us
  waiting for transfers between devices  186 us (27%)
  Pallas kernels  159 us (23%)
  starting transfers between devices  124 us (18%)
  local copies, waits for them, and re-layouts  79.4 us (12%)
  blocking collectives  44.3 us (6%)
  other arithmetic  42.4 us (6%)
  matrix products  38.2 us (6%)
    ppermute x70, waiting for transfers between devices, shift(): return lax.ppermute(array, axis, [(i, (i + by) % n) for i in range(n)])  125 us
    ppermute x70, starting transfers between devices, shift(): return lax.ppermute(array, axis, [(i, (i + by) % n) for i in range(n)])  79.9 us
    pallas_call x8, Pallas kernels, products(): pl.pallas_call(kernel, grid_spec=pltpu.PrefetchScalarGridSpec(num_scalar_...  50.7 us
    all_to_all x1, blocking collectives, shards(): first = lax.all_to_all(first, FSDP, 0, 0, tiled=True)  44.3 us
    unnamed x208, local copies, waits for them, and re-layouts  34.3 us
    ppermute x6, waiting for transfers between devices, flip(): return lax.ppermute(array, (XL, XH), moves)  29 us
    pallas_call x2, Pallas kernels, assemble_quarters(): pl.pallas_call(kernel, grid_spec=pltpu.PrefetchScalarGridSpec(num_scalar_...  27.1 us
    pallas_call x1, Pallas kernels, feed_forward(): pl.pallas_call(kernel, grid=(units // part,), in_specs=[whole(tokens, wid...  22.5 us
  transfers between devices with their start and end apart: 83, of which 26 were waited for; matrix products, arithmetic and copies ran while one was open for 17% of the time, Pallas kernels for 17%

profile of v4, /device:TPU:1, one launch (start us, length us, event | category | flops | bytes accessed | tf_op | source)
XLA Modules:
  0.0 677.0 jit_solution(7097418333252425745)
XLA Ops:
  12.3 44.3 %all_to_all.40.refs_0_ = bf16[8,784,256]{2,1,0:T(8,128)(2,1)S(1)} all-to-all(bf16[8,784,256]{2,1,0:T(8,128)(2,1)S(1)} %pack.1), channel_id=1, replica_groups=mesh['fsdp_0'=4,'fsdp_1'=2,'context_0'=4,'context_1'=2,'context_2'=2] {'..., dimensions={0} | all-to-all | bytes 6422528 | tf_op jit(solution)/shard_map/all_to_all | solution.py:697
  81.2 15.1 %collective-permute-done.refs_1_ = bf16[8,256,256]{2,1,0:T(8,128)(2,1)S(1)} collective-permute-done((bf16[8,256,256]{2,1,0:T(8,128)(2,1)S(1)}, bf16[8,256,256]{2,1,0:T(8,128)(2,1)S(1)}, u32[]{:S(2)}, u32[]{:S(2)}) %collective-permute-start) | collective-permute-done | bytes 1048608 | tf_op jit(solution)/shard_map/ppermute | solution.py:30
  96.3 23.4 %collective-permute-done.1.refs_2_ = bf16[8,256,256]{2,1,0:T(8,128)(2,1)} collective-permute-done((bf16[8,256,256]{2,1,0:T(8,128)(2,1)S(1)}, bf16[8,256,256]{2,1,0:T(8,128)(2,1)}, u32[]{:S(2)}, u32[]{:S(2)}) %collective-permute-start.1) | collective-permute-done | bytes 1048608 | tf_op jit(solution)/shard_map/ppermute | solution.py:30
  130.8 9.9 %assemble.2 = bf16[2048,2048]{1,0:T(8,128)(2,1)S(1)} custom-call(s32[18]{0:T(128)S(1)} %stack.583.at_ref, bf16[1024,2048]{1,0:T(8,128)(2,1)} %bitcast.33.refs_0_, bf16[1024,2048]{1,0:T(8,128)(2,1)} %bitcast.34.refs_1_), custom_call_target="tpu_custom_call" | custom-call | flops 30000001024 | bytes 1024 | tf_op jit(solution)/shard_map/assemble/pallas_call | solution.py:224
  177.7 8.0 %collective-permute-done.12 = bf16[128,2048]{1,0:T(8,128)(2,1)} collective-permute-done((bf16[128,2048]{1,0:T(8,128)(2,1)}, bf16[128,2048]{1,0:T(8,128)(2,1)}, u32[]{:S(2)}, u32[]{:S(2)}) %collective-permute-start.12) | collective-permute-done | bytes 524320 | tf_op jit(solution)/shard_map/ppermute | solution.py:30
  192.5 7.5 %attend.1 = (bf16[128,2048]{1,0:T(8,128)(2,1)S(1)}, f32[8,256]{1,0:T(8,128)S(1)}, f32[8,256]{1,0:T(8,128)S(1)}) custom-call(bf16[128,2048]{1,0:T(8,128)(2,1)S(1)} %fusion.1.q_ref, bf16[2048,256]{1,0:T(8,128)(2,1)S(1)} %bitcast.233, bf16[128,2048]{1,0:T(8,128)(2,1)S(1)} %bitcast.235, s32[2048,128]{1,0:T(8,128)S(1)} %broadcast_in_dim.40.place_ref, ...), custom_call_target="tpu_custom_call" | custom-call | bytes 1024 | tf_op jit(solution)/shard_map/attend/pallas_call | solution.py:436
  201.0 13.1 %assemble_quarters.2 = bf16[8,2,128,2048]{3,2,1,0:T(8,128)(2,1)} custom-call(s32[32]{0:T(128)S(1)} %stack.593.at_ref, bf16[8,256,256]{2,1,0:T(8,128)(2,1)S(1)} %get-tuple-element.194.refs_0_, bf16[8,256,256]{2,1,0:T(8,128)(2,1)S(1)} %copy-done.14, bf16[8,256,256]{2,1,0:T(8,128)(2,1)} %collective-permute-done.1.refs_2_, ...), custom_call_target="tpu_custom_call" | custom-call | bytes 1024 | tf_op jit(solution)/shard_map/assemble_quarters/pallas_call | solution.py:156
  236.9 14.0 %assemble_quarters.3 = bf16[8,2,128,2048]{3,2,1,0:T(8,128)(2,1)} custom-call(s32[32]{0:T(128)S(1)} %stack.593.at_ref, bf16[8,256,256]{2,1,0:T(8,128)(2,1)} %slice.137.refs_0_, bf16[8,256,256]{2,1,0:T(8,128)(2,1)} %collective-permute-done.8.refs_1_, bf16[8,256,256]{2,1,0:T(8,128)(2,1)} %collective-permute-done.9.refs_2_, ...), custom_call_target="tpu_custom_call" | custom-call | flops 30000001024 | bytes 1024 | tf_op jit(solution)/shard_map/assemble_quarters/pallas_call | solution.py:156
  262.2 22.5 %feed_forward.1 = (bf16[512,2048]{1,0:T(8,128)(2,1)}, bf16[512,2048]{1,0:T(8,128)(2,1)}, f32[1,2048]{1,0:T(1,128)}, bf16[128,2048]{1,0:T(8,128)(2,1)}, bf16[128,...) custom-call(bf16[512,2048]{1,0:T(8,128)(2,1)} %copy-done.69, ...), custom_call_target="tpu_custom_call" | custom-call | flops 30000001024 | bytes 1024 | tf_op jit(solution)/shard_map/feed_forward/pallas_call | solution.py:543
  284.7 7.2 %products.8 = bf16[1024,2048]{1,0:T(8,128)(2,1)} custom-call(s32[12]{0:T(128)} %stack.628.at_ref, bf16[512,2048]{1,0:T(8,128)(2,1)} %get-tuple-element.269.refs_0_.refs_1_, bf16[512,2048]{1,0:T(8,128)(2,1)} %get-tuple-element.269.refs_0_.refs_1_, bf16[512,2048]{1,0:T(8,128)(2,1)} %get-tuple-element.404.dy_ref.refs_2_), custom_call_target="tpu_custom_call" | custom-call | flops 30000001024 | bytes 1024 | tf_op jit(solution)/shard_map/products/pallas_call | solution.py:624
  301.4 7.8 %products.10 = bf16[2048,1024]{1,0:T(8,128)(2,1)} custom-call(s32[20]{0:T(128)} %stack.646.at_ref, bf16[512,2048]{1,0:T(8,128)(2,1)} %copy-done.69, bf16[512,2048]{1,0:T(8,128)(2,1)} %copy-done.69, bf16[512,2048]{1,0:T(8,128)(2,1)} %copy-done.69, bf16[512,2048]{1,0:T(8,128)(2,1)} %copy-done.69, bf16[512,2048]{1,0:T(8,128)(2,1)} %get-tuple-element.247.refs_4_), custom_call_target="tpu_custom_call" | custom-call | flops 30000001024 | bytes 1024 | tf_op jit(solution)/shard_map/products/pallas_call | solution.py:624
  311.8 8.8 %products.9 = (bf16[256,2048]{1,0:T(8,128)(2,1)}, bf16[256,2048]{1,0:T(8,128)(2,1)}, bf16[256,2048]{1,0:T(8,128)(2,1)}, bf16[256,2048]{1,0:T(8,128)(2,1)}) custom-call(s32[12]{0:T(128)} %stack.619.at_ref, bf16[512,2048]{1,0:T(8,128)(2,1)} %get-tuple-element.269.refs_0_.refs_1_, bf16[512,2048]{1,0:T(8,128)(2,1)} %get-tuple-element.269.refs_0_.refs_1_, ...), custom_call_target="tpu_custom_call" | custom-call | flops 30000001024 | bytes 1024 | tf_op jit(solution)/shard_map/products/pallas_call | solution.py:624
  342.6 8.5 %attend_back.1 = (bf16[128,2048]{1,0:T(8,128)(2,1)S(1)}, bf16[2048,256]{1,0:T(8,128)(2,1)S(1)}) custom-call(bf16[128,2048]{1,0:T(8,128)(2,1)S(1)} %copy-done.8, bf16[128,2048]{1,0:T(8,128)(2,1)S(1)} %convolution_convert_fusion.1.g_ref, bf16[2048,256]{1,0:T(8,128)(2,1)S(1)} %bitcast.234, bf16[128,2048]{1,0:T(8,128)(2,1)S(1)} %bitcast.237, ...), custom_call_target="tpu_custom_call" | custom-call | flops 30000001024 | bytes 1024 | tf_op jit(solution)/shard_map/attend_back/pallas_call | solution.py:494
  354.1 9.0 %products.11 = (bf16[512,1024]{1,0:T(8,128)(2,1)}, bf16[512,1024]{1,0:T(8,128)(2,1)}, bf16[512,1024]{1,0:T(8,128)(2,1)}, bf16[512,1024]{1,0:T(8,128)(2,1)}) custom-call(s32[20]{0:T(128)} %stack.637.at_ref, bf16[512,2048]{1,0:T(8,128)(2,1)} %copy-done.69, bf16[512,2048]{1,0:T(8,128)(2,1)} %copy-done.69, bf16[512,2048]{1,0:T(8,128)(2,1)} %copy-done.69, ...), custom_call_target="tpu_custom_call" | custom-call | flops 30000001024 | bytes 1024 | tf_op jit(solution)/shard_map/products/pallas_call | solution.py:624
  365.8 11.0 %collective-permute-done.28 = bf16[256,2048]{1,0:T(8,128)(2,1)S(1)} collective-permute-done((bf16[256,2048]{1,0:T(8,128)(2,1)}, bf16[256,2048]{1,0:T(8,128)(2,1)S(1)}, u32[]{:S(2)}, u32[]{:S(2)}) %collective-permute-start.28) | collective-permute-done | bytes 1048608 | tf_op jit(solution)/shard_map/ppermute | solution.py:30
  389.0 9.1 %convolution_convert_fusion = bf16[512,2048]{1,0:T(8,128)(2,1)} fusion(bf16[512,2048]{1,0:T(8,128)(2,1)S(1)} %copy-done.95, bf16[2048,2048]{1,0:T(8,128)(2,1)} %copy-done.35), kind=kOutput, calls=%fused_computation.1 | convolution fusion | flops 4296015872 | bytes 12582912 | tf_op jit(solution)/shard_map/dot_general | solution.py:365
  413.4 19.7 %collective-permute-done.37 = bf16[128,4096]{1,0:T(8,128)(2,1)} collective-permute-done((bf16[128,4096]{1,0:T(8,128)(2,1)S(1)}, bf16[128,4096]{1,0:T(8,128)(2,1)}, u32[]{:S(2)}, u32[]{:S(2)}) %collective-permute-start.37) | collective-permute-done | bytes 1048608 | tf_op jit(solution)/shard_map/ppermute | solution.py:30
  435.1 18.5 %collective-permute-done.35 = bf16[512,1024]{1,0:T(8,128)(2,1)S(1)} collective-permute-done((bf16[512,1024]{1,0:T(8,128)(2,1)}, bf16[512,1024]{1,0:T(8,128)(2,1)S(1)}, u32[]{:S(2)}, u32[]{:S(2)}) %collective-permute-start.35) | collective-permute-done | bytes 1048608 | tf_op jit(solution)/shard_map/ppermute | solution.py:815
  493.9 7.2 %fusion.43 = f32[128,2048]{1,0:T(8,128)} fusion(bf16[128,2048]{1,0:T(8,128)(2,1)S(1)} %get-tuple-element.288, bf16[2048,2048]{1,0:T(8,128)(2,1)} %copy-done.2), kind=kOutput, calls=%fused_computation.149 | convolution fusion | flops 1073741824 | bytes 9961472 | tf_op jit(solution)/shard_map/dot_general | solution.py:373
  568.2 14.4 %all-to-all-done.5 = bf16[128,16,256]{2,1,0:T(8,128)(2,1)S(1)} async-done(((bf16[128,16,256]{2,1,0:T(8,128)(2,1)}), bf16[128,16,256]{2,1,0:T(8,128)(2,1)S(1)}, u32[]{:S(2)}, u32[]{:S(2)}) %all-to-all-start.5) | async-done | bytes 1048608 | tf_op jit(solution)/shard_map/all_to_all | solution.py:957
  605.6 9.2 %collective-permute-done.67.refs_2_ = bf16[2,128,1024]{2,1,0:T(8,128)(2,1)} collective-permute-done((bf16[2,128,1024]{2,1,0:T(8,128)(2,1)}, bf16[2,128,1024]{2,1,0:T(8,128)(2,1)}, u32[]{:S(2)}, u32[]{:S(2)}) %collective-permute-start.67) | collective-permute-done | bytes 524320 | tf_op jit(solution)/shard_map/ppermute | solution.py:30
  614.7 11.7 %collective-permute-done.68.refs_3_ = bf16[2,128,1024]{2,1,0:T(8,128)(2,1)} collective-permute-done((bf16[2,128,1024]{2,1,0:T(8,128)(2,1)}, bf16[2,128,1024]{2,1,0:T(8,128)(2,1)}, u32[]{:S(2)}, u32[]{:S(2)}) %collective-permute-start.68) | collective-permute-done | bytes 524320 | tf_op jit(solution)/shard_map/ppermute | solution.py:30
  643.5 11.2 %lay_both.1 = (f32[1024,2048]{1,0:T(8,128)}, f32[256,8192]{1,0:T(8,128)}) custom-call(s32[8]{0:T(128)} %stack.677.at_ref, bf16[2,4,128,1024]{3,2,1,0:T(8,128)(2,1)} %maximum_select_fusion.refs_0_, bf16[2,128,1024]{2,1,0:T(8,128)(2,1)} %maximum_select_fusion.1.refs_1_, bf16[2,128,1024]{2,1,0:T(8,128)(2,1)} %collective-permute-done.67.refs_2_, ...), custom_call_target="tpu_custom_call" | custom-call | flops 30000001024 | bytes 1024 | tf_op jit(solution)/shard_map/lay_both/pallas_call | solution.py:278
  667.6 8.9 %laid_out.1 = (f32[256,2048]{1,0:T(8,128)}, f32[256,2048]{1,0:T(8,128)}, f32[256,256]{1,0:T(8,128)}) custom-call(s32[1]{0:T(128)} %bitcast.9.at_ref.core_ref, bf16[8,16,4352]{2,1,0:T(8,128)(2,1)S(1)} %all-to-all-done.7.mine_ref, bf16[8,16,4352]{2,1,0:T(8,128)(2,1)} %collective-permute-done.75.theirs_ref), custom_call_target="tpu_custom_call" | custom-call | flops 30000001024 | bytes 1024 | tf_op jit(solution)/shard_map/laid_out/pallas_call | solution.py:344
  (528 shorter events, 353.5 us)
Async XLA Ops:
  60.8 59.4 %all-to-all-start.1 = ((bf16[8,128,2048]{2,1,0:T(8,128)(2,1)}), bf16[8,128,2048]{2,1,0:T(8,128)(2,1)}, u32[]{:S(2)}, u32[]{:S(2)}) async-start(bf16[8,128,2048]{2,1,0:T(8,128)(2,1)} %copy-done.6), calls=%async_computation.1 | async-start | bytes 8388608 | tf_op jit(solution)/shard_map/all_to_all | solution.py:706
  72.5 47.2 %collective-permute-start.1 = (bf16[8,256,256]{2,1,0:T(8,128)(2,1)S(1)}, bf16[8,256,256]{2,1,0:T(8,128)(2,1)}, u32[]{:S(2)}, u32[]{:S(2)}) collective-permute-start(bf16[8,256,256]{2,1,0:T(8,128)(2,1)S(1)} %get-tuple-element.194.refs_0_), channel_id=1, source_target_pairs={{0,8},{4,12},{8,0},{12,4},{1,9},{5,13},{9,1},{13,5},{2,10},{6,14},... | collective-permute-start | bytes 3145736 | tf_op jit(solution)/shard_map/ppermute | solution.py:30
  75.8 44.5 %collective-permute-start.2 = (bf16[8,256,256]{2,1,0:T(8,128)(2,1)S(1)}, bf16[8,256,256]{2,1,0:T(8,128)(2,1)}, u32[]{:S(2)}, u32[]{:S(2)}) collective-permute-start(bf16[8,256,256]{2,1,0:T(8,128)(2,1)S(1)} %get-tuple-element.194.refs_0_), channel_id=1, source_target_pairs={{0,12},{4,0},{8,4},{12,8},{1,13},{5,1},{9,5},{13,9},{2,14},{6,2},{... | collective-permute-start | bytes 3145736 | tf_op jit(solution)/shard_map/ppermute | solution.py:30
  155.9 58.4 %collective-permute-start.14 = (bf16[512,2048]{1,0:T(8,128)(2,1)}, bf16[512,2048]{1,0:T(8,128)(2,1)}, u32[]{:S(2)}, u32[]{:S(2)}) collective-permute-start(bf16[512,2048]{1,0:T(8,128)(2,1)} %constant_dynamic-slice_fusion), channel_id=1, source_target_pairs={{0,16},{16,0},{1,17},{17,1},{2,18},{18,2},{3,19},{19,3},{4,20},{20... | collective-permute-start | bytes 6291464 | tf_op jit(solution)/shard_map/ppermute | solution.py:30
  164.5 49.7 %collective-permute-start.8 = (bf16[8,256,256]{2,1,0:T(8,128)(2,1)}, bf16[8,256,256]{2,1,0:T(8,128)(2,1)}, u32[]{:S(2)}, u32[]{:S(2)}) collective-permute-start(bf16[8,256,256]{2,1,0:T(8,128)(2,1)} %slice.137.refs_0_), channel_id=1, source_target_pairs={{0,4},{4,8},{8,12},{12,0},{1,5},{5,9},{9,13},{13,1},{2,6},{6,10},{... | collective-permute-start | bytes 3145736 | tf_op jit(solution)/shard_map/ppermute | solution.py:30
  164.6 49.6 %collective-permute-start.9 = (bf16[8,256,256]{2,1,0:T(8,128)(2,1)}, bf16[8,256,256]{2,1,0:T(8,128)(2,1)}, u32[]{:S(2)}, u32[]{:S(2)}) collective-permute-start(bf16[8,256,256]{2,1,0:T(8,128)(2,1)} %slice.137.refs_0_), channel_id=1, source_target_pairs={{0,8},{4,12},{8,0},{12,4},{1,9},{5,13},{9,1},{13,5},{2,10},{6,14},... | collective-permute-start | bytes 3145736 | tf_op jit(solution)/shard_map/ppermute | solution.py:30
  166.9 47.3 %collective-permute-start.10 = (bf16[8,256,256]{2,1,0:T(8,128)(2,1)}, bf16[8,256,256]{2,1,0:T(8,128)(2,1)}, u32[]{:S(2)}, u32[]{:S(2)}) collective-permute-start(bf16[8,256,256]{2,1,0:T(8,128)(2,1)} %slice.137.refs_0_), channel_id=1, source_target_pairs={{0,12},{4,0},{8,4},{12,8},{1,13},{5,1},{9,5},{13,9},{2,14},{6,2},{... | collective-permute-start | bytes 3145736 | tf_op jit(solution)/shard_map/ppermute | solution.py:30
  227.0 31.9 %collective-permute-start.15 = (bf16[128,2048]{1,0:T(8,128)(2,1)}, bf16[128,2048]{1,0:T(8,128)(2,1)S(1)}, u32[]{:S(2)}, u32[]{:S(2)}) collective-permute-start(bf16[128,2048]{1,0:T(8,128)(2,1)} %add_convert_fusion.1), channel_id=1, source_target_pairs={{0,32},{32,64},{64,96},{96,0},{1,33},{33,65},{65,97},{97,1},{2,34}... | collective-permute-start | bytes 1572872 | tf_op jit(solution)/shard_map/ppermute | solution.py:30
  309.2 41.9 %collective-permute-start.30 = (bf16[2048,1024]{1,0:T(8,128)(2,1)}, bf16[2048,1024]{1,0:T(8,128)(2,1)}, u32[]{:S(2)}, u32[]{:S(2)}) collective-permute-start(bf16[2048,1024]{1,0:T(8,128)(2,1)} %products.10), channel_id=1, source_target_pairs={{0,1},{1,0},{2,3},{3,2},{4,5},{5,4},{6,7},{7,6},{8,9},{9,8},{10,11... | collective-permute-start | bytes 12582920 | tf_op jit(solution)/shard_map/ppermute | solution.py:30
  329.2 36.6 %collective-permute-start.27 = (bf16[256,2048]{1,0:T(8,128)(2,1)}, bf16[256,2048]{1,0:T(8,128)(2,1)S(1)}, u32[]{:S(2)}, u32[]{:S(2)}) collective-permute-start(bf16[256,2048]{1,0:T(8,128)(2,1)} %get-tuple-element.244), channel_id=1, source_target_pairs={{0,4},{4,8},{8,12},{12,0},{1,5},{5,9},{9,13},{13,1},{2,6},{6,10},{... | collective-permute-start | bytes 3145736 | tf_op jit(solution)/shard_map/ppermute | solution.py:30
  329.3 47.4 %collective-permute-start.28 = (bf16[256,2048]{1,0:T(8,128)(2,1)}, bf16[256,2048]{1,0:T(8,128)(2,1)S(1)}, u32[]{:S(2)}, u32[]{:S(2)}) collective-permute-start(bf16[256,2048]{1,0:T(8,128)(2,1)} %get-tuple-element.245), channel_id=1, source_target_pairs={{0,8},{4,12},{8,0},{12,4},{1,9},{5,13},{9,1},{13,5},{2,10},{6,14},... | collective-permute-start | bytes 3145736 | tf_op jit(solution)/shard_map/ppermute | solution.py:30
  331.6 46.2 %collective-permute-start.29 = (bf16[256,2048]{1,0:T(8,128)(2,1)}, bf16[256,2048]{1,0:T(8,128)(2,1)S(1)}, u32[]{:S(2)}, u32[]{:S(2)}) collective-permute-start(bf16[256,2048]{1,0:T(8,128)(2,1)} %get-tuple-element.246), channel_id=1, source_target_pairs={{0,12},{4,0},{8,4},{12,8},{1,13},{5,1},{9,5},{13,9},{2,14},{6,2},{... | collective-permute-start | bytes 3145736 | tf_op jit(solution)/shard_map/ppermute | solution.py:30
  383.8 29.5 %collective-permute-start.38 = (bf16[128,4096]{1,0:T(8,128)(2,1)S(1)}, bf16[128,4096]{1,0:T(8,128)(2,1)}, u32[]{:S(2)}, u32[]{:S(2)}) collective-permute-start(bf16[128,4096]{1,0:T(8,128)(2,1)S(1)} %constant_dynamic-update-slice_fusion.8), channel_id=1, source_target_pairs={{0,64},{32,96},{64,0},{96,32},{1,65},{33,97},{65,1},{97,33},{2,66}... | collective-permute-start | bytes 3145736 | tf_op jit(solution)/shard_map/ppermute | solution.py:30
  384.2 48.8 %collective-permute-start.37 = (bf16[128,4096]{1,0:T(8,128)(2,1)S(1)}, bf16[128,4096]{1,0:T(8,128)(2,1)}, u32[]{:S(2)}, u32[]{:S(2)}) collective-permute-start(bf16[128,4096]{1,0:T(8,128)(2,1)S(1)} %constant_dynamic-update-slice_fusion.8), channel_id=1, source_target_pairs={{0,32},{32,64},{64,96},{96,0},{1,33},{33,65},{65,97},{97,1},{2,34}... | collective-permute-start | bytes 3145736 | tf_op jit(solution)/shard_map/ppermute | solution.py:30
  409.8 43.9 %collective-permute-start.35 = (bf16[512,1024]{1,0:T(8,128)(2,1)}, bf16[512,1024]{1,0:T(8,128)(2,1)S(1)}, u32[]{:S(2)}, u32[]{:S(2)}) collective-permute-start(bf16[512,1024]{1,0:T(8,128)(2,1)} %get-tuple-element.264), channel_id=1, source_target_pairs={{0,16},{2,18},{16,0},{18,2},{1,17},{3,19},{17,1},{19,3},{4,20},{6,... | collective-permute-start | bytes 3145736 | tf_op jit(solution)/shard_map/ppermute | solution.py:815
  410.6 47.6 %collective-permute-start.36 = (bf16[512,1024]{1,0:T(8,128)(2,1)}, bf16[512,1024]{1,0:T(8,128)(2,1)S(1)}, u32[]{:S(2)}, u32[]{:S(2)}) collective-permute-start(bf16[512,1024]{1,0:T(8,128)(2,1)} %get-tuple-element.265), channel_id=1, source_target_pairs={{0,18},{2,16},{16,2},{18,0},{1,19},{3,17},{17,3},{19,1},{4,22},{6,... | collective-permute-start | bytes 3145736 | tf_op jit(solution)/shard_map/ppermute | solution.py:815
  458.2 29.6 %collective-permute-start.53 = (bf16[128,256]{1,0:T(8,128)(2,1)S(1)}, bf16[128,256]{1,0:T(8,128)(2,1)S(1)}, u32[]{:S(2)}, u32[]{:S(2)}) collective-permute-start(bf16[128,256]{1,0:T(8,128)(2,1)S(1)} %fusion.23), channel_id=1, source_target_pairs={{0,96},{32,0},{64,32},{96,64},{1,97},{33,1},{65,33},{97,65},{2,98}... | collective-permute-start | bytes 196616 | tf_op jit(solution)/shard_map/ppermute | solution.py:30
  460.2 30.1 %collective-permute-start.52 = (bf16[128,256]{1,0:T(8,128)(2,1)S(1)}, bf16[128,256]{1,0:T(8,128)(2,1)S(1)}, u32[]{:S(2)}, u32[]{:S(2)}) collective-permute-start(bf16[128,256]{1,0:T(8,128)(2,1)S(1)} %fusion.23), channel_id=1, source_target_pairs={{0,64},{32,96},{64,0},{96,32},{1,65},{33,97},{65,1},{97,33},{2,66}... | collective-permute-start | bytes 196616 | tf_op jit(solution)/shard_map/ppermute | solution.py:30
  461.4 30.1 %collective-permute-start.51 = (bf16[128,256]{1,0:T(8,128)(2,1)S(1)}, bf16[128,256]{1,0:T(8,128)(2,1)S(1)}, u32[]{:S(2)}, u32[]{:S(2)}) collective-permute-start(bf16[128,256]{1,0:T(8,128)(2,1)S(1)} %fusion.23), channel_id=1, source_target_pairs={{0,32},{32,64},{64,96},{96,0},{1,33},{33,65},{65,97},{97,1},{2,34}... | collective-permute-start | bytes 196616 | tf_op jit(solution)/shard_map/ppermute | solution.py:30
  483.2 39.1 %all-to-all-start.3 = ((bf16[16,16,2048]{2,1,0:T(8,128)(2,1)}), bf16[16,16,2048]{2,1,0:T(8,128)(2,1)}, u32[]{:S(2)}, u32[]{:S(2)}) async-start(bf16[16,16,2048]{2,1,0:T(8,128)(2,1)} %bitcast.266), calls=%async_computation.3 | async-start | bytes 2097152 | tf_op jit(solution)/shard_map/all_to_all | solution.py:891
  491.5 30.8 %collective-permute-start.54 = (bf16[128,2048]{1,0:T(8,128)(2,1)}, bf16[128,2048]{1,0:T(8,128)(2,1)}, u32[]{:S(2)}, u32[]{:S(2)}) collective-permute-start(bf16[128,2048]{1,0:T(8,128)(2,1)} %get-tuple-element.375), channel_id=1, source_target_pairs={{0,96},{32,0},{64,32},{96,64},{1,97},{33,1},{65,33},{97,65},{2,98}... | collective-permute-start | bytes 1572872 | tf_op jit(solution)/shard_map/ppermute | solution.py:30
  493.1 29.2 %collective-permute-start.55 = (bf16[128,2048]{1,0:T(8,128)(2,1)}, bf16[128,2048]{1,0:T(8,128)(2,1)}, u32[]{:S(2)}, u32[]{:S(2)}) collective-permute-start(bf16[128,2048]{1,0:T(8,128)(2,1)} %get-tuple-element.374), channel_id=1, source_target_pairs={{0,64},{32,96},{64,0},{96,32},{1,65},{33,97},{65,1},{97,33},{2,66}... | collective-permute-start | bytes 1572872 | tf_op jit(solution)/shard_map/ppermute | solution.py:30
  589.2 37.4 %collective-permute-start.66 = (bf16[4,128,1024]{2,1,0:T(8,128)(2,1)}, bf16[4,128,1024]{2,1,0:T(8,128)(2,1)}, u32[]{:S(2)}, u32[]{:S(2)}) collective-permute-start(bf16[4,128,1024]{2,1,0:T(8,128)(2,1)} %pad_maximum_fusion.3), channel_id=1, source_target_pairs={{0,2},{2,0},{1,3},{3,1},{4,6},{6,4},{5,7},{7,5},{8,10},{10,8},{9,1... | collective-permute-start | bytes 3145736 | tf_op jit(solution)/shard_map/ppermute | solution.py:30
  595.4 31.0 %collective-permute-start.68 = (bf16[2,128,1024]{2,1,0:T(8,128)(2,1)}, bf16[2,128,1024]{2,1,0:T(8,128)(2,1)}, u32[]{:S(2)}, u32[]{:S(2)}) collective-permute-start(bf16[2,128,1024]{2,1,0:T(8,128)(2,1)} %maximum_select_fusion.1.refs_1_), channel_id=1, source_target_pairs={{0,8},{4,12},{8,0},{12,4},{1,9},{5,13},{9,1},{13,5},{2,10},{6,14},... | collective-permute-start | bytes 1572872 | tf_op jit(solution)/shard_map/ppermute | solution.py:30
  (155 other events, 2238.1 us)
